TPU v7x, 256 devices: a whole 4x4x8 slice. The times are simulated.
256 devices in a mesh: passage: 32 (over x_lo, z, core), span: 4 (over y), radial: 2 (over x_hi).
Axes of the slice: x: 4 (x_hi: 2, x_lo: 2; x = x_hi * 2 + x_lo), y: 4, z: 8, core: 2. Of those that a mesh axis runs over, the one named last changes fastest.
Arguments:
- right_side: float32 [1024, 320], P(('passage', 'span', 'radial'))
- mass: float32 [1024, 320], P(('passage', 'span', 'radial')), may hold values from 1 to 4
- volume_jac: float32 [1024, 3, 5, 5], P(('passage', 'span', 'radial')), may hold values from -0.6 to 0.6
- face_flux: float32 [1024, 6, 5, 5], P(('passage', 'span', 'radial')), may hold values from -1.2 to 1.2
- face_visc: float32 [1024, 6, 5, 5], P(('passage', 'span', 'radial')), may hold values from -0.3 to 0.3
- block_inverse: bfloat16 [1024, 320, 320], P(('passage', 'span', 'radial'))
- coarse_inverse: float32 [32, 2, 160, 160], P('passage', 'radial')
- neighbours: int32 [1024, 6], P(('passage', 'span', 'radial')), may hold values from 0 to 1023, as said below
- orientation: int32 [1024, 6], P(('passage', 'span', 'radial')), may hold values from 0 to 7
- bc_tags: int32 [1024, 6], P(('passage', 'span', 'radial')), may hold values from 0 to 2, as said below
- coarse_group: int32 [1024], P(('passage', 'span', 'radial')), may hold values from 0 to 3
Outputs:
- update: float32 [1024, 320], P(('passage', 'span', 'radial'))
- lin_residual: float32 [1024, 320], P(('passage', 'span', 'radial'))
Inputs may be any that keep to these rules, and one draw needn't show every extreme that they name: `neighbours`: the elements form a structured grid of (1 * passage devices) x (1 * span devices) x (4 * radial devices), periodic along the passage direction; each device holds one 1 x 1 x 4 block of it, in an order of its own. The element across face f touches through its face f xor 1 and lies on the same device or on the next device along direction f // 2. Where bc_tags is not 0 the entry is the element itself. `bc_tags`: 0 on interior faces (periodic ones too), 1 for a slip wall, 2 for far field; not 0 exactly on the faces at the two ends of the span and radial directions of the grid.
All inputs are finite; a program needn't handle non-finite values.
Results may differ from a plain program's by a relative error of at most 0.0068.
Values sent between devices are 32-bit elements; how exact they have to be, the bound alone decides.
No kernel may reach another device: no remote copies, remote signals or barrier semaphores. Data moves between devices by JAX's collectives and lax.ppermute only.
A program may use at most 128 MiB of HBM per device.

v0:
```python
import math

import jax
import jax.numpy as jnp
import numpy as np
from jax import lax
from jax.experimental import pallas as pl
from jax.experimental.pallas import tpu as pltpu
from jax.sharding import PartitionSpec as P

QN = 4
VARS = 5
CG = 4
ELEMS = 4
NODES = QN**3
ROWS = 320
KC = 160
STRIDE = 8
RW = ELEMS * STRIDE
FACE = QN * QN
SOURCES = 9
WIDE = 256
SCALAR0 = KC
AXES = ("passage", "span", "radial")
HIGHEST = lax.Precision.HIGHEST
F32 = jnp.float32


def lobatto_nodes():
    inner_node = 1.0 / math.sqrt(5.0)
    return np.array([-1.0, -inner_node, inner_node, 1.0])


def derivative_table():
    nodes = lobatto_nodes()
    weights = np.ones(QN)
    for row_id in range(QN):
        for col_id in range(QN):
            if col_id != row_id:
                weights[row_id] = weights[row_id] / (nodes[row_id] - nodes[col_id])
    result = np.zeros((QN, QN))
    for row_id in range(QN):
        for col_id in range(QN):
            if col_id != row_id:
                result[row_id, col_id] = (
                    weights[col_id] / weights[row_id] / (nodes[row_id] - nodes[col_id])
                )
        result[row_id, row_id] = -np.sum(result[row_id])
    return result


def vertex_table():
    nodes = lobatto_nodes()
    shapes = np.stack([(1.0 - nodes) / 2.0, (1.0 + nodes) / 2.0])
    first_part = shapes[:, None, None, :, None, None]
    second_part = shapes[None, :, None, None, :, None]
    third_part = shapes[None, None, :, None, None, :]
    return (first_part * second_part * third_part).reshape(8, NODES)


def coords(node):
    return (node // 16, node // 4 % 4, node % 4)


def others(node, axis):
    picked = [c for i, c in enumerate(coords(node)) if i != axis]
    return picked[0] * QN + picked[1]


def layer_of(face):
    return 0 if face % 2 == 0 else QN - 1


def tables():
    dmat = derivative_table()
    de = np.zeros((NODES, 3 * NODES + 6 * 2 * FACE), np.float32)
    place = np.zeros((6, 8, FACE, NODES), np.float32)
    for node in range(NODES):
        for axis in range(3):
            for target in range(NODES):
                if others(node, axis) == others(target, axis):
                    de[node, axis * NODES + target] = dmat[
                        coords(target)[axis], coords(node)[axis]
                    ]
        for face in range(6):
            axis = face // 2
            spot = others(node, axis)
            base = 3 * NODES + face * 2 * FACE
            de[node, base + FACE + spot] = dmat[layer_of(face), coords(node)[axis]]
            if coords(node)[axis] == layer_of(face):
                de[node, base + spot] = 1.0
                place[face, :, spot, node] = 1.0
    turn = np.zeros((FACE, 8, FACE), np.float32)
    for code in range(8):
        for i in range(QN):
            for j in range(QN):
                a = QN - 1 - i if code & 2 else i
                b = QN - 1 - j if code & 1 else j
                if code & 4:
                    a, b = b, a
                turn[a * QN + b, code, i * QN + j] = 1.0
    rtab = vertex_table().astype(np.float32)
    restrict = np.zeros((NODES, WIDE), np.float32)
    restrict[:, :KC] = np.tile(rtab.T, (1, CG * VARS))
    spread = np.ascontiguousarray(restrict.T)
    own_lanes = np.zeros((RW, ROWS), np.float32)
    for row in range(RW):
        v = row % STRIDE
        if v < VARS:
            own_lanes[row, v * NODES : (v + 1) * NODES] = 1.0
    cols = SOURCES * 2 * RW
    tile = np.zeros((16, cols), np.float32)
    colcode = np.zeros((8, cols), np.float32)
    for col in range(cols):
        source, kind, n, v = col // (2 * RW), col // RW % 2, col // STRIDE % ELEMS, col % STRIDE
        if v < VARS:
            tile[kind * 8 + v, col] = 1.0
        colcode[0, col] = source * ELEMS + n
        for axis in range(3):
            colcode[1 + axis, col] = (-1.0 if v == 1 + axis else 1.0) * (-1.0 if kind else 1.0)
    vtile = np.zeros((24, 3 * RW), np.float32)
    vmask = np.zeros((RW, 3 * RW), np.float32)
    for col in range(3 * RW):
        axis, n, v = col // RW, col // STRIDE % ELEMS, col % STRIDE
        if v < VARS:
            vtile[axis * 8 + v, col] = 1.0
        vmask[n * STRIDE : (n + 1) * STRIDE, col] = 1.0
    return dict(
        de=de,
        place=place.reshape(6 * 8 * FACE, NODES),
        turn=turn.reshape(FACE, 8 * FACE),
        restrict=restrict,
        spread=spread,
        own_lanes=own_lanes,
        tile=tile,
        colcode=colcode,
        vtile=vtile,
        vmask=vmask,
    )


def exact_dot(a, b):
    return jnp.dot(a, b, precision=HIGHEST, preferred_element_type=F32)


def exact_dot_t(a, b):
    return lax.dot_general(
        a, b, (((1,), (1,)), ((), ())), precision=HIGHEST, preferred_element_type=F32
    )


def total(values):
    return jnp.sum(values, axis=(0, 1), keepdims=True)


def member_mask(group_ref):
    row = lax.broadcasted_iota(jnp.int32, (STRIDE, WIDE), 0)
    lane = lax.broadcasted_iota(jnp.int32, (STRIDE, WIDE), 1)
    pieces = []
    for e in range(ELEMS):
        hit = (lane // (VARS * 8) == group_ref[e]) & (lane // 8 % VARS == row)
        pieces.append(jnp.where(hit & (lane < KC), 1.0, 0.0))
    return jnp.concatenate(pieces, axis=0)


def message(member, restrict, vector, scalars):
    row = jnp.sum(member * exact_dot(vector, restrict), axis=0, keepdims=True)
    lane = lax.broadcasted_iota(jnp.int32, (1, WIDE), 1)
    for i, value in enumerate(scalars):
        row = jnp.where(lane == SCALAR0 + i, value, row)
    return row


def read_scalars(table_ref, count):
    sums = jnp.sum(table_ref[:, 128:256], axis=0, keepdims=True)
    return [sums[:, SCALAR0 - 128 + i : SCALAR0 - 128 + i + 1] for i in range(count)]


def read_coarse(table_ref, pos_ref):
    rows = table_ref[pl.ds(pl.multiple_of(pos_ref[0] * 8, 8), 8), :]
    row = lax.broadcasted_iota(jnp.int32, (8, WIDE), 0)
    return jnp.sum(jnp.where(row % 2 == pos_ref[2], rows, 0.0), axis=0, keepdims=True)


def coarse_values(coarse, cinv_ref, member_ref, spread_ref):
    solved = exact_dot_t(coarse[:, :KC], cinv_ref[0, 0])
    return exact_dot(member_ref[:, :KC] * solved, spread_ref[:KC, :])


def apply_blocks(blocks_ref, own_lanes, parts):
    stacked = []
    for part in parts:
        pair = jnp.concatenate([part, part], axis=1)
        stacked.append(jnp.concatenate([pair, pair, part], axis=1) * own_lanes)
    wide = jnp.concatenate(stacked, axis=0).astype(jnp.bfloat16)
    pieces = []
    for e in range(ELEMS):
        out = lax.dot_general(
            wide, blocks_ref[e], (((1,), (1,)), ((), ())), preferred_element_type=F32
        )
        mine = out[e * STRIDE : (e + 1) * STRIDE]
        for i in range(1, len(parts)):
            mine = mine + out[i * RW + e * STRIDE : i * RW + (e + 1) * STRIDE]
        pieces.append(jnp.broadcast_to(jnp.sum(mine, axis=0, keepdims=True), (STRIDE, ROWS)))
    full = jnp.concatenate(pieces, axis=0) * own_lanes
    half = full[:, :128] + full[:, 128:256]
    return half[:, :NODES] + half[:, NODES:] + full[:, 256:]


def rounded(values):
    return [values.astype(jnp.bfloat16).astype(F32)]


def two_parts(values):
    high = values.astype(jnp.bfloat16).astype(F32)
    return [high, values - high]


def face_of(grown, face):
    base = 3 * NODES + face * 2 * FACE
    return grown[:, base : base + 2 * FACE]


def write_sends(pos_ref, grown, send_refs):
    p_odd, s_odd, r = pos_ref[0] % 2, pos_ref[1] % 2, pos_ref[2]
    faces = [face_of(grown, f) for f in range(6)]
    send_refs[0][...] = jnp.where(p_odd == 0, faces[1], faces[0])
    send_refs[1][...] = jnp.where(p_odd == 0, faces[0], faces[1])
    send_refs[2][...] = jnp.where(s_odd == 0, faces[3], faces[2])
    send_refs[3][...] = jnp.where(s_odd == 0, faces[2], faces[3])
    send_refs[4][...] = jnp.where(r == 0, faces[5], faces[4])


def jacobian(vector, grown, recv, mass, amat, omask, vmat, turn, place):
    slopes = jnp.concatenate([grown[:, i * NODES : (i + 1) * NODES] for i in range(3)], axis=0)
    result = 1.5 * mass * vector + exact_dot(vmat, slopes)
    pieces = []
    for source in list(recv) + [face_of(grown, f) for f in range(2, 6)]:
        pieces += [source[:, :FACE], source[:, FACE : 2 * FACE]]
    terms = exact_dot(amat, jnp.concatenate(pieces, axis=0))
    laid = exact_dot(terms, turn) * omask
    laid = jnp.concatenate([laid[f * RW : (f + 1) * RW] for f in range(6)], axis=1)
    return result + exact_dot(laid, place)


def start_kernel(rs_ref, mass_ref, group_ref, restrict_ref, x_ref, massw_ref, member_ref, table_ref):
    x_ref[...] = jnp.zeros_like(x_ref)
    massw_ref[...] = jnp.zeros_like(massw_ref)
    for e in range(ELEMS):
        for v in range(VARS):
            lanes = slice(v * NODES, (v + 1) * NODES)
            row = e * STRIDE + v
            x_ref[row : row + 1, :] = rs_ref[e : e + 1, lanes]
            massw_ref[row : row + 1, :] = mass_ref[e : e + 1, lanes]
    member = member_mask(group_ref)
    member_ref[...] = member
    x = x_ref[...]
    row = message(member, restrict_ref[...], x, [total(x * x)])
    table_ref[...] = jnp.broadcast_to(row, table_ref.shape)


def setup_kernel(
    pos_ref,
    neigh_ref,
    orient_ref,
    tags_ref,
    vj_ref,
    flux_ref,
    visc_ref,
    tile_ref,
    colcode_ref,
    vtile_ref,
    vmask_ref,
    amat_ref,
    omask_ref,
    vmat_ref,
    coef_ref,
    vcoef_ref,
):
    p_odd, s_odd = pos_ref[0] % 2, pos_ref[1] % 2
    device = pos_ref[3]
    coef_ref[...] = jnp.zeros_like(coef_ref)
    vcoef_ref[...] = jnp.zeros_like(vcoef_ref)
    for e in range(ELEMS):
        for axis in range(3):
            vcoef_ref[e * STRIDE : e * STRIDE + VARS, axis * 8 : axis * 8 + VARS] = vj_ref[e, axis]
        for f in range(6):
            row = f * RW + e * STRIDE
            coef_ref[row : row + VARS, 0:VARS] = flux_ref[e, f]
            coef_ref[row : row + VARS, 8 : 8 + VARS] = visc_ref[e, f]
    vmat_ref[...] = exact_dot(vcoef_ref[...], vtile_ref[...]) * vmask_ref[...]
    cols = SOURCES * 2 * RW
    lane = lax.broadcasted_iota(jnp.int32, (STRIDE, 8 * FACE), 1)
    colcode = jnp.broadcast_to(colcode_ref[0:1, :], (STRIDE, cols))
    for f in range(6):
        axis = f // 2
        spread = exact_dot(coef_ref[f * RW : (f + 1) * RW, :], tile_ref[...])
        signs = jnp.broadcast_to(colcode_ref[1 + axis : 2 + axis, :], (STRIDE, cols))
        for e in range(ELEMS):
            near = neigh_ref[e, f]
            tag = tags_ref[e, f]
            spot = near % ELEMS
            crossing = near // ELEMS != device
            if f == 0:
                source = 1 - p_odd
            elif f == 1:
                source = p_odd
            elif f == 2:
                source = 3 - s_odd
            elif f == 3:
                source = 2 + s_odd
            else:
                source = jnp.where(crossing, 4, 8 if f == 4 else 7)
            code = source * ELEMS + spot
            turn_code = orient_ref[e, f]
            if f >= 2:
                wall_code = (5 + f - 2) * ELEMS + e
                code = jnp.where(tag == 0, code, jnp.where(tag == 1, wall_code, -1))
                turn_code = jnp.where(tag == 0, turn_code, 0)
            rows = slice(f * RW + e * STRIDE, f * RW + (e + 1) * STRIDE)
            values = spread[e * STRIDE : (e + 1) * STRIDE]
            values = jnp.where(tag == 1, values * signs, values)
            amat_ref[rows, :] = jnp.where(colcode == code.astype(F32), -values, 0.0)
            omask_ref[rows, :] = jnp.where(lane // FACE == turn_code, 1.0, 0.0)


def first_kernel(step, *refs):
    if step == 0:
        pos, table, x, blocks, cinv, member, spread, own, de = refs[:9]
        z_ref, coarse_ref, scal_ref, first_ref, grown_ref, *sends = refs[9:]
        beta = jnp.sqrt(read_scalars(table, 1)[0])
        z = x[...] / beta
        coarse = read_coarse(table, pos) / beta
        scal_ref[...] = jnp.broadcast_to(beta, scal_ref.shape)
        parts = rounded(z)
    elif step == 1:
        pos, table, x, b0, coarse0, blocks, cinv, member, spread, own, de = refs[:11]
        z_ref, scal_ref, first_ref, grown_ref, *sends = refs[11:]
        h00, square = read_scalars(table, 2)
        h10 = jnp.sqrt(jnp.maximum(square - h00 * h00, 1e-7 * square))
        z = (x[...] - h00 * b0[...]) / h10
        coarse = (read_coarse(table, pos) - h00 * coarse0[...]) / h10
        row = lax.broadcasted_iota(jnp.int32, scal_ref.shape, 0)
        scal_ref[...] = jnp.where(row == 0, h00, jnp.where(row == 1, h10, square))
        parts = rounded(z)
    else:
        pos, c0, c1, c2, c3, x, blocks, cinv, member, spread, own, de = refs[:12]
        first_ref, grown_ref, *sends = refs[12:]
        z_ref = None
        z = x[...]
        coarse = (c0[...] + c1[...]) + (c2[...] + c3[...])
        parts = two_parts(z)
    if z_ref is not None:
        z_ref[...] = z
    if step == 0:
        coarse_ref[...] = coarse
    first = apply_blocks(blocks, own[...], parts) + coarse_values(coarse, cinv, member, spread)
    first_ref[...] = first
    grown = exact_dot(first, de[...])
    grown_ref[...] = grown
    write_sends(pos, grown, sends)


def second_kernel(step, *refs):
    pos, z, first, grown = refs[:4]
    recv = [r[...] for r in refs[4:9]]
    mass, amat, omask, vmat, turn, place, blocks, own, de = refs[9:18]
    search_ref, grown2_ref, *sends = refs[18:]
    mapped = jacobian(
        first[...],
        grown[...],
        recv,
        mass[...],
        amat[...],
        omask[...],
        vmat[...],
        turn[...],
        place[...],
    )
    defect = z[...] - mapped
    parts = two_parts(defect) if step == 2 else rounded(defect)
    search = first[...] + apply_blocks(blocks, own[...], parts)
    search_ref[...] = search
    grown2 = exact_dot(search, de[...])
    grown2_ref[...] = grown2
    write_sends(pos, grown2, sends)


def third_kernel(step, *refs):
    search, grown = refs[:2]
    recv = [r[...] for r in refs[2:7]]
    mass, amat, omask, vmat, turn, place = refs[7:13]
    mapped = jacobian(
        search[...],
        grown[...],
        recv,
        mass[...],
        amat[...],
        omask[...],
        vmat[...],
        turn[...],
        place[...],
    )
    if step == 0:
        member, restrict, b0, w_ref, table_ref = refs[13:]
        scalars = [total(mapped * b0[...]), total(mapped * mapped)]
        row = message(member[...], restrict[...], mapped, scalars)
        table_ref[...] = jnp.broadcast_to(row, table_ref.shape)
    elif step == 1:
        member, restrict, w_ref, row_ref = refs[13:]
        row_ref[...] = message(member[...], restrict[...], mapped, [])
    else:
        b0, b1, w1, w_ref, table_ref = refs[13:]
        scalars = [total(w1[...] * b[...]) for b in (b0, b1, w1)]
        scalars += [total(mapped * b[...]) for b in (b0, b1, w1)]
        scalars += [total(mapped * mapped)]
        lane = lax.broadcasted_iota(jnp.int32, (1, 128), 1)
        row = jnp.zeros((1, 128), F32)
        for i, value in enumerate(scalars):
            row = jnp.where(lane == i, value, row)
        table_ref[...] = jnp.broadcast_to(row, table_ref.shape)
    w_ref[...] = mapped


def least_squares(matrix, beta):
    iters = len(matrix) - 1
    target = [beta] + [jnp.zeros_like(beta)] * iters
    for k in range(iters):
        top, low = matrix[k][k], matrix[k + 1][k]
        radius = jnp.sqrt(top * top + low * low)
        cosine, sine = top / radius, low / radius
        for later in range(k, iters):
            upper, lower = matrix[k][later], matrix[k + 1][later]
            matrix[k][later] = cosine * upper + sine * lower
            matrix[k + 1][later] = -sine * upper + cosine * lower
        upper, lower = target[k], target[k + 1]
        target[k] = cosine * upper + sine * lower
        target[k + 1] = -sine * upper + cosine * lower
    weights = [None] * iters
    for k in reversed(range(iters)):
        value = target[k]
        for later in range(k + 1, iters):
            value = value - matrix[k][later] * weights[later]
        weights[k] = value / matrix[k][k]
    return weights


def final_kernel(table, scal0, scal1, x, s0, s1, s2, w0, w1, w2, update_ref, residual_ref):
    sums = jnp.sum(table[...], axis=0, keepdims=True)
    g0, g1, g2, q0, q1, qw, qq = [sums[:, i : i + 1] for i in range(7)]
    beta = scal0[0:1, 0:1]
    h00, h10, square0 = [scal1[i : i + 1, 0:1] for i in range(3)]
    h01, h11 = g0, g1
    h21 = jnp.sqrt(jnp.maximum(g2 - h01 * h01 - h11 * h11, 1e-7 * g2))
    cross = h00 * h01 + h10 * h11
    h02 = (q0 - h01 * h00 - h11 * h01) / h21
    h12 = (q1 - h01 * h10 - h11 * h11) / h21
    with_w1 = (qw - h01 * cross - h11 * g2) / h21
    h22 = (with_w1 - h01 * h02 - h11 * h12) / h21
    with_w0 = h00 * q0 + h10 * q1
    square = qq + h01 * h01 * square0 + h11 * h11 * g2
    square = square - 2.0 * (h01 * with_w0 + h11 * qw - h01 * h11 * cross)
    square = square / (h21 * h21)
    h32 = jnp.sqrt(jnp.maximum(square - h02 * h02 - h12 * h12 - h22 * h22, 1e-7 * square))
    zero = jnp.zeros_like(beta)
    hess = [[h00, h01, h02], [h10, h11, h12], [zero, h21, h22], [zero, zero, h32]]
    y0, y1, y2 = least_squares(hess, beta)
    y2 = y2 / h21
    y0 = y0 - y2 * h01
    y1 = y1 - y2 * h11
    update = y0 * s0[...] + y1 * s1[...] + y2 * s2[...]
    residual = x[...] - (y0 * w0[...] + y1 * w1[...] + y2 * w2[...])
    for e in range(ELEMS):
        for v in range(VARS):
            lanes = slice(v * NODES, (v + 1) * NODES)
            row = e * STRIDE + v
            update_ref[e : e + 1, lanes] = update[row : row + 1, :]
            residual_ref[e : e + 1, lanes] = residual[row : row + 1, :]


VMEM = pltpu.VMEM
SMEM = pltpu.SMEM


def call(kernel, name, args, outs, smem=(), scratch=()):
    return pl.pallas_call(
        kernel,
        name=name,
        out_shape=[jax.ShapeDtypeStruct(shape, F32) for shape in outs],
        in_specs=[
            pl.BlockSpec(memory_space=SMEM if i in smem else VMEM) for i in range(len(args))
        ],
        out_specs=[pl.BlockSpec(memory_space=VMEM)] * len(outs),
        scratch_shapes=[VMEM(shape, F32) for shape in scratch],
        compiler_params=pltpu.CompilerParams(vmem_limit_bytes=32 * 1024 * 1024),
    )(*args)


def with_step(kernel, step):
    def run(*refs):
        kernel(step, *refs)

    return run


def body(
    right_side,
    mass,
    volume_jac,
    face_flux,
    face_visc,
    block_inverse,
    coarse_inverse,
    neighbours,
    orientation,
    bc_tags,
    coarse_group,
):
    t = {name: jnp.asarray(value) for name, value in tables().items()}
    n_pass, n_span = lax.axis_size("passage"), lax.axis_size("span")
    n_rad = lax.axis_size("radial")
    devices = n_pass * n_span * n_rad
    p, s, r = (lax.axis_index(a) for a in AXES)
    pos = jnp.stack([p, s, r, (p * n_span + s) * n_rad + r]).astype(jnp.int32)

    pass_a = [(i, i ^ 1) for i in range(n_pass)]
    pass_b = [(i, (i + 1 if i % 2 else i - 1) % n_pass) for i in range(n_pass)]
    span_a = [(i, i ^ 1) for i in range(n_span)]
    span_b = [(i, i + 1 if i % 2 else i - 1) for i in range(1, n_span - 1)]
    rad = [(0, 1), (1, 0)]

    def exchange(sends):
        got = [None] * 5
        got[4] = lax.ppermute(sends[4], "radial", rad)
        got[3] = lax.ppermute(sends[3], "span", span_b)
        got[2] = lax.ppermute(sends[2], "span", span_a)
        got[1] = lax.ppermute(sends[1], "passage", pass_b)
        got[0] = lax.ppermute(sends[0], "passage", pass_a)
        return got

    vec = (RW, NODES)
    grow = (RW, t["de"].shape[1])
    send = (RW, 2 * FACE)

    x, massw, member, table = call(
        start_kernel,
        "start",
        (right_side, mass, coarse_group, t["restrict"]),
        [vec, vec, (RW, WIDE), (devices, WIDE)],
        smem=(2,),
    )
    amat, omask, vmat = call(
        setup_kernel,
        "setup",
        (
            pos,
            neighbours,
            orientation,
            bc_tags,
            volume_jac,
            face_flux,
            face_visc,
            t["tile"],
            t["colcode"],
            t["vtile"],
            t["vmask"],
        ),
        [(6 * RW, SOURCES * 2 * RW), (6 * RW, 8 * FACE), (RW, 3 * RW)],
        smem=(0, 1, 2, 3),
        scratch=[(6 * RW, 16), (RW, 24)],
    )
    operator = (massw, amat, omask, vmat, t["turn"], t["place"])
    table = lax.all_to_all(table, AXES, 0, 0, tiled=True)

    basis, search, images, scalars = [], [], [], []
    coarse0 = row = None
    for step in range(3):
        tail = (block_inverse, coarse_inverse, member, t["spread"], t["own_lanes"], t["de"])
        outs = [vec, grow] + [send] * 5
        kernel = with_step(first_kernel, step)
        if step == 0:
            z, coarse0, scal, first, grown, *sends = call(
                kernel,
                "first0",
                (pos, table, x) + tail,
                [vec, (1, WIDE), (8, 128)] + outs,
                smem=(0,),
            )
            scalars.append(scal)
        elif step == 1:
            z, scal, first, grown, *sends = call(
                kernel,
                "first1",
                (pos, table, images[0], basis[0], coarse0) + tail,
                [vec, (8, 128)] + outs,
                smem=(0,),
            )
            scalars.append(scal)
        else:
            rows = [lax.ppermute(row, "span", [(i, i ^ k) for i in range(n_span)]) for k in (2, 3, 1)]
            z = images[1]
            first, grown, *sends = call(
                kernel, "first2", (pos, row, *rows, z) + tail, outs, smem=(0,)
            )
        basis.append(z)
        recv = exchange(sends)
        direction, grown, *sends = call(
            with_step(second_kernel, step),
            "second%d" % step,
            (pos, z, first, grown, *recv) + operator + (block_inverse, t["own_lanes"], t["de"]),
            outs,
            smem=(0,),
        )
        search.append(direction)
        recv = exchange(sends)
        kernel = with_step(third_kernel, step)
        head = (direction, grown, *recv) + operator
        if step == 0:
            image, table = call(
                kernel,
                "third0",
                head + (member, t["restrict"], basis[0]),
                [vec, (devices, WIDE)],
            )
            table = lax.all_to_all(table, AXES, 0, 0, tiled=True)
        elif step == 1:
            image, row = call(kernel, "third1", head + (member, t["restrict"]), [vec, (1, WIDE)])
        else:
            image, table = call(
                kernel,
                "third2",
                head + (basis[0], basis[1], basis[2]),
                [vec, (devices, 128)],
            )
            table = lax.all_to_all(table, AXES, 0, 0, tiled=True)
        images.append(image)

    update, residual = call(
        final_kernel,
        "final",
        (table, *scalars, x, *search, *images),
        [right_side.shape] * 2,
    )
    return (update, residual)


def solution(mesh):
    rows = P(AXES, None)
    blocks = P(AXES, None, None)
    jac = P(AXES, None, None, None)
    in_specs = (
        rows,
        rows,
        jac,
        jac,
        jac,
        blocks,
        P("passage", "radial", None, None),
        rows,
        rows,
        rows,
        P(AXES),
    )
    return jax.shard_map(body, mesh=mesh, in_specs=in_specs, out_specs=(rows, rows), check_vma=False)
```

profile of v0, /device:TPU:1, one launch (start us, length us, event | category | flops | bytes accessed | tf_op | source)
XLA Modules:
  0.0 169.3 jit_solution(5101910401256102835)
XLA Ops:
  5.4 15.7 %all-to-all-start = ((f32[256,1,256]{2,1,0:T(1,128)}), f32[256,1,256]{2,1,0:T(1,128)S(1)}, u32[]{:S(2)}, u32[]{:S(2)}) async-start(f32[256,1,256]{2,1,0:T(1,128)} %copy.26), calls=%async_computation | async-start | bytes 524288 | tf_op jit(solution)/shard_map/all_to_all | solution.py:573
  21.1 15.1 %all-to-all-done = f32[256,1,256]{2,1,0:T(1,128)S(1)} async-done(((f32[256,1,256]{2,1,0:T(1,128)}), f32[256,1,256]{2,1,0:T(1,128)S(1)}, u32[]{:S(2)}, u32[]{:S(2)}) %all-to-all-start) | async-done | bytes 262176 | tf_op jit(solution)/shard_map/all_to_all | solution.py:573
  36.4 1.9 %first0.1 = (f32[32,64]{1,0:T(8,128)S(1)}, f32[1,256]{1,0:T(1,128)S(1)}, f32[8,128]{1,0:T(8,128)S(1)}, f32[32,64]{1,0:T(8,128)S(1)}, f32[32,384]{1,0:T(8,128)S(1...) custom-call(s32[4]{0:T(128)S(1)} %pad_add_fusion.refs_0_.pos_ref, ...), custom_call_target="tpu_custom_call" | custom-call | tf_op jit(solution)/shard_map/first0/pallas_call | solution.py:486
  40.4 1.5 collective-permute-start.4
  42.7 1.3 setup.1
  44.7 2.8 %second0.1 = (f32[32,64]{1,0:T(8,128)S(1)}, f32[32,384]{1,0:T(8,128)S(1)}, f32[32,32]{1,0:T(8,128)S(1)}, f32[32,32]{1,0:T(8,128)S(1)}, f32[32,32]{1,0:T(8,128)S(...) custom-call(s32[4]{0:T(128)S(1)} %pad_add_fusion.refs_0_.pos_ref, ...), custom_call_target="tpu_custom_call" | custom-call | tf_op jit(solution)/shard_map/second0/pallas_call | solution.py:486
  47.5 2.0 %collective-permute-start.5 = (f32[32,32]{1,0:T(8,128)S(1)}, f32[32,32]{1,0:T(8,128)S(1)}, u32[]{:S(2)}, u32[]{:S(2)}) collective-permute-start(f32[32,32]{1,0:T(8,128)S(1)} %get-tuple-element.79), channel_id=1, source_target_pairs={{0,8},{8,0},{16,24},{24,16},{32,40},{40,32},{48,56},{56,48},{64,72... | collective-permute-start | bytes 12296 | tf_op jit(solution)/shard_map/ppermute | solution.py:538
  50.2 3.2 %collective-permute-start.7 = (f32[32,32]{1,0:T(8,128)S(1)}, f32[32,32]{1,0:T(8,128)S(1)}, u32[]{:S(2)}, u32[]{:S(2)}) collective-permute-start(f32[32,32]{1,0:T(8,128)S(1)} %get-tuple-element.81), channel_id=1, source_target_pairs={{0,2},{2,0},{4,6},{6,4},{1,3},{3,1},{5,7},{7,5},{8,10},{10,8},{12,... | collective-permute-start | bytes 12296 | tf_op jit(solution)/shard_map/ppermute | solution.py:536
  55.1 3.1 %collective-permute-done.9.refs_6_ = f32[32,32]{1,0:T(8,128)S(1)} collective-permute-done((f32[32,32]{1,0:T(8,128)S(1)}, f32[32,32]{1,0:T(8,128)S(1)}, u32[]{:S(2)}, u32[]{:S(2)}) %collective-permute-start.9) | collective-permute-done | bytes 4128 | tf_op jit(solution)/shard_map/ppermute | solution.py:534
  58.2 1.7 third0.1
  60.2 25.7 %all_to_all.33 = f32[256,1,256]{2,1,0:T(1,128)S(1)} all-to-all(f32[256,1,256]{2,1,0:T(1,128)S(1)} %copy.30), channel_id=1, replica_groups=mesh['passage'=32,'span'=4,'radial'=2] {'passage','span','radial'}, dimensions={0} | all-to-all | bytes 524288 | tf_op jit(solution)/shard_map/all_to_all | solution.py:625
  85.9 2.0 %first1.1 = (f32[32,64]{1,0:T(8,128)S(1)}, f32[8,128]{1,0:T(8,128)S(1)}, f32[32,64]{1,0:T(8,128)S(1)}, f32[32,384]{1,0:T(8,128)S(1)}, f32[32,32]{1,0:T(8,128)S(1...) custom-call(s32[4]{0:T(128)S(1)} %pad_add_fusion.refs_0_.pos_ref, ...), custom_call_target="tpu_custom_call" | custom-call | tf_op jit(solution)/shard_map/first1/pallas_call | solution.py:486
  90.0 1.4 collective-permute-start.14
  91.7 2.5 %collective-permute-done.14.refs_8_ = f32[32,32]{1,0:T(8,128)S(1)} collective-permute-done((f32[32,32]{1,0:T(8,128)S(1)}, f32[32,32]{1,0:T(8,128)S(1)}, u32[]{:S(2)}, u32[]{:S(2)}) %collective-permute-start.14) | collective-permute-done | bytes 4128 | tf_op jit(solution)/shard_map/ppermute | solution.py:534
  94.2 2.9 %second1.1 = (f32[32,64]{1,0:T(8,128)S(1)}, f32[32,384]{1,0:T(8,128)S(1)}, f32[32,32]{1,0:T(8,128)S(1)}, f32[32,32]{1,0:T(8,128)S(1)}, f32[32,32]{1,0:T(8,128)S(...) custom-call(s32[4]{0:T(128)S(1)} %pad_add_fusion.refs_0_.pos_ref, f32[32,64]{1,0:T(8,128)S(1)} %get-tuple-element.87.refs_1_.refs_14_, ...), custom_call_target="tpu_custom_call" | custom-call | tf_op jit(solution)/shard_map/second1/pallas_call | solution.py:486
  97.0 1.8 %collective-permute-start.15 = (f32[32,32]{1,0:T(8,128)S(1)}, f32[32,32]{1,0:T(8,128)S(1)}, u32[]{:S(2)}, u32[]{:S(2)}) collective-permute-start(f32[32,32]{1,0:T(8,128)S(1)} %get-tuple-element.97), channel_id=1, source_target_pairs={{0,8},{8,0},{16,24},{24,16},{32,40},{40,32},{48,56},{56,48},{64,72... | collective-permute-start | bytes 12296 | tf_op jit(solution)/shard_map/ppermute | solution.py:538
  99.8 3.1 %collective-permute-start.17 = (f32[32,32]{1,0:T(8,128)S(1)}, f32[32,32]{1,0:T(8,128)S(1)}, u32[]{:S(2)}, u32[]{:S(2)}) collective-permute-start(f32[32,32]{1,0:T(8,128)S(1)} %get-tuple-element.99), channel_id=1, source_target_pairs={{0,2},{2,0},{4,6},{6,4},{1,3},{3,1},{5,7},{7,5},{8,10},{10,8},{12,... | collective-permute-start | bytes 12296 | tf_op jit(solution)/shard_map/ppermute | solution.py:536
  104.6 3.1 %collective-permute-done.19.refs_6_ = f32[32,32]{1,0:T(8,128)S(1)} collective-permute-done((f32[32,32]{1,0:T(8,128)S(1)}, f32[32,32]{1,0:T(8,128)S(1)}, u32[]{:S(2)}, u32[]{:S(2)}) %collective-permute-start.19) | collective-permute-done | bytes 4128 | tf_op jit(solution)/shard_map/ppermute | solution.py:534
  107.8 1.7 third1.1
  109.4 2.5 %collective-permute-start.22 = (f32[1,256]{1,0:T(1,128)S(1)}, f32[1,256]{1,0:T(1,128)S(1)}, u32[]{:S(2)}, u32[]{:S(2)}) collective-permute-start(f32[1,256]{1,0:T(1,128)S(1)} %get-tuple-element.103.refs_1_), channel_id=1, source_target_pairs={{0,2},{2,0},{4,6},{6,4},{1,3},{3,1},{5,7},{7,5},{8,10},{10,8},{12,... | collective-permute-start | bytes 3080 | tf_op jit(solution)/shard_map/ppermute | solution.py:600
  113.8 1.7 %collective-permute-done.21.refs_3_ = f32[1,256]{1,0:T(1,128)S(1)} collective-permute-done((f32[1,256]{1,0:T(1,128)S(1)}, f32[1,256]{1,0:T(1,128)S(1)}, u32[]{:S(2)}, u32[]{:S(2)}) %collective-permute-start.21) | collective-permute-done | bytes 1056 | tf_op jit(solution)/shard_map/ppermute | solution.py:600
  116.7 1.8 %first2.1 = (f32[32,64]{1,0:T(8,128)S(1)}, f32[32,384]{1,0:T(8,128)S(1)}, f32[32,32]{1,0:T(8,128)S(1)}, f32[32,32]{1,0:T(8,128)S(1)}, f32[32,32]{1,0:T(8,128)S(1...) custom-call(s32[4]{0:T(128)S(1)} %pad_add_fusion.refs_0_.pos_ref, f32[1,256]{1,0:T(1,128)S(1)} %get-tuple-element.103.refs_1_, ...), custom_call_target="tpu_custom_call" | custom-call | tf_op jit(solution)/shard_map/first2/pallas_call | solution.py:486
  118.5 3.7 %collective-permute-start.23 = (f32[32,32]{1,0:T(8,128)S(1)}, f32[32,32]{1,0:T(8,128)S(1)}, u32[]{:S(2)}, u32[]{:S(2)}) collective-permute-start(f32[32,32]{1,0:T(8,128)S(1)} %get-tuple-element.106), channel_id=1, source_target_pairs={{0,8},{8,0},{16,24},{24,16},{32,40},{40,32},{48,56},{56,48},{64,72... | collective-permute-start | bytes 12296 | tf_op jit(solution)/shard_map/ppermute | solution.py:538
  123.8 1.4 collective-permute-start.27
  126.1 2.5 %collective-permute-done.27.refs_8_ = f32[32,32]{1,0:T(8,128)S(1)} collective-permute-done((f32[32,32]{1,0:T(8,128)S(1)}, f32[32,32]{1,0:T(8,128)S(1)}, u32[]{:S(2)}, u32[]{:S(2)}) %collective-permute-start.27) | collective-permute-done | bytes 4128 | tf_op jit(solution)/shard_map/ppermute | solution.py:534
  128.6 2.9 %second2.1 = (f32[32,64]{1,0:T(8,128)S(1)}, f32[32,384]{1,0:T(8,128)S(1)}, f32[32,32]{1,0:T(8,128)S(1)}, f32[32,32]{1,0:T(8,128)S(1)}, f32[32,32]{1,0:T(8,128)S(...) custom-call(s32[4]{0:T(128)S(1)} %pad_add_fusion.refs_0_.pos_ref, ...), custom_call_target="tpu_custom_call" | custom-call | tf_op jit(solution)/shard_map/second2/pallas_call | solution.py:486
  133.1 4.4 %collective-permute-start.30 = (f32[32,32]{1,0:T(8,128)S(1)}, f32[32,32]{1,0:T(8,128)S(1)}, u32[]{:S(2)}, u32[]{:S(2)}) collective-permute-start(f32[32,32]{1,0:T(8,128)S(1)} %get-tuple-element.115), channel_id=1, source_target_pairs={{0,2},{2,0},{4,6},{6,4},{1,3},{3,1},{5,7},{7,5},{8,10},{10,8},{12,... | collective-permute-start | bytes 12296 | tf_op jit(solution)/shard_map/ppermute | solution.py:536
  138.1 1.5 collective-permute-start.32
  139.6 2.7 %collective-permute-done.32.refs_6_ = f32[32,32]{1,0:T(8,128)S(1)} collective-permute-done((f32[32,32]{1,0:T(8,128)S(1)}, f32[32,32]{1,0:T(8,128)S(1)}, u32[]{:S(2)}, u32[]{:S(2)}) %collective-permute-start.32) | collective-permute-done | bytes 4128 | tf_op jit(solution)/shard_map/ppermute | solution.py:534
  142.3 1.6 third2.1
  143.9 23.9 %all_to_all.34 = f32[256,1,128]{2,1,0:T(1,128)S(1)} all-to-all(f32[256,1,128]{2,1,0:T(1,128)S(1)} %bitcast.21), channel_id=1, replica_groups=mesh['passage'=32,'span'=4,'radial'=2] {'passage','span','radial'}, dimensions={0} | all-to-all | bytes 262144 | tf_op jit(solution)/shard_map/all_to_all | solution.py:635
  167.8 1.4 final.1
  (102 shorter events, 23.9 us)
Async XLA Ops:
  5.4 30.8 %all-to-all-start = ((f32[256,1,256]{2,1,0:T(1,128)}), f32[256,1,256]{2,1,0:T(1,128)S(1)}, u32[]{:S(2)}, u32[]{:S(2)}) async-start(f32[256,1,256]{2,1,0:T(1,128)} %copy.26), calls=%async_computation | async-start | bytes 524288 | tf_op jit(solution)/shard_map/all_to_all | solution.py:573
  38.3 5.7 %collective-permute-start = (f32[32,32]{1,0:T(8,128)S(1)}, f32[32,32]{1,0:T(8,128)S(1)}, u32[]{:S(2)}, u32[]{:S(2)}) collective-permute-start(f32[32,32]{1,0:T(8,128)S(1)} %get-tuple-element.68), channel_id=1, source_target_pairs={{0,8},{8,0},{16,24},{24,16},{32,40},{40,32},{48,56},{56,48},{64,72... | collective-permute-start | bytes 12296 | tf_op jit(solution)/shard_map/ppermute | solution.py:538
  39.1 5.0 %collective-permute-start.1 = (f32[32,32]{1,0:T(8,128)S(1)}, f32[32,32]{1,0:T(8,128)S(1)}, u32[]{:S(2)}, u32[]{:S(2)}) collective-permute-start(f32[32,32]{1,0:T(8,128)S(1)} %get-tuple-element.69), channel_id=1, source_target_pairs={{0,248},{8,16},{16,8},{24,32},{32,24},{40,48},{48,40},{56,64},{64,... | collective-permute-start | bytes 12296 | tf_op jit(solution)/shard_map/ppermute | solution.py:537
  39.7 4.3 %collective-permute-start.2 = (f32[32,32]{1,0:T(8,128)S(1)}, f32[32,32]{1,0:T(8,128)S(1)}, u32[]{:S(2)}, u32[]{:S(2)}) collective-permute-start(f32[32,32]{1,0:T(8,128)S(1)} %get-tuple-element.70), channel_id=1, source_target_pairs={{0,2},{2,0},{4,6},{6,4},{1,3},{3,1},{5,7},{7,5},{8,10},{10,8},{12,... | collective-permute-start | bytes 12296 | tf_op jit(solution)/shard_map/ppermute | solution.py:536
  39.7 4.3 %collective-permute-start.3 = (f32[32,32]{1,0:T(8,128)S(1)}, f32[32,32]{1,0:T(8,128)S(1)}, u32[]{:S(2)}, u32[]{:S(2)}) collective-permute-start(f32[32,32]{1,0:T(8,128)S(1)} %get-tuple-element.71), channel_id=1, source_target_pairs={{2,4},{4,2},{3,5},{5,3},{10,12},{12,10},{11,13},{13,11},{18,20},{2... | collective-permute-start | bytes 12296 | tf_op jit(solution)/shard_map/ppermute | solution.py:535
  40.4 4.2 %collective-permute-start.4 = (f32[32,32]{1,0:T(8,128)S(1)}, f32[32,32]{1,0:T(8,128)S(1)}, u32[]{:S(2)}, u32[]{:S(2)}) collective-permute-start(f32[32,32]{1,0:T(8,128)S(1)} %get-tuple-element.72), channel_id=1, source_target_pairs={{0,1},{1,0},{2,3},{3,2},{4,5},{5,4},{6,7},{7,6},{8,9},{9,8},{10,11... | collective-permute-start | bytes 12296 | tf_op jit(solution)/shard_map/ppermute | solution.py:534
  47.5 7.6 %collective-permute-start.5 = (f32[32,32]{1,0:T(8,128)S(1)}, f32[32,32]{1,0:T(8,128)S(1)}, u32[]{:S(2)}, u32[]{:S(2)}) collective-permute-start(f32[32,32]{1,0:T(8,128)S(1)} %get-tuple-element.79), channel_id=1, source_target_pairs={{0,8},{8,0},{16,24},{24,16},{32,40},{40,32},{48,56},{56,48},{64,72... | collective-permute-start | bytes 12296 | tf_op jit(solution)/shard_map/ppermute | solution.py:538
  49.5 5.6 %collective-permute-start.6 = (f32[32,32]{1,0:T(8,128)S(1)}, f32[32,32]{1,0:T(8,128)S(1)}, u32[]{:S(2)}, u32[]{:S(2)}) collective-permute-start(f32[32,32]{1,0:T(8,128)S(1)} %get-tuple-element.80), channel_id=1, source_target_pairs={{0,248},{8,16},{16,8},{24,32},{32,24},{40,48},{48,40},{56,64},{64,... | collective-permute-start | bytes 12296 | tf_op jit(solution)/shard_map/ppermute | solution.py:537
  50.2 4.9 %collective-permute-start.7 = (f32[32,32]{1,0:T(8,128)S(1)}, f32[32,32]{1,0:T(8,128)S(1)}, u32[]{:S(2)}, u32[]{:S(2)}) collective-permute-start(f32[32,32]{1,0:T(8,128)S(1)} %get-tuple-element.81), channel_id=1, source_target_pairs={{0,2},{2,0},{4,6},{6,4},{1,3},{3,1},{5,7},{7,5},{8,10},{10,8},{12,... | collective-permute-start | bytes 12296 | tf_op jit(solution)/shard_map/ppermute | solution.py:536
  54.0 4.2 %collective-permute-start.9 = (f32[32,32]{1,0:T(8,128)S(1)}, f32[32,32]{1,0:T(8,128)S(1)}, u32[]{:S(2)}, u32[]{:S(2)}) collective-permute-start(f32[32,32]{1,0:T(8,128)S(1)} %get-tuple-element.83), channel_id=1, source_target_pairs={{0,1},{1,0},{2,3},{3,2},{4,5},{5,4},{6,7},{7,6},{8,9},{9,8},{10,11... | collective-permute-start | bytes 12296 | tf_op jit(solution)/shard_map/ppermute | solution.py:534
  87.9 3.5 %collective-permute-start.10 = (f32[32,32]{1,0:T(8,128)S(1)}, f32[32,32]{1,0:T(8,128)S(1)}, u32[]{:S(2)}, u32[]{:S(2)}) collective-permute-start(f32[32,32]{1,0:T(8,128)S(1)} %get-tuple-element.90), channel_id=1, source_target_pairs={{0,8},{8,0},{16,24},{24,16},{32,40},{40,32},{48,56},{56,48},{64,72... | collective-permute-start | bytes 12296 | tf_op jit(solution)/shard_map/ppermute | solution.py:538
  88.6 3.2 %collective-permute-start.11 = (f32[32,32]{1,0:T(8,128)S(1)}, f32[32,32]{1,0:T(8,128)S(1)}, u32[]{:S(2)}, u32[]{:S(2)}) collective-permute-start(f32[32,32]{1,0:T(8,128)S(1)} %get-tuple-element.91), channel_id=1, source_target_pairs={{0,248},{8,16},{16,8},{24,32},{32,24},{40,48},{48,40},{56,64},{64,... | collective-permute-start | bytes 12296 | tf_op jit(solution)/shard_map/ppermute | solution.py:537
  89.0 2.7 %collective-permute-start.12 = (f32[32,32]{1,0:T(8,128)S(1)}, f32[32,32]{1,0:T(8,128)S(1)}, u32[]{:S(2)}, u32[]{:S(2)}) collective-permute-start(f32[32,32]{1,0:T(8,128)S(1)} %get-tuple-element.92), channel_id=1, source_target_pairs={{0,2},{2,0},{4,6},{6,4},{1,3},{3,1},{5,7},{7,5},{8,10},{10,8},{12,... | collective-permute-start | bytes 12296 | tf_op jit(solution)/shard_map/ppermute | solution.py:536
  89.3 2.4 %collective-permute-start.13 = (f32[32,32]{1,0:T(8,128)S(1)}, f32[32,32]{1,0:T(8,128)S(1)}, u32[]{:S(2)}, u32[]{:S(2)}) collective-permute-start(f32[32,32]{1,0:T(8,128)S(1)} %get-tuple-element.93), channel_id=1, source_target_pairs={{2,4},{4,2},{3,5},{5,3},{10,12},{12,10},{11,13},{13,11},{18,20},{2... | collective-permute-start | bytes 12296 | tf_op jit(solution)/shard_map/ppermute | solution.py:535
  90.0 4.2 %collective-permute-start.14 = (f32[32,32]{1,0:T(8,128)S(1)}, f32[32,32]{1,0:T(8,128)S(1)}, u32[]{:S(2)}, u32[]{:S(2)}) collective-permute-start(f32[32,32]{1,0:T(8,128)S(1)} %get-tuple-element.94), channel_id=1, source_target_pairs={{0,1},{1,0},{2,3},{3,2},{4,5},{5,4},{6,7},{7,6},{8,9},{9,8},{10,11... | collective-permute-start | bytes 12296 | tf_op jit(solution)/shard_map/ppermute | solution.py:534
  97.0 7.6 %collective-permute-start.15 = (f32[32,32]{1,0:T(8,128)S(1)}, f32[32,32]{1,0:T(8,128)S(1)}, u32[]{:S(2)}, u32[]{:S(2)}) collective-permute-start(f32[32,32]{1,0:T(8,128)S(1)} %get-tuple-element.97), channel_id=1, source_target_pairs={{0,8},{8,0},{16,24},{24,16},{32,40},{40,32},{48,56},{56,48},{64,72... | collective-permute-start | bytes 12296 | tf_op jit(solution)/shard_map/ppermute | solution.py:538
  98.8 5.8 %collective-permute-start.16 = (f32[32,32]{1,0:T(8,128)S(1)}, f32[32,32]{1,0:T(8,128)S(1)}, u32[]{:S(2)}, u32[]{:S(2)}) collective-permute-start(f32[32,32]{1,0:T(8,128)S(1)} %get-tuple-element.98), channel_id=1, source_target_pairs={{0,248},{8,16},{16,8},{24,32},{32,24},{40,48},{48,40},{56,64},{64,... | collective-permute-start | bytes 12296 | tf_op jit(solution)/shard_map/ppermute | solution.py:537
  99.8 4.8 %collective-permute-start.17 = (f32[32,32]{1,0:T(8,128)S(1)}, f32[32,32]{1,0:T(8,128)S(1)}, u32[]{:S(2)}, u32[]{:S(2)}) collective-permute-start(f32[32,32]{1,0:T(8,128)S(1)} %get-tuple-element.99), channel_id=1, source_target_pairs={{0,2},{2,0},{4,6},{6,4},{1,3},{3,1},{5,7},{7,5},{8,10},{10,8},{12,... | collective-permute-start | bytes 12296 | tf_op jit(solution)/shard_map/ppermute | solution.py:536
  103.6 4.2 %collective-permute-start.19 = (f32[32,32]{1,0:T(8,128)S(1)}, f32[32,32]{1,0:T(8,128)S(1)}, u32[]{:S(2)}, u32[]{:S(2)}) collective-permute-start(f32[32,32]{1,0:T(8,128)S(1)} %get-tuple-element.101), channel_id=1, source_target_pairs={{0,1},{1,0},{2,3},{3,2},{4,5},{5,4},{6,7},{7,6},{8,9},{9,8},{10,11... | collective-permute-start | bytes 12296 | tf_op jit(solution)/shard_map/ppermute | solution.py:534
  109.4 4.4 %collective-permute-start.22 = (f32[1,256]{1,0:T(1,128)S(1)}, f32[1,256]{1,0:T(1,128)S(1)}, u32[]{:S(2)}, u32[]{:S(2)}) collective-permute-start(f32[1,256]{1,0:T(1,128)S(1)} %get-tuple-element.103.refs_1_), channel_id=1, source_target_pairs={{0,2},{2,0},{4,6},{6,4},{1,3},{3,1},{5,7},{7,5},{8,10},{10,8},{12,... | collective-permute-start | bytes 3080 | tf_op jit(solution)/shard_map/ppermute | solution.py:600
  111.9 3.6 %collective-permute-start.21 = (f32[1,256]{1,0:T(1,128)S(1)}, f32[1,256]{1,0:T(1,128)S(1)}, u32[]{:S(2)}, u32[]{:S(2)}) collective-permute-start(f32[1,256]{1,0:T(1,128)S(1)} %get-tuple-element.103.refs_1_), channel_id=1, source_target_pairs={{0,6},{2,4},{4,2},{6,0},{1,7},{3,5},{5,3},{7,1},{8,14},{10,12},{12... | collective-permute-start | bytes 3080 | tf_op jit(solution)/shard_map/ppermute | solution.py:600
  112.8 3.9 %collective-permute-start.20 = (f32[1,256]{1,0:T(1,128)S(1)}, f32[1,256]{1,0:T(1,128)S(1)}, u32[]{:S(2)}, u32[]{:S(2)}) collective-permute-start(f32[1,256]{1,0:T(1,128)S(1)} %get-tuple-element.103.refs_1_), channel_id=1, source_target_pairs={{0,4},{2,6},{4,0},{6,2},{1,5},{3,7},{5,1},{7,3},{8,12},{10,14},{12... | collective-permute-start | bytes 3080 | tf_op jit(solution)/shard_map/ppermute | solution.py:600
  118.5 6.7 %collective-permute-start.23 = (f32[32,32]{1,0:T(8,128)S(1)}, f32[32,32]{1,0:T(8,128)S(1)}, u32[]{:S(2)}, u32[]{:S(2)}) collective-permute-start(f32[32,32]{1,0:T(8,128)S(1)} %get-tuple-element.106), channel_id=1, source_target_pairs={{0,8},{8,0},{16,24},{24,16},{32,40},{40,32},{48,56},{56,48},{64,72... | collective-permute-start | bytes 12296 | tf_op jit(solution)/shard_map/ppermute | solution.py:538
  122.2 3.2 %collective-permute-start.24 = (f32[32,32]{1,0:T(8,128)S(1)}, f32[32,32]{1,0:T(8,128)S(1)}, u32[]{:S(2)}, u32[]{:S(2)}) collective-permute-start(f32[32,32]{1,0:T(8,128)S(1)} %get-tuple-element.107), channel_id=1, source_target_pairs={{0,248},{8,16},{16,8},{24,32},{32,24},{40,48},{48,40},{56,64},{64,... | collective-permute-start | bytes 12296 | tf_op jit(solution)/shard_map/ppermute | solution.py:537
  123.1 3.0 %collective-permute-start.25 = (f32[32,32]{1,0:T(8,128)S(1)}, f32[32,32]{1,0:T(8,128)S(1)}, u32[]{:S(2)}, u32[]{:S(2)}) collective-permute-start(f32[32,32]{1,0:T(8,128)S(1)} %get-tuple-element.108), channel_id=1, source_target_pairs={{0,2},{2,0},{4,6},{6,4},{1,3},{3,1},{5,7},{7,5},{8,10},{10,8},{12,... | collective-permute-start | bytes 12296 | tf_op jit(solution)/shard_map/ppermute | solution.py:536
  123.1 3.0 %collective-permute-start.26 = (f32[32,32]{1,0:T(8,128)S(1)}, f32[32,32]{1,0:T(8,128)S(1)}, u32[]{:S(2)}, u32[]{:S(2)}) collective-permute-start(f32[32,32]{1,0:T(8,128)S(1)} %get-tuple-element.109), channel_id=1, source_target_pairs={{2,4},{4,2},{3,5},{5,3},{10,12},{12,10},{11,13},{13,11},{18,20},{2... | collective-permute-start | bytes 12296 | tf_op jit(solution)/shard_map/ppermute | solution.py:535
  123.8 4.8 %collective-permute-start.27 = (f32[32,32]{1,0:T(8,128)S(1)}, f32[32,32]{1,0:T(8,128)S(1)}, u32[]{:S(2)}, u32[]{:S(2)}) collective-permute-start(f32[32,32]{1,0:T(8,128)S(1)} %get-tuple-element.110), channel_id=1, source_target_pairs={{0,1},{1,0},{2,3},{3,2},{4,5},{5,4},{6,7},{7,6},{8,9},{9,8},{10,11... | collective-permute-start | bytes 12296 | tf_op jit(solution)/shard_map/ppermute | solution.py:534
  131.5 8.1 %collective-permute-start.28 = (f32[32,32]{1,0:T(8,128)S(1)}, f32[32,32]{1,0:T(8,128)S(1)}, u32[]{:S(2)}, u32[]{:S(2)}) collective-permute-start(f32[32,32]{1,0:T(8,128)S(1)} %get-tuple-element.113), channel_id=1, source_target_pairs={{0,8},{8,0},{16,24},{24,16},{32,40},{40,32},{48,56},{56,48},{64,72... | collective-permute-start | bytes 12296 | tf_op jit(solution)/shard_map/ppermute | solution.py:538
  132.0 7.6 %collective-permute-start.29 = (f32[32,32]{1,0:T(8,128)S(1)}, f32[32,32]{1,0:T(8,128)S(1)}, u32[]{:S(2)}, u32[]{:S(2)}) collective-permute-start(f32[32,32]{1,0:T(8,128)S(1)} %get-tuple-element.114), channel_id=1, source_target_pairs={{0,248},{8,16},{16,8},{24,32},{32,24},{40,48},{48,40},{56,64},{64,... | collective-permute-start | bytes 12296 | tf_op jit(solution)/shard_map/ppermute | solution.py:537
  133.1 6.5 %collective-permute-start.30 = (f32[32,32]{1,0:T(8,128)S(1)}, f32[32,32]{1,0:T(8,128)S(1)}, u32[]{:S(2)}, u32[]{:S(2)}) collective-permute-start(f32[32,32]{1,0:T(8,128)S(1)} %get-tuple-element.115), channel_id=1, source_target_pairs={{0,2},{2,0},{4,6},{6,4},{1,3},{3,1},{5,7},{7,5},{8,10},{10,8},{12,... | collective-permute-start | bytes 12296 | tf_op jit(solution)/shard_map/ppermute | solution.py:536
  137.5 2.1 %collective-permute-start.31 = (f32[32,32]{1,0:T(8,128)S(1)}, f32[32,32]{1,0:T(8,128)S(1)}, u32[]{:S(2)}, u32[]{:S(2)}) collective-permute-start(f32[32,32]{1,0:T(8,128)S(1)} %get-tuple-element.116), channel_id=1, source_target_pairs={{2,4},{4,2},{3,5},{5,3},{10,12},{12,10},{11,13},{13,11},{18,20},{2... | collective-permute-start | bytes 12296 | tf_op jit(solution)/shard_map/ppermute | solution.py:535
  138.1 4.2 %collective-permute-start.32 = (f32[32,32]{1,0:T(8,128)S(1)}, f32[32,32]{1,0:T(8,128)S(1)}, u32[]{:S(2)}, u32[]{:S(2)}) collective-permute-start(f32[32,32]{1,0:T(8,128)S(1)} %get-tuple-element.117), channel_id=1, source_target_pairs={{0,1},{1,0},{2,3},{3,2},{4,5},{5,4},{6,7},{7,6},{8,9},{9,8},{10,11... | collective-permute-start | bytes 12296 | tf_op jit(solution)/shard_map/ppermute | solution.py:534
  (24 other events, 184.2 us)
where the time goes:
time: 170 us; the launch traced here: 169 us
  starting transfers between devices  57 us (34%)
  blocking collectives  49.6 us (29%)
  waiting for transfers between devices  33.7 us (20%)
  Pallas kernels  22.7 us (13%)
  local copies, waits for them, and re-layouts  5.08 us (3%)
    all_to_all x2, blocking collectives, body(): table = lax.all_to_all(table, AXES, 0, 0, tiled=True)  49.6 us
    pallas_call x12, Pallas kernels, call(): pl.pallas_call(kernel, name=name, out_shape=[jax.ShapeDtypeStruct(shape,...  22.7 us
    all_to_all x1, starting transfers between devices, body(): table = lax.all_to_all(table, AXES, 0, 0, tiled=True)  15.7 us
    all_to_all x1, waiting for transfers between devices, body(): table = lax.all_to_all(table, AXES, 0, 0, tiled=True)  15.1 us
    ppermute x6, waiting for transfers between devices, exchange(): got[4] = lax.ppermute(sends[4], 'radial', rad)  14.4 us
    ppermute x6, starting transfers between devices, exchange(): got[2] = lax.ppermute(sends[2], 'span', span_a)  11 us
    ppermute x6, starting transfers between devices, exchange(): got[0] = lax.ppermute(sends[0], 'passage', pass_a)  9.35 us
    ppermute x6, starting transfers between devices, exchange(): got[4] = lax.ppermute(sends[4], 'radial', rad)  7.91 us
  transfers between devices with their start and end apart: 34, of which 12 were waited for; matrix products, arithmetic and copies ran while one was open for 0% of the time, Pallas kernels for 1%

commit v1 on v0

v1 whole, which is shorter than its diff:
```python
import math

import jax
import jax.numpy as jnp
import numpy as np
from jax import lax
from jax.experimental import pallas as pl
from jax.experimental.pallas import tpu as pltpu
from jax.sharding import PartitionSpec as P

QN = 4
VARS = 5
CG = 4
ELEMS = 4
NODES = QN**3
ROWS = 320
KC = 160
STRIDE = 8
RW = ELEMS * STRIDE
FACE = QN * QN
SOURCES = ((0, 1), (2, 3, 5, 6), (4, 7, 8))
WIDE = 256
AXES = ("passage", "span", "radial")
NEIGH, ORIENT, TAGS, GROUP, PLACE = 0, 6, 12, 18, 19
HIGHEST = lax.Precision.HIGHEST
F32 = jnp.float32


def lobatto_nodes():
    inner_node = 1.0 / math.sqrt(5.0)
    return np.array([-1.0, -inner_node, inner_node, 1.0])


def derivative_table():
    nodes = lobatto_nodes()
    weights = np.ones(QN)
    for row_id in range(QN):
        for col_id in range(QN):
            if col_id != row_id:
                weights[row_id] = weights[row_id] / (nodes[row_id] - nodes[col_id])
    result = np.zeros((QN, QN))
    for row_id in range(QN):
        for col_id in range(QN):
            if col_id != row_id:
                result[row_id, col_id] = (
                    weights[col_id] / weights[row_id] / (nodes[row_id] - nodes[col_id])
                )
        result[row_id, row_id] = -np.sum(result[row_id])
    return result


def vertex_table():
    nodes = lobatto_nodes()
    shapes = np.stack([(1.0 - nodes) / 2.0, (1.0 + nodes) / 2.0])
    first_part = shapes[:, None, None, :, None, None]
    second_part = shapes[None, :, None, None, :, None]
    third_part = shapes[None, None, :, None, None, :]
    return (first_part * second_part * third_part).reshape(8, NODES)


def coords(node):
    return (node // 16, node // 4 % 4, node % 4)


def others(node, axis):
    picked = [c for i, c in enumerate(coords(node)) if i != axis]
    return picked[0] * QN + picked[1]


def layer_of(face):
    return 0 if face % 2 == 0 else QN - 1


def stacked(values):
    high = values.astype(jnp.bfloat16)
    low = (values - high.astype(np.float32)).astype(jnp.bfloat16)
    return np.concatenate([high, high, low], axis=0)


def tables():
    dmat = derivative_table()
    de = np.zeros((NODES, 3 * NODES + 6 * 2 * FACE), np.float32)
    place = np.zeros((6, 1, FACE, NODES), np.float32)
    for node in range(NODES):
        for axis in range(3):
            for target in range(NODES):
                if others(node, axis) == others(target, axis):
                    de[node, axis * NODES + target] = dmat[
                        coords(target)[axis], coords(node)[axis]
                    ]
        for face in range(6):
            axis = face // 2
            spot = others(node, axis)
            base = 3 * NODES + face * 2 * FACE
            de[node, base + FACE + spot] = dmat[layer_of(face), coords(node)[axis]]
            if coords(node)[axis] == layer_of(face):
                de[node, base + spot] = 1.0
                place[face, :, spot, node] = 1.0
    turn = np.zeros((FACE, 8, FACE), np.float32)
    for code in range(8):
        for i in range(QN):
            for j in range(QN):
                a = QN - 1 - i if code & 2 else i
                b = QN - 1 - j if code & 1 else j
                if code & 4:
                    a, b = b, a
                turn[a * QN + b, code, i * QN + j] = 1.0
    rtab = vertex_table().astype(np.float32)
    restrict = np.zeros((NODES, WIDE), np.float32)
    restrict[:, :KC] = np.tile(rtab.T, (1, CG * VARS))
    lay = np.einsum("aob,fbk->foak", turn, place[:, 0]).reshape(6 * 8 * FACE, NODES)
    own_lanes = np.zeros((RW, ROWS), np.float32)
    for row in range(RW):
        v = row % STRIDE
        if v < VARS:
            own_lanes[row, v * NODES : (v + 1) * NODES] = 1.0
    tile = np.zeros((80, 6 * 256), np.float32)
    colcode = np.full((8, 6 * 256), -100.0, np.float32)
    for face in range(6):
        axis = face // 2
        for place_id, source in enumerate(SOURCES[axis]):
            for col in range(2 * RW):
                kind, n, v = col // RW, col // STRIDE % ELEMS, col % STRIDE
                lane = face * 256 + place_id * 2 * RW + col
                if v < VARS:
                    tile[kind * 40 + v * 8 + face, lane] = 1.0
                colcode[0, lane] = source * ELEMS + n
                colcode[1, lane] = (-1.0 if v == 1 + axis else 1.0) * (-1.0 if kind else 1.0)
    rows = np.zeros((RW, 24), np.float32)
    for e in range(ELEMS):
        for u in range(VARS):
            rows[e * STRIDE + u, u * ELEMS + e] = 1.0
    vtile = np.zeros((24, 3 * RW), np.float32)
    vmask = np.zeros((RW, 3 * RW), np.float32)
    for col in range(3 * RW):
        axis, n, v = col // RW, col // STRIDE % ELEMS, col % STRIDE
        if v < VARS:
            vtile[axis * 8 + v, col] = 1.0
        vmask[n * STRIDE : (n + 1) * STRIDE, col] = 1.0
    return dict(
        de=stacked(de),
        lay=lay.astype(jnp.bfloat16),
        restrict=stacked(restrict),
        spread=stacked(np.ascontiguousarray(restrict.T)),
        own_lanes=own_lanes,
        tile=tile,
        colcode=colcode,
        rows=rows,
        vtile=vtile,
        vmask=vmask,
    )


def exact_dot(a, b):
    return jnp.dot(a, b, precision=HIGHEST, preferred_element_type=F32)


def halves(values):
    high = values.astype(jnp.bfloat16)
    return high, (values - high.astype(F32)).astype(jnp.bfloat16)


def left_stack(values):
    high = values.astype(jnp.bfloat16).astype(F32)
    return jnp.concatenate([high, values - high, high], axis=1).astype(jnp.bfloat16)


def right_stack(values):
    high, low = halves(values)
    return jnp.concatenate([high, low, high], axis=0)


def dot(a, b):
    return jnp.dot(a, b, preferred_element_type=F32)


def total(values):
    return jnp.sum(values, axis=(0, 1), keepdims=True)


def member_mask(ints_ref):
    row = lax.broadcasted_iota(jnp.int32, (STRIDE, WIDE), 0)
    lane = lax.broadcasted_iota(jnp.int32, (STRIDE, WIDE), 1)
    pieces = []
    for e in range(ELEMS):
        hit = (lane // (VARS * 8) == ints_ref[e, GROUP]) & (lane // 8 % VARS == row)
        pieces.append(jnp.where(hit & (lane < KC), 1.0, 0.0))
    return jnp.concatenate(pieces, axis=0)


def coarse_row(member, restrict, vector):
    return jnp.sum(member * dot(left_stack(vector), restrict), axis=0, keepdims=True)


def scalar_row(scalars):
    lane = lax.broadcasted_iota(jnp.int32, (1, 128), 1)
    row = jnp.zeros((1, 128), F32)
    for i, value in enumerate(scalars):
        row = jnp.where(lane == i, value, row)
    return row


def read_scalars(table_ref, count):
    sums = jnp.sum(table_ref[...], axis=0, keepdims=True)
    return [sums[:, i : i + 1] for i in range(count)]


def coarse_values(coarse, cinv_ref, member_ref, spread_ref):
    solved = lax.dot_general(
        left_stack(coarse[:, :KC]),
        cinv_ref[...],
        (((1,), (1,)), ((), ())),
        preferred_element_type=F32,
    )
    solved = jnp.concatenate([solved, jnp.zeros((1, WIDE - KC), F32)], axis=1)
    return dot(left_stack(member_ref[...] * solved), spread_ref[...])


def apply_blocks(turned_ref, own_lanes, parts):
    stacked = []
    for part in parts:
        pair = jnp.concatenate([part, part], axis=1)
        stacked.append(jnp.concatenate([pair, pair, part], axis=1) * own_lanes)
    pieces = []
    for e in range(ELEMS):
        rows = [part[e * STRIDE : (e + 1) * STRIDE] for part in stacked]
        rows = jnp.concatenate(rows, axis=0) if len(rows) > 1 else rows[0]
        out = dot(rows.astype(jnp.bfloat16), turned_ref[e])
        pieces.append(jnp.broadcast_to(jnp.sum(out, axis=0, keepdims=True), (STRIDE, ROWS)))
    full = jnp.concatenate(pieces, axis=0) * own_lanes
    half = full[:, :128] + full[:, 128:256]
    return half[:, :NODES] + half[:, NODES:] + full[:, 256:]


def rounded(values):
    return [values.astype(jnp.bfloat16).astype(F32)]


def two_parts(values):
    high = values.astype(jnp.bfloat16).astype(F32)
    return [high, values - high]


def face_of(grown, face):
    base = 3 * NODES + face * 2 * FACE
    return grown[:, base : base + 2 * FACE]


def pack(grown, face):
    values = face_of(grown, face)
    rows = [values[e * STRIDE : (e + 1) * STRIDE] for e in range(ELEMS)]
    return jnp.concatenate(rows, axis=1)


def copies(tile, slot):
    lane = lax.broadcasted_iota(jnp.int32, tile.shape, 1)
    values = jnp.where(lane // FACE == slot, tile, 0.0)
    for shift in (FACE, 2 * FACE, 4 * FACE):
        values = values + pltpu.roll(values, shift, 1)
    return values


def unpack(tile):
    return [copies(tile, e * 2 + kind) for kind in range(2) for e in range(ELEMS)]


def write_sends(ints_ref, grown, send_refs):
    p_odd, s_odd, r = ints_ref[0, PLACE] % 2, ints_ref[1, PLACE] % 2, ints_ref[2, PLACE]
    faces = [pack(grown, f) for f in range(6)]
    send_refs[0][...] = jnp.where(r == 0, faces[5], faces[4])
    send_refs[1][...] = jnp.where(p_odd == 0, faces[0], faces[1])
    send_refs[2][...] = jnp.where(s_odd == 0, faces[3], faces[2])
    send_refs[3][...] = jnp.where(s_odd == 0, faces[2], faces[3])
    send_refs[4][...] = jnp.where(p_odd == 0, faces[1], faces[0])


def place_terms(groups, omask_ref, lay_ref, first_face):
    laid = []
    for i, terms in enumerate(groups):
        base = (first_face + 2 * i) * RW
        terms = terms * omask_ref[base : base + 2 * RW, :]
        laid += [terms[:RW], terms[RW:]]
    laid = jnp.concatenate(laid, axis=1)
    high, low = halves(laid)
    out = dot(jnp.concatenate([high, low], axis=0), lay_ref[first_face * 8 * FACE :, :])
    return out[:RW] + out[RW:]


def halo_part(recv, rem, omask_ref, lay_ref):
    rad, pass_b, span_a, span_b, pass_a = [unpack(r[...]) for r in recv]
    groups = []
    for pieces, mat in ((pass_a + pass_b, rem[0]), (span_a + span_b, rem[1]), (rad, rem[2])):
        groups.append(dot(mat[...], right_stack(jnp.concatenate(pieces, axis=0))))
    return place_terms(groups, omask_ref, lay_ref, 0)


def start_kernel(rs_ref, table_ref):
    rs = rs_ref[...]
    table_ref[...] = jnp.broadcast_to(scalar_row([total(rs * rs)]), table_ref.shape)


def prepare_kernel(rs_ref, mass_ref, ints_ref, restrict_ref, x_ref, massw_ref, member_ref, row_ref):
    x_ref[...] = jnp.zeros_like(x_ref)
    massw_ref[...] = jnp.zeros_like(massw_ref)
    for e in range(ELEMS):
        for v in range(VARS):
            lanes = slice(v * NODES, (v + 1) * NODES)
            row = e * STRIDE + v
            x_ref[row : row + 1, :] = rs_ref[e : e + 1, lanes]
            massw_ref[row : row + 1, :] = mass_ref[e : e + 1, lanes]
    member = member_mask(ints_ref)
    member_ref[...] = member
    row_ref[...] = coarse_row(member, restrict_ref[...], x_ref[...])


def setup_kernel(
    ints_ref,
    volume_ref,
    flux_ref,
    visc_ref,
    blocks_ref,
    rows_ref,
    tile_ref,
    colcode_ref,
    vtile_ref,
    vmask_ref,
    cinv_ref,
    rem0_ref,
    rem1_ref,
    rem2_ref,
    loc1_ref,
    loc2_ref,
    omask_ref,
    vmat_ref,
    cinv3_ref,
    turned_ref,
    coef_ref,
    amat_ref,
):
    p_odd, s_odd = ints_ref[0, PLACE] % 2, ints_ref[1, PLACE] % 2
    device = ints_ref[3, PLACE]
    coef_ref[...] = jnp.zeros_like(coef_ref)
    for u in range(VARS):
        here = slice(u * ELEMS, (u + 1) * ELEMS)
        for axis in range(3):
            coef_ref[here, 80 + axis * 8 : 80 + axis * 8 + VARS] = volume_ref[axis, u]
        for v in range(VARS):
            coef_ref[here, v * 8 : v * 8 + 6] = flux_ref[u, v]
            coef_ref[here, 40 + v * 8 : 40 + v * 8 + 6] = visc_ref[u, v]
    coef = exact_dot(rows_ref[...], coef_ref[...])
    vmat_ref[...] = right_factor(exact_dot(coef[:, 80:104], vtile_ref[...]) * vmask_ref[...])
    cinv3_ref[...] = right_factor(cinv_ref[0, 0])
    for e in range(ELEMS):
        turned_ref[e] = blocks_ref[e].T
    spread = exact_dot(coef[:, :80], tile_ref[...])
    lane = lax.broadcasted_iota(jnp.int32, (STRIDE, 8 * FACE), 1)
    for f in range(6):
        cols = slice(f * 256, (f + 1) * 256)
        colcode = jnp.broadcast_to(colcode_ref[0:1, cols], (STRIDE, 256))
        signs = jnp.broadcast_to(colcode_ref[1:2, cols], (STRIDE, 256))
        for e in range(ELEMS):
            near = ints_ref[e, NEIGH + f]
            tag = ints_ref[e, TAGS + f]
            spot = near % ELEMS
            crossing = near // ELEMS != device
            if f == 0:
                source = 1 - p_odd
            elif f == 1:
                source = p_odd
            elif f == 2:
                source = 3 - s_odd
            elif f == 3:
                source = 2 + s_odd
            else:
                source = jnp.where(crossing, 4, 8 if f == 4 else 7)
            code = source * ELEMS + spot
            turn_code = ints_ref[e, ORIENT + f]
            if f >= 2:
                wall_code = (5 + f - 2) * ELEMS + e
                code = jnp.where(tag == 0, code, jnp.where(tag == 1, wall_code, -1))
                turn_code = jnp.where(tag == 0, turn_code, 0)
            rows = slice(f * RW + e * STRIDE, f * RW + (e + 1) * STRIDE)
            values = spread[e * STRIDE : (e + 1) * STRIDE, cols]
            values = jnp.where(tag == 1, values * signs, values)
            amat_ref[rows, :] = jnp.where(colcode == code.astype(F32), -values, 0.0)
            omask_ref[rows, :] = jnp.where(lane // FACE == turn_code, 1.0, 0.0)
    one = 2 * RW
    rem0_ref[...] = right_factor(amat_ref[:one, : 2 * one])
    rem1_ref[...] = right_factor(amat_ref[one : 2 * one, : 2 * one])
    loc1_ref[...] = right_factor(amat_ref[one : 2 * one, 2 * one : 4 * one])
    rem2_ref[...] = right_factor(amat_ref[2 * one :, :one])
    loc2_ref[...] = right_factor(amat_ref[2 * one :, one : 3 * one])


def right_factor(values):
    high = values.astype(jnp.bfloat16).astype(F32)
    return jnp.concatenate([high, high, values - high], axis=1).astype(jnp.bfloat16)


def coarse_kernel(r0, r1, r2, r3, cinv, member, spread, coarse_ref):
    coarse = (r0[...] + r1[...]) + (r2[...] + r3[...])
    coarse_ref[...] = coarse_values(coarse, cinv, member, spread)


def blocks_kernel(x, blocks, own, out_ref):
    out_ref[...] = apply_blocks(blocks, own[...], two_parts(x[...]))


def finish_first(ints, first, de, first_ref, grown_ref, sends):
    first_ref[...] = first
    grown = dot(left_stack(first), de[...])
    grown_ref[...] = grown
    write_sends(ints, grown, sends)


def first0_kernel(ints, table, x, coarse, blocks, own, de, *outs):
    z_ref, coarse_ref, scal_ref, first_ref, grown_ref, *sends = outs
    beta = jnp.sqrt(read_scalars(table, 1)[0])
    z = x[...] / beta
    z_ref[...] = z
    scal_ref[...] = jnp.broadcast_to(beta, scal_ref.shape)
    scaled = coarse[...] / beta
    coarse_ref[...] = scaled
    first = apply_blocks(blocks, own[...], rounded(z)) + scaled
    finish_first(ints, first, de, first_ref, grown_ref, sends)


def first1_kernel(ints, table, x, coarse, b0, coarse0, blocks, own, de, *outs):
    z_ref, scal_ref, first_ref, grown_ref, *sends = outs
    h00, square = read_scalars(table, 2)
    h10 = jnp.sqrt(jnp.maximum(square - h00 * h00, 1e-7 * square))
    z = (x[...] - h00 * b0[...]) / h10
    z_ref[...] = z
    row = lax.broadcasted_iota(jnp.int32, scal_ref.shape, 0)
    scal_ref[...] = jnp.where(row == 0, h00, jnp.where(row == 1, h10, square))
    scaled = (coarse[...] - h00 * coarse0[...]) / h10
    first = apply_blocks(blocks, own[...], rounded(z)) + scaled
    finish_first(ints, first, de, first_ref, grown_ref, sends)


def first2_kernel(ints, r0, r1, r2, r3, fine, cinv, member, spread, de, *outs):
    first_ref, grown_ref, *sends = outs
    coarse = (r0[...] + r1[...]) + (r2[...] + r3[...])
    first = fine[...] + coarse_values(coarse, cinv, member, spread)
    finish_first(ints, first, de, first_ref, grown_ref, sends)


def local_kernel(x, grown_ref, mass, vmat, loc1, loc2, omask, lay, out_ref):
    grown = grown_ref[...]
    slopes = jnp.concatenate([grown[:, i * NODES : (i + 1) * NODES] for i in range(3)], axis=0)
    result = 1.5 * mass[...] * x[...] + dot(vmat[...], right_stack(slopes))
    groups = []
    for faces, mat in (((2, 3), loc1), ((4, 5), loc2)):
        pieces = []
        for f in faces:
            base = 3 * NODES + f * 2 * FACE
            tile = grown[:, base // 128 * 128 : base // 128 * 128 + 128]
            slot = base % 128 // FACE
            pieces += [copies(tile, slot), copies(tile, slot + 1)]
        groups.append(dot(mat[...], right_stack(jnp.concatenate(pieces, axis=0))))
    out_ref[...] = result + place_terms(groups, omask, lay, 2)


def second_kernel(step, *refs):
    ints, z, first, local = refs[:4]
    recv = refs[4:9]
    rem, omask, lay, blocks, own, de = refs[9:12], *refs[12:17]
    search_ref, grown_ref, *sends = refs[17:]
    defect = z[...] - (local[...] + halo_part(recv, rem, omask, lay))
    parts = two_parts(defect) if step == 2 else rounded(defect)
    search = first[...] + apply_blocks(blocks, own[...], parts)
    search_ref[...] = search
    grown = dot(left_stack(search), de[...])
    grown_ref[...] = grown
    write_sends(ints, grown, sends)


def third_kernel(step, *refs):
    local = refs[0]
    recv = refs[1:6]
    rem, omask, lay = refs[6:9], refs[9], refs[10]
    mapped = local[...] + halo_part(recv, rem, omask, lay)
    if step == 0:
        member, restrict, b0, w_ref, table_ref, row_ref = refs[11:]
        scalars = [total(mapped * b0[...]), total(mapped * mapped)]
    elif step == 1:
        member, restrict, w_ref, row_ref = refs[11:]
    else:
        b0, b1, w1, w_ref, table_ref = refs[11:]
        scalars = [total(w1[...] * b[...]) for b in (b0, b1, w1)]
        scalars += [total(mapped * b[...]) for b in (b0, b1, w1)]
        scalars += [total(mapped * mapped)]
    w_ref[...] = mapped
    if step != 1:
        table_ref[...] = jnp.broadcast_to(scalar_row(scalars), table_ref.shape)
    if step != 2:
        row_ref[...] = coarse_row(member[...], restrict[...], mapped)


def inverse_sqrt(value):
    guess = lax.rsqrt(value)
    return guess * (1.5 - 0.5 * (value * guess) * guess)


def least_squares(matrix, beta):
    iters = len(matrix) - 1
    target = [beta] + [jnp.zeros_like(beta)] * iters
    inverse = []
    for k in range(iters):
        top, low = matrix[k][k], matrix[k + 1][k]
        scale = inverse_sqrt(top * top + low * low)
        inverse.append(scale)
        cosine, sine = top * scale, low * scale
        for later in range(k + 1, iters):
            upper, lower = matrix[k][later], matrix[k + 1][later]
            matrix[k][later] = cosine * upper + sine * lower
            matrix[k + 1][later] = -sine * upper + cosine * lower
        upper, lower = target[k], target[k + 1]
        target[k] = cosine * upper + sine * lower
        target[k + 1] = -sine * upper + cosine * lower
    weights = [None] * iters
    for k in reversed(range(iters)):
        value = target[k]
        for later in range(k + 1, iters):
            value = value - matrix[k][later] * weights[later]
        weights[k] = value * inverse[k]
    return weights


def final_kernel(table, scal0, scal1, x, s0, s1, s2, w0, w1, w2, update_ref, residual_ref):
    sums = jnp.sum(table[...], axis=0, keepdims=True)
    g0, g1, g2, q0, q1, qw, qq = [sums[:, i : i + 1] for i in range(7)]
    beta = scal0[0:1, 0:1]
    h00, h10, square0 = [scal1[i : i + 1, 0:1] for i in range(3)]
    h01, h11 = g0, g1
    squared = jnp.maximum(g2 - h01 * h01 - h11 * h11, 1e-7 * g2)
    inv21 = inverse_sqrt(squared)
    h21 = squared * inv21
    cross = h00 * h01 + h10 * h11
    h02 = (q0 - h01 * h00 - h11 * h01) * inv21
    h12 = (q1 - h01 * h10 - h11 * h11) * inv21
    with_w1 = (qw - h01 * cross - h11 * g2) * inv21
    h22 = (with_w1 - h01 * h02 - h11 * h12) * inv21
    with_w0 = h00 * q0 + h10 * q1
    square = qq + h01 * h01 * square0 + h11 * h11 * g2
    square = square - 2.0 * (h01 * with_w0 + h11 * qw - h01 * h11 * cross)
    square = square * inv21 * inv21
    h32 = jnp.sqrt(jnp.maximum(square - h02 * h02 - h12 * h12 - h22 * h22, 1e-7 * square))
    zero = jnp.zeros_like(beta)
    hess = [[h00, h01, h02], [h10, h11, h12], [zero, h21, h22], [zero, zero, h32]]
    y0, y1, y2 = least_squares(hess, beta)
    y2 = y2 * inv21
    y0 = y0 - y2 * h01
    y1 = y1 - y2 * h11
    update = y0 * s0[...] + y1 * s1[...] + y2 * s2[...]
    residual = x[...] - (y0 * w0[...] + y1 * w1[...] + y2 * w2[...])
    for e in range(ELEMS):
        for v in range(VARS):
            lanes = slice(v * NODES, (v + 1) * NODES)
            row = e * STRIDE + v
            update_ref[e : e + 1, lanes] = update[row : row + 1, :]
            residual_ref[e : e + 1, lanes] = residual[row : row + 1, :]


VMEM = pltpu.VMEM
SMEM = pltpu.SMEM


def shape_of(out):
    return out if isinstance(out, jax.ShapeDtypeStruct) else jax.ShapeDtypeStruct(out, F32)


def call(kernel, name, args, outs, smem=(), scratch=(), raw=()):
    return pl.pallas_call(
        kernel,
        name=name,
        out_shape=[shape_of(out) for out in outs],
        in_specs=[
            pl.BlockSpec()
            if i in raw
            else pl.BlockSpec(memory_space=SMEM if i in smem else VMEM)
            for i in range(len(args))
        ],
        out_specs=[pl.BlockSpec(memory_space=VMEM)] * len(outs),
        scratch_shapes=[VMEM(shape, F32) for shape in scratch],
        compiler_params=pltpu.CompilerParams(vmem_limit_bytes=32 * 1024 * 1024),
    )(*args)


def with_step(kernel, step):
    def run(*refs):
        kernel(step, *refs)

    return run


def body(
    right_side,
    mass,
    volume_jac,
    face_flux,
    face_visc,
    block_inverse,
    coarse_inverse,
    neighbours,
    orientation,
    bc_tags,
    coarse_group,
):
    t = {name: jnp.asarray(value) for name, value in tables().items()}
    n_pass, n_span = lax.axis_size("passage"), lax.axis_size("span")
    n_rad = lax.axis_size("radial")
    devices = n_pass * n_span * n_rad
    p, s, r = (lax.axis_index(a) for a in AXES)
    place = jnp.stack([p, s, r, (p * n_span + s) * n_rad + r]).astype(jnp.int32)
    ints = [neighbours, orientation, bc_tags, coarse_group[:, None], place[:, None]]
    ints = jnp.concatenate(ints, axis=1)
    volume_t = jnp.transpose(volume_jac, (1, 2, 0, 3))
    flux_t, visc_t = (jnp.transpose(a, (2, 3, 0, 1)) for a in (face_flux, face_visc))

    pass_a = [(i, i ^ 1) for i in range(n_pass)]
    pass_b = [(i, (i + 1 if i % 2 else i - 1) % n_pass) for i in range(n_pass)]
    span_a = [(i, i ^ 1) for i in range(n_span)]
    span_b = [(i, (i + 1 if i % 2 else i - 1) % n_span) for i in range(n_span)]
    rad = [(0, 1), (1, 0)]

    def exchange(sends):
        ways = (
            ("radial", rad),
            ("passage", pass_b),
            ("span", span_a),
            ("span", span_b),
            ("passage", pass_a),
        )
        return [lax.ppermute(x, axis, way) for x, (axis, way) in zip(sends, ways)]

    def span_rows(row):
        return [row] + [
            lax.ppermute(row, "span", [(i, i ^ k) for i in range(n_span)]) for k in (2, 3, 1)
        ]

    vec = (RW, NODES)
    grow = (RW, t["de"].shape[1])
    send = (STRIDE, 128)
    table_shape = (devices, 128)

    def half_floats(*shape):
        return jax.ShapeDtypeStruct(shape, jnp.bfloat16)

    (table,) = call(start_kernel, "start", (right_side,), [table_shape], raw=(0,))
    table = lax.all_to_all(table, AXES, 0, 0, tiled=True)
    x, massw, member, row = call(
        prepare_kernel,
        "prepare",
        (right_side, mass, ints, t["restrict"]),
        [vec, vec, (RW, WIDE), (1, WIDE)],
        smem=(2,),
        raw=(0, 1, 3),
    )
    rows = span_rows(row)
    pair = half_floats(2 * RW, 3 * 4 * RW)
    rem0, rem1, rem2, loc1, loc2, omask, vmat, cinv3, turned = call(
        setup_kernel,
        "setup",
        (
            ints,
            volume_t,
            flux_t,
            visc_t,
            block_inverse,
            t["rows"],
            t["tile"],
            t["colcode"],
            t["vtile"],
            t["vmask"],
            coarse_inverse,
        ),
        [
            pair,
            pair,
            half_floats(2 * RW, 3 * 2 * RW),
            pair,
            pair,
            (6 * RW, 8 * FACE),
            half_floats(RW, 9 * RW),
            half_floats(KC, 3 * KC),
            half_floats(*block_inverse.shape),
        ],
        smem=(0,),
        raw=tuple(range(1, 11)),
        scratch=[(24, 104), (6 * RW, 256)],
    )
    remote = (rem0, rem1, rem2, omask, t["lay"])
    near = (massw, vmat, loc1, loc2, omask, t["lay"])

    def local_part(vector, grown, step):
        return call(local_kernel, "local%d" % step, (vector, grown) + near, [vec])[0]

    coarse_tables = (cinv3, member, t["spread"])
    tail = (turned, t["own_lanes"], t["de"])
    basis, search, images, scalars = [], [], [], []
    coarse0 = None
    outs = [vec, grow] + [send] * 5
    for step in range(3):
        if step < 2:
            (coarse,) = call(coarse_kernel, "coarse%d" % step, (*rows, *coarse_tables), [vec])
        if step == 0:
            z, coarse0, scal, first, grown, *sends = call(
                first0_kernel,
                "first0",
                (ints, table, x, coarse) + tail,
                [vec, vec, (8, 128)] + outs,
                smem=(0,),
            )
            scalars.append(scal)
        elif step == 1:
            z, scal, first, grown, *sends = call(
                first1_kernel,
                "first1",
                (ints, table, images[0], coarse, basis[0], coarse0) + tail,
                [vec, (8, 128)] + outs,
                smem=(0,),
            )
            scalars.append(scal)
        else:
            z = images[1]
            (fine,) = call(blocks_kernel, "fine", (z, turned, t["own_lanes"]), [vec])
            first, grown, *sends = call(
                first2_kernel,
                "first2",
                (ints, *rows, fine, *coarse_tables, t["de"]),
                outs,
                smem=(0,),
            )
        basis.append(z)
        recv = exchange(sends)
        local = local_part(first, grown, step)
        direction, grown, *sends = call(
            with_step(second_kernel, step),
            "second%d" % step,
            (ints, z, first, local, *recv) + remote + tail,
            outs,
            smem=(0,),
        )
        search.append(direction)
        recv = exchange(sends)
        local = local_part(direction, grown, step)
        kernel = with_step(third_kernel, step)
        args = (local, *recv) + remote
        if step == 0:
            image, table, row = call(
                kernel,
                "third0",
                args + (member, t["restrict"], basis[0]),
                [vec, table_shape, (1, WIDE)],
            )
            table = lax.all_to_all(table, AXES, 0, 0, tiled=True)
            rows = span_rows(row)
        elif step == 1:
            image, row = call(kernel, "third1", args + (member, t["restrict"]), [vec, (1, WIDE)])
            rows = span_rows(row)
        else:
            image, table = call(kernel, "third2", args + tuple(basis), [vec, table_shape])
            table = lax.all_to_all(table, AXES, 0, 0, tiled=True)
        images.append(image)

    update, residual = call(
        final_kernel,
        "final",
        (table, *scalars, x, *search, *images),
        [right_side.shape] * 2,
    )
    return (update, residual)


def solution(mesh):
    rows = P(AXES, None)
    blocks = P(AXES, None, None)
    jac = P(AXES, None, None, None)
    in_specs = (
        rows,
        rows,
        jac,
        jac,
        jac,
        blocks,
        P("passage", "radial", None, None),
        rows,
        rows,
        rows,
        P(AXES),
    )
    return jax.shard_map(body, mesh=mesh, in_specs=in_specs, out_specs=(rows, rows), check_vma=False)
```

time: 170 us -> 144 us (0.85)
  blocking collectives: 49.6 us -> 22.7 us
  starting transfers between devices: 57 us -> 77.1 us
  waiting for transfers between devices: 33.7 us -> 18.4 us
  Pallas kernels: 22.7 us -> 20.7 us
    all_to_all x2 -> x1, blocking collectives: 49.6 us -> 22.7 us  [body(): table = lax.all_to_all(table, AXES, 0, 0, tiled=True)]
    all_to_all x1 -> x2, starting transfers between devices: 15.7 us -> 26.6 us  [body(): table = lax.all_to_all(table, AXES, 0, 0, tiled=True)]
    ppermute x33 -> x39, starting transfers between devices: 41.3 us -> 50.5 us  [the longest x30 39.4 us: exchange(): return [lax.ppermute(x, axis, way) for x, (axis, way) in zip(sends, ways)]]
    ppermute x33 -> x39, waiting for transfers between devices: 18.6 us -> 9.82 us  [the longest x9 5.03 us: span_rows(): lax.ppermute(row, 'span', [(i, i ^ k) for i in range(n_span)])]
    all_to_all x1 -> x2, waiting for transfers between devices: 15.1 us -> 8.55 us  [body(): table = lax.all_to_all(table, AXES, 0, 0, tiled=True)]
    pallas_call x12 -> x22, Pallas kernels: 22.7 us -> 20.7 us  [call(): pl.pallas_call(kernel, name=name, out_shape=[shape_of(out) for out in out...]
    unnamed x49 -> x44, local copies, waits for them, and re-layouts: 3.84 us -> 3.46 us
  transfers between devices with their start and end apart: 34 -> 41, of which waited for: 12 -> 14; matrix products, arithmetic and copies ran while one was open for 0% -> 0% of each run, Pallas kernels for 1% -> 5%
where the time goes in v1:
time: 144 us
  starting transfers between devices  77.1 us (54%)
  blocking collectives  22.7 us (16%)
  Pallas kernels  20.7 us (14%)
  waiting for transfers between devices  18.4 us (13%)
  local copies, waits for them, and re-layouts  3.74 us (3%)
    ppermute x30, starting transfers between devices, exchange(): return [lax.ppermute(x, axis, way) for x, (axis, way) in zip(sends, ways)]  39.4 us
    all_to_all x2, starting transfers between devices, body(): table = lax.all_to_all(table, AXES, 0, 0, tiled=True)  26.6 us
    all_to_all x1, blocking collectives, body(): table = lax.all_to_all(table, AXES, 0, 0, tiled=True)  22.7 us
    pallas_call x22, Pallas kernels, call(): pl.pallas_call(kernel, name=name, out_shape=[shape_of(out) for out in out...  20.7 us
    ppermute x9, starting transfers between devices, span_rows(): lax.ppermute(row, 'span', [(i, i ^ k) for i in range(n_span)])  11.2 us
    all_to_all x2, waiting for transfers between devices, body(): table = lax.all_to_all(table, AXES, 0, 0, tiled=True)  8.55 us
    ppermute x9, waiting for transfers between devices, span_rows(): lax.ppermute(row, 'span', [(i, i ^ k) for i in range(n_span)])  5.03 us
    ppermute x30, waiting for transfers between devices, exchange(): return [lax.ppermute(x, axis, way) for x, (axis, way) in zip(sends, ways)]  4.79 us
  transfers between devices with their start and end apart: 41, of which 14 were waited for; matrix products, arithmetic and copies ran while one was open for 0% of the time, Pallas kernels for 5%

profile of v1, /device:TPU:1, one launch (start us, length us, event | category | flops | bytes accessed | tf_op | source)
XLA Modules:
  0.0 143.9 jit_solution(5751914409733330330)
XLA Ops:
  2.1 15.7 %all-to-all-start = ((f32[256,1,128]{2,1,0:T(1,128)}), f32[256,1,128]{2,1,0:T(1,128)S(1)}, u32[]{:S(2)}, u32[]{:S(2)}) async-start(f32[256,1,128]{2,1,0:T(1,128)} %bitcast.7), calls=%async_computation | async-start | bytes 262144 | tf_op jit(solution)/shard_map/all_to_all | solution.py:651
  19.6 1.5 %collective-permute-start.2 = (f32[1,256]{1,0:T(1,128)S(1)}, f32[1,256]{1,0:T(1,128)S(1)}, u32[]{:S(2)}, u32[]{:S(2)}) collective-permute-start(f32[1,256]{1,0:T(1,128)S(1)} %get-tuple-element.70.r0), channel_id=1, source_target_pairs={{0,2},{2,0},{4,6},{6,4},{1,3},{3,1},{5,7},{7,5},{8,10},{10,8},{12,... | collective-permute-start | bytes 3080 | tf_op jit(solution)/shard_map/ppermute | solution.py:639
  21.0 1.8 %collective-permute-start.1 = (f32[1,256]{1,0:T(1,128)S(1)}, f32[1,256]{1,0:T(1,128)S(1)}, u32[]{:S(2)}, u32[]{:S(2)}) collective-permute-start(f32[1,256]{1,0:T(1,128)S(1)} %get-tuple-element.70.r0), channel_id=1, source_target_pairs={{0,6},{2,4},{4,2},{6,0},{1,7},{3,5},{5,3},{7,1},{8,14},{10,12},{12... | collective-permute-start | bytes 3080 | tf_op jit(solution)/shard_map/ppermute | solution.py:639
  25.8 1.4 setup.1
  27.7 3.1 %all-to-all-done = f32[256,1,128]{2,1,0:T(1,128)S(1)} async-done(((f32[256,1,128]{2,1,0:T(1,128)}), f32[256,1,128]{2,1,0:T(1,128)S(1)}, u32[]{:S(2)}, u32[]{:S(2)}) %all-to-all-start) | async-done | bytes 131104 | tf_op jit(solution)/shard_map/all_to_all | solution.py:651
  32.9 2.5 %collective-permute-start.4 = (f32[8,128]{1,0:T(8,128)S(1)}, f32[8,128]{1,0:T(8,128)S(1)}, u32[]{:S(2)}, u32[]{:S(2)}) collective-permute-start(f32[8,128]{1,0:T(8,128)S(1)} %get-tuple-element.83), channel_id=1, source_target_pairs={{0,248},{8,16},{16,8},{24,32},{32,24},{40,48},{48,40},{56,64},{64,... | collective-permute-start | bytes 12296 | tf_op jit(solution)/shard_map/ppermute | solution.py:635
  35.8 1.9 %collective-permute-start.6 = (f32[8,128]{1,0:T(8,128)S(1)}, f32[8,128]{1,0:T(8,128)S(1)}, u32[]{:S(2)}, u32[]{:S(2)}) collective-permute-start(f32[8,128]{1,0:T(8,128)S(1)} %get-tuple-element.85), channel_id=1, source_target_pairs={{0,6},{2,4},{4,2},{6,0},{1,7},{3,5},{5,3},{7,1},{8,14},{10,12},{12... | collective-permute-start | bytes 12296 | tf_op jit(solution)/shard_map/ppermute | solution.py:635
  37.7 2.4 %collective-permute-start.7 = (f32[8,128]{1,0:T(8,128)S(1)}, f32[8,128]{1,0:T(8,128)S(1)}, u32[]{:S(2)}, u32[]{:S(2)}) collective-permute-start(f32[8,128]{1,0:T(8,128)S(1)} %get-tuple-element.86), channel_id=1, source_target_pairs={{0,8},{8,0},{16,24},{24,16},{32,40},{40,32},{48,56},{56,48},{64,72... | collective-permute-start | bytes 12296 | tf_op jit(solution)/shard_map/ppermute | solution.py:635
  40.9 1.8 %second0.1 = (f32[32,64]{1,0:T(8,128)S(1)}, f32[32,384]{1,0:T(8,128)S(1)}, f32[8,128]{1,0:T(8,128)S(1)}, f32[8,128]{1,0:T(8,128)S(1)}, f32[8,128]{1,0:T(8,128)S(...) custom-call(s32[4,20]{1,0:T(4,128)S(1)} %concatenate.3.ints_ref.ints.refs_0_, ...), custom_call_target="tpu_custom_call" | custom-call | tf_op jit(solution)/shard_map/second0/pallas_call | solution.py:574
  42.7 1.8 %collective-permute-start.8 = (f32[8,128]{1,0:T(8,128)S(1)}, f32[8,128]{1,0:T(8,128)S(1)}, u32[]{:S(2)}, u32[]{:S(2)}) collective-permute-start(f32[8,128]{1,0:T(8,128)S(1)} %get-tuple-element.92), channel_id=1, source_target_pairs={{0,1},{1,0},{2,3},{3,2},{4,5},{5,4},{6,7},{7,6},{8,9},{9,8},{10,11... | collective-permute-start | bytes 12296 | tf_op jit(solution)/shard_map/ppermute | solution.py:635
  45.5 3.3 %collective-permute-start.12 = (f32[8,128]{1,0:T(8,128)S(1)}, f32[8,128]{1,0:T(8,128)S(1)}, u32[]{:S(2)}, u32[]{:S(2)}) collective-permute-start(f32[8,128]{1,0:T(8,128)S(1)} %get-tuple-element.96), channel_id=1, source_target_pairs={{0,8},{8,0},{16,24},{24,16},{32,40},{40,32},{48,56},{56,48},{64,72... | collective-permute-start | bytes 12296 | tf_op jit(solution)/shard_map/ppermute | solution.py:635
  51.0 11.0 %all-to-all-start.1 = ((f32[256,1,128]{2,1,0:T(1,128)}), f32[256,1,128]{2,1,0:T(1,128)S(1)}, u32[]{:S(2)}, u32[]{:S(2)}) async-start(f32[256,1,128]{2,1,0:T(1,128)} %bitcast.13), calls=%async_computation.1 | async-start | bytes 262144 | tf_op jit(solution)/shard_map/all_to_all | solution.py:757
  61.9 1.5 %collective-permute-start.15 = (f32[1,256]{1,0:T(1,128)S(1)}, f32[1,256]{1,0:T(1,128)S(1)}, u32[]{:S(2)}, u32[]{:S(2)}) collective-permute-start(f32[1,256]{1,0:T(1,128)S(1)} %get-tuple-element.99.r0), channel_id=1, source_target_pairs={{0,2},{2,0},{4,6},{6,4},{1,3},{3,1},{5,7},{7,5},{8,10},{10,8},{12,... | collective-permute-start | bytes 3080 | tf_op jit(solution)/shard_map/ppermute | solution.py:639
  63.4 1.8 %collective-permute-start.14 = (f32[1,256]{1,0:T(1,128)S(1)}, f32[1,256]{1,0:T(1,128)S(1)}, u32[]{:S(2)}, u32[]{:S(2)}) collective-permute-start(f32[1,256]{1,0:T(1,128)S(1)} %get-tuple-element.99.r0), channel_id=1, source_target_pairs={{0,6},{2,4},{4,2},{6,0},{1,7},{3,5},{5,3},{7,1},{8,14},{10,12},{12... | collective-permute-start | bytes 3080 | tf_op jit(solution)/shard_map/ppermute | solution.py:639
  67.0 2.1 %collective-permute-done.13.r1 = f32[1,256]{1,0:T(1,128)S(1)} collective-permute-done((f32[1,256]{1,0:T(1,128)S(1)}, f32[1,256]{1,0:T(1,128)S(1)}, u32[]{:S(2)}, u32[]{:S(2)}) %collective-permute-start.13) | collective-permute-done | bytes 1056 | tf_op jit(solution)/shard_map/ppermute | solution.py:639
  69.5 5.4 %all-to-all-done.1 = f32[256,1,128]{2,1,0:T(1,128)S(1)} async-done(((f32[256,1,128]{2,1,0:T(1,128)}), f32[256,1,128]{2,1,0:T(1,128)S(1)}, u32[]{:S(2)}, u32[]{:S(2)}) %all-to-all-start.1) | async-done | bytes 131104 | tf_op jit(solution)/shard_map/all_to_all | solution.py:757
  74.9 1.4 %first1.1 = (f32[32,64]{1,0:T(8,128)S(1)}, f32[8,128]{1,0:T(8,128)S(1)}, f32[32,64]{1,0:T(8,128)S(1)}, f32[32,384]{1,0:T(8,128)S(1)}, f32[8,128]{1,0:T(8,128)S(1...) custom-call(s32[4,20]{1,0:T(4,128)S(1)} %concatenate.3.ints_ref.ints.refs_0_, ...), custom_call_target="tpu_custom_call" | custom-call | tf_op jit(solution)/shard_map/first1/pallas_call | solution.py:574
  77.1 1.9 %collective-permute-start.17 = (f32[8,128]{1,0:T(8,128)S(1)}, f32[8,128]{1,0:T(8,128)S(1)}, u32[]{:S(2)}, u32[]{:S(2)}) collective-permute-start(f32[8,128]{1,0:T(8,128)S(1)} %get-tuple-element.105), channel_id=1, source_target_pairs={{0,248},{8,16},{16,8},{24,32},{32,24},{40,48},{48,40},{56,64},{64,... | collective-permute-start | bytes 12296 | tf_op jit(solution)/shard_map/ppermute | solution.py:635
  81.6 1.5 %collective-permute-done.19.refs_7_ = f32[8,128]{1,0:T(8,128)S(1)} collective-permute-done((f32[8,128]{1,0:T(8,128)S(1)}, f32[8,128]{1,0:T(8,128)S(1)}, u32[]{:S(2)}, u32[]{:S(2)}) %collective-permute-start.19) | collective-permute-done | bytes 4128 | tf_op jit(solution)/shard_map/ppermute | solution.py:635
  83.1 1.8 %second1.1 = (f32[32,64]{1,0:T(8,128)S(1)}, f32[32,384]{1,0:T(8,128)S(1)}, f32[8,128]{1,0:T(8,128)S(1)}, f32[8,128]{1,0:T(8,128)S(1)}, f32[8,128]{1,0:T(8,128)S(...) custom-call(s32[4,20]{1,0:T(4,128)S(1)} %concatenate.3.ints_ref.ints.refs_0_, ...), custom_call_target="tpu_custom_call" | custom-call | tf_op jit(solution)/shard_map/second1/pallas_call | solution.py:574
  84.8 1.6 %collective-permute-start.21 = (f32[8,128]{1,0:T(8,128)S(1)}, f32[8,128]{1,0:T(8,128)S(1)}, u32[]{:S(2)}, u32[]{:S(2)}) collective-permute-start(f32[8,128]{1,0:T(8,128)S(1)} %get-tuple-element.111), channel_id=1, source_target_pairs={{0,1},{1,0},{2,3},{3,2},{4,5},{5,4},{6,7},{7,6},{8,9},{9,8},{10,11... | collective-permute-start | bytes 12296 | tf_op jit(solution)/shard_map/ppermute | solution.py:635
  86.5 2.2 %collective-permute-start.22 = (f32[8,128]{1,0:T(8,128)S(1)}, f32[8,128]{1,0:T(8,128)S(1)}, u32[]{:S(2)}, u32[]{:S(2)}) collective-permute-start(f32[8,128]{1,0:T(8,128)S(1)} %get-tuple-element.112), channel_id=1, source_target_pairs={{0,248},{8,16},{16,8},{24,32},{32,24},{40,48},{48,40},{56,64},{64,... | collective-permute-start | bytes 12296 | tf_op jit(solution)/shard_map/ppermute | solution.py:635
  94.6 1.8 %collective-permute-start.26 = (f32[1,256]{1,0:T(1,128)S(1)}, f32[1,256]{1,0:T(1,128)S(1)}, u32[]{:S(2)}, u32[]{:S(2)}) collective-permute-start(f32[1,256]{1,0:T(1,128)S(1)} %get-tuple-element.117.r0), channel_id=1, source_target_pairs={{0,4},{2,6},{4,0},{6,2},{1,5},{3,7},{5,1},{7,3},{8,12},{10,14},{12... | collective-permute-start | bytes 3080 | tf_op jit(solution)/shard_map/ppermute | solution.py:639
  99.8 3.1 %collective-permute-start.29 = (f32[8,128]{1,0:T(8,128)S(1)}, f32[8,128]{1,0:T(8,128)S(1)}, u32[]{:S(2)}, u32[]{:S(2)}) collective-permute-start(f32[8,128]{1,0:T(8,128)S(1)} %get-tuple-element.120), channel_id=1, source_target_pairs={{0,1},{1,0},{2,3},{3,2},{4,5},{5,4},{6,7},{7,6},{8,9},{9,8},{10,11... | collective-permute-start | bytes 12296 | tf_op jit(solution)/shard_map/ppermute | solution.py:635
  104.8 1.9 %collective-permute-start.32 = (f32[8,128]{1,0:T(8,128)S(1)}, f32[8,128]{1,0:T(8,128)S(1)}, u32[]{:S(2)}, u32[]{:S(2)}) collective-permute-start(f32[8,128]{1,0:T(8,128)S(1)} %get-tuple-element.123), channel_id=1, source_target_pairs={{0,6},{2,4},{4,2},{6,0},{1,7},{3,5},{5,3},{7,1},{8,14},{10,12},{12... | collective-permute-start | bytes 12296 | tf_op jit(solution)/shard_map/ppermute | solution.py:635
  106.7 2.3 %collective-permute-start.33 = (f32[8,128]{1,0:T(8,128)S(1)}, f32[8,128]{1,0:T(8,128)S(1)}, u32[]{:S(2)}, u32[]{:S(2)}) collective-permute-start(f32[8,128]{1,0:T(8,128)S(1)} %get-tuple-element.124), channel_id=1, source_target_pairs={{0,8},{8,0},{16,24},{24,16},{32,40},{40,32},{48,56},{56,48},{64,72... | collective-permute-start | bytes 12296 | tf_op jit(solution)/shard_map/ppermute | solution.py:635
  109.8 1.8 %second2.1 = (f32[32,64]{1,0:T(8,128)S(1)}, f32[32,384]{1,0:T(8,128)S(1)}, f32[8,128]{1,0:T(8,128)S(1)}, f32[8,128]{1,0:T(8,128)S(1)}, f32[8,128]{1,0:T(8,128)S(...) custom-call(s32[4,20]{1,0:T(4,128)S(1)} %concatenate.3.ints_ref.ints.refs_0_, ...), custom_call_target="tpu_custom_call" | custom-call | tf_op jit(solution)/shard_map/second2/pallas_call | solution.py:574
  112.5 1.4 collective-permute-start.35
  113.9 1.8 %collective-permute-start.37 = (f32[8,128]{1,0:T(8,128)S(1)}, f32[8,128]{1,0:T(8,128)S(1)}, u32[]{:S(2)}, u32[]{:S(2)}) collective-permute-start(f32[8,128]{1,0:T(8,128)S(1)} %get-tuple-element.130), channel_id=1, source_target_pairs={{0,6},{2,4},{4,2},{6,0},{1,7},{3,5},{5,3},{7,1},{8,14},{10,12},{12... | collective-permute-start | bytes 12296 | tf_op jit(solution)/shard_map/ppermute | solution.py:635
  115.7 2.5 %collective-permute-start.38 = (f32[8,128]{1,0:T(8,128)S(1)}, f32[8,128]{1,0:T(8,128)S(1)}, u32[]{:S(2)}, u32[]{:S(2)}) collective-permute-start(f32[8,128]{1,0:T(8,128)S(1)} %get-tuple-element.131), channel_id=1, source_target_pairs={{0,8},{8,0},{16,24},{24,16},{32,40},{40,32},{48,56},{56,48},{64,72... | collective-permute-start | bytes 12296 | tf_op jit(solution)/shard_map/ppermute | solution.py:635
  119.7 22.7 %all_to_all.33 = f32[256,1,128]{2,1,0:T(1,128)S(1)} all-to-all(f32[256,1,128]{2,1,0:T(1,128)S(1)} %bitcast.25), channel_id=1, replica_groups=mesh['passage'=32,'span'=4,'radial'=2] {'passage','span','radial'}, dimensions={0} | all-to-all | bytes 262144 | tf_op jit(solution)/shard_map/all_to_all | solution.py:764
  142.4 1.4 final.1
  (121 shorter events, 32.8 us)
Async XLA Ops:
  2.1 28.7 %all-to-all-start = ((f32[256,1,128]{2,1,0:T(1,128)}), f32[256,1,128]{2,1,0:T(1,128)S(1)}, u32[]{:S(2)}, u32[]{:S(2)}) async-start(f32[256,1,128]{2,1,0:T(1,128)} %bitcast.7), calls=%async_computation | async-start | bytes 262144 | tf_op jit(solution)/shard_map/all_to_all | solution.py:651
  19.6 7.6 %collective-permute-start.2 = (f32[1,256]{1,0:T(1,128)S(1)}, f32[1,256]{1,0:T(1,128)S(1)}, u32[]{:S(2)}, u32[]{:S(2)}) collective-permute-start(f32[1,256]{1,0:T(1,128)S(1)} %get-tuple-element.70.r0), channel_id=1, source_target_pairs={{0,2},{2,0},{4,6},{6,4},{1,3},{3,1},{5,7},{7,5},{8,10},{10,8},{12,... | collective-permute-start | bytes 3080 | tf_op jit(solution)/shard_map/ppermute | solution.py:639
  21.0 6.2 %collective-permute-start.1 = (f32[1,256]{1,0:T(1,128)S(1)}, f32[1,256]{1,0:T(1,128)S(1)}, u32[]{:S(2)}, u32[]{:S(2)}) collective-permute-start(f32[1,256]{1,0:T(1,128)S(1)} %get-tuple-element.70.r0), channel_id=1, source_target_pairs={{0,6},{2,4},{4,2},{6,0},{1,7},{3,5},{5,3},{7,1},{8,14},{10,12},{12... | collective-permute-start | bytes 3080 | tf_op jit(solution)/shard_map/ppermute | solution.py:639
  22.8 4.4 %collective-permute-start = (f32[1,256]{1,0:T(1,128)S(1)}, f32[1,256]{1,0:T(1,128)S(1)}, u32[]{:S(2)}, u32[]{:S(2)}) collective-permute-start(f32[1,256]{1,0:T(1,128)S(1)} %get-tuple-element.70.r0), channel_id=1, source_target_pairs={{0,4},{2,6},{4,0},{6,2},{1,5},{3,7},{5,1},{7,3},{8,12},{10,14},{12... | collective-permute-start | bytes 3080 | tf_op jit(solution)/shard_map/ppermute | solution.py:639
  32.1 8.5 %collective-permute-start.3 = (f32[8,128]{1,0:T(8,128)S(1)}, f32[8,128]{1,0:T(8,128)S(1)}, u32[]{:S(2)}, u32[]{:S(2)}) collective-permute-start(f32[8,128]{1,0:T(8,128)S(1)} %get-tuple-element.82), channel_id=1, source_target_pairs={{0,1},{1,0},{2,3},{3,2},{4,5},{5,4},{6,7},{7,6},{8,9},{9,8},{10,11... | collective-permute-start | bytes 12296 | tf_op jit(solution)/shard_map/ppermute | solution.py:635
  32.9 7.7 %collective-permute-start.4 = (f32[8,128]{1,0:T(8,128)S(1)}, f32[8,128]{1,0:T(8,128)S(1)}, u32[]{:S(2)}, u32[]{:S(2)}) collective-permute-start(f32[8,128]{1,0:T(8,128)S(1)} %get-tuple-element.83), channel_id=1, source_target_pairs={{0,248},{8,16},{16,8},{24,32},{32,24},{40,48},{48,40},{56,64},{64,... | collective-permute-start | bytes 12296 | tf_op jit(solution)/shard_map/ppermute | solution.py:635
  35.5 5.2 %collective-permute-start.5 = (f32[8,128]{1,0:T(8,128)S(1)}, f32[8,128]{1,0:T(8,128)S(1)}, u32[]{:S(2)}, u32[]{:S(2)}) collective-permute-start(f32[8,128]{1,0:T(8,128)S(1)} %get-tuple-element.84), channel_id=1, source_target_pairs={{0,2},{2,0},{4,6},{6,4},{1,3},{3,1},{5,7},{7,5},{8,10},{10,8},{12,... | collective-permute-start | bytes 12296 | tf_op jit(solution)/shard_map/ppermute | solution.py:635
  35.8 4.8 %collective-permute-start.6 = (f32[8,128]{1,0:T(8,128)S(1)}, f32[8,128]{1,0:T(8,128)S(1)}, u32[]{:S(2)}, u32[]{:S(2)}) collective-permute-start(f32[8,128]{1,0:T(8,128)S(1)} %get-tuple-element.85), channel_id=1, source_target_pairs={{0,6},{2,4},{4,2},{6,0},{1,7},{3,5},{5,3},{7,1},{8,14},{10,12},{12... | collective-permute-start | bytes 12296 | tf_op jit(solution)/shard_map/ppermute | solution.py:635
  42.7 6.6 %collective-permute-start.8 = (f32[8,128]{1,0:T(8,128)S(1)}, f32[8,128]{1,0:T(8,128)S(1)}, u32[]{:S(2)}, u32[]{:S(2)}) collective-permute-start(f32[8,128]{1,0:T(8,128)S(1)} %get-tuple-element.92), channel_id=1, source_target_pairs={{0,1},{1,0},{2,3},{3,2},{4,5},{5,4},{6,7},{7,6},{8,9},{9,8},{10,11... | collective-permute-start | bytes 12296 | tf_op jit(solution)/shard_map/ppermute | solution.py:635
  44.5 4.8 %collective-permute-start.9 = (f32[8,128]{1,0:T(8,128)S(1)}, f32[8,128]{1,0:T(8,128)S(1)}, u32[]{:S(2)}, u32[]{:S(2)}) collective-permute-start(f32[8,128]{1,0:T(8,128)S(1)} %get-tuple-element.93), channel_id=1, source_target_pairs={{0,248},{8,16},{16,8},{24,32},{32,24},{40,48},{48,40},{56,64},{64,... | collective-permute-start | bytes 12296 | tf_op jit(solution)/shard_map/ppermute | solution.py:635
  44.5 4.8 %collective-permute-start.10 = (f32[8,128]{1,0:T(8,128)S(1)}, f32[8,128]{1,0:T(8,128)S(1)}, u32[]{:S(2)}, u32[]{:S(2)}) collective-permute-start(f32[8,128]{1,0:T(8,128)S(1)} %get-tuple-element.94), channel_id=1, source_target_pairs={{0,2},{2,0},{4,6},{6,4},{1,3},{3,1},{5,7},{7,5},{8,10},{10,8},{12,... | collective-permute-start | bytes 12296 | tf_op jit(solution)/shard_map/ppermute | solution.py:635
  44.8 4.5 %collective-permute-start.11 = (f32[8,128]{1,0:T(8,128)S(1)}, f32[8,128]{1,0:T(8,128)S(1)}, u32[]{:S(2)}, u32[]{:S(2)}) collective-permute-start(f32[8,128]{1,0:T(8,128)S(1)} %get-tuple-element.95), channel_id=1, source_target_pairs={{0,6},{2,4},{4,2},{6,0},{1,7},{3,5},{5,3},{7,1},{8,14},{10,12},{12... | collective-permute-start | bytes 12296 | tf_op jit(solution)/shard_map/ppermute | solution.py:635
  45.5 4.2 %collective-permute-start.12 = (f32[8,128]{1,0:T(8,128)S(1)}, f32[8,128]{1,0:T(8,128)S(1)}, u32[]{:S(2)}, u32[]{:S(2)}) collective-permute-start(f32[8,128]{1,0:T(8,128)S(1)} %get-tuple-element.96), channel_id=1, source_target_pairs={{0,8},{8,0},{16,24},{24,16},{32,40},{40,32},{48,56},{56,48},{64,72... | collective-permute-start | bytes 12296 | tf_op jit(solution)/shard_map/ppermute | solution.py:635
  51.0 24.0 %all-to-all-start.1 = ((f32[256,1,128]{2,1,0:T(1,128)}), f32[256,1,128]{2,1,0:T(1,128)S(1)}, u32[]{:S(2)}, u32[]{:S(2)}) async-start(f32[256,1,128]{2,1,0:T(1,128)} %bitcast.13), calls=%async_computation.1 | async-start | bytes 262144 | tf_op jit(solution)/shard_map/all_to_all | solution.py:757
  61.9 3.9 %collective-permute-start.15 = (f32[1,256]{1,0:T(1,128)S(1)}, f32[1,256]{1,0:T(1,128)S(1)}, u32[]{:S(2)}, u32[]{:S(2)}) collective-permute-start(f32[1,256]{1,0:T(1,128)S(1)} %get-tuple-element.99.r0), channel_id=1, source_target_pairs={{0,2},{2,0},{4,6},{6,4},{1,3},{3,1},{5,7},{7,5},{8,10},{10,8},{12,... | collective-permute-start | bytes 3080 | tf_op jit(solution)/shard_map/ppermute | solution.py:639
  63.4 3.6 %collective-permute-start.14 = (f32[1,256]{1,0:T(1,128)S(1)}, f32[1,256]{1,0:T(1,128)S(1)}, u32[]{:S(2)}, u32[]{:S(2)}) collective-permute-start(f32[1,256]{1,0:T(1,128)S(1)} %get-tuple-element.99.r0), channel_id=1, source_target_pairs={{0,6},{2,4},{4,2},{6,0},{1,7},{3,5},{5,3},{7,1},{8,14},{10,12},{12... | collective-permute-start | bytes 3080 | tf_op jit(solution)/shard_map/ppermute | solution.py:639
  65.2 3.9 %collective-permute-start.13 = (f32[1,256]{1,0:T(1,128)S(1)}, f32[1,256]{1,0:T(1,128)S(1)}, u32[]{:S(2)}, u32[]{:S(2)}) collective-permute-start(f32[1,256]{1,0:T(1,128)S(1)} %get-tuple-element.99.r0), channel_id=1, source_target_pairs={{0,4},{2,6},{4,0},{6,2},{1,5},{3,7},{5,1},{7,3},{8,12},{10,14},{12... | collective-permute-start | bytes 3080 | tf_op jit(solution)/shard_map/ppermute | solution.py:639
  76.3 4.1 %collective-permute-start.16 = (f32[8,128]{1,0:T(8,128)S(1)}, f32[8,128]{1,0:T(8,128)S(1)}, u32[]{:S(2)}, u32[]{:S(2)}) collective-permute-start(f32[8,128]{1,0:T(8,128)S(1)} %get-tuple-element.104), channel_id=1, source_target_pairs={{0,1},{1,0},{2,3},{3,2},{4,5},{5,4},{6,7},{7,6},{8,9},{9,8},{10,11... | collective-permute-start | bytes 12296 | tf_op jit(solution)/shard_map/ppermute | solution.py:635
  79.4 3.7 %collective-permute-start.19 = (f32[8,128]{1,0:T(8,128)S(1)}, f32[8,128]{1,0:T(8,128)S(1)}, u32[]{:S(2)}, u32[]{:S(2)}) collective-permute-start(f32[8,128]{1,0:T(8,128)S(1)} %get-tuple-element.107), channel_id=1, source_target_pairs={{0,6},{2,4},{4,2},{6,0},{1,7},{3,5},{5,3},{7,1},{8,14},{10,12},{12... | collective-permute-start | bytes 12296 | tf_op jit(solution)/shard_map/ppermute | solution.py:635
  84.8 6.4 %collective-permute-start.21 = (f32[8,128]{1,0:T(8,128)S(1)}, f32[8,128]{1,0:T(8,128)S(1)}, u32[]{:S(2)}, u32[]{:S(2)}) collective-permute-start(f32[8,128]{1,0:T(8,128)S(1)} %get-tuple-element.111), channel_id=1, source_target_pairs={{0,1},{1,0},{2,3},{3,2},{4,5},{5,4},{6,7},{7,6},{8,9},{9,8},{10,11... | collective-permute-start | bytes 12296 | tf_op jit(solution)/shard_map/ppermute | solution.py:635
  86.5 4.7 %collective-permute-start.22 = (f32[8,128]{1,0:T(8,128)S(1)}, f32[8,128]{1,0:T(8,128)S(1)}, u32[]{:S(2)}, u32[]{:S(2)}) collective-permute-start(f32[8,128]{1,0:T(8,128)S(1)} %get-tuple-element.112), channel_id=1, source_target_pairs={{0,248},{8,16},{16,8},{24,32},{32,24},{40,48},{48,40},{56,64},{64,... | collective-permute-start | bytes 12296 | tf_op jit(solution)/shard_map/ppermute | solution.py:635
  88.6 3.7 %collective-permute-start.24 = (f32[8,128]{1,0:T(8,128)S(1)}, f32[8,128]{1,0:T(8,128)S(1)}, u32[]{:S(2)}, u32[]{:S(2)}) collective-permute-start(f32[8,128]{1,0:T(8,128)S(1)} %get-tuple-element.114), channel_id=1, source_target_pairs={{0,6},{2,4},{4,2},{6,0},{1,7},{3,5},{5,3},{7,1},{8,14},{10,12},{12... | collective-permute-start | bytes 12296 | tf_op jit(solution)/shard_map/ppermute | solution.py:635
  93.1 3.7 %collective-permute-start.28 = (f32[1,256]{1,0:T(1,128)S(1)}, f32[1,256]{1,0:T(1,128)S(1)}, u32[]{:S(2)}, u32[]{:S(2)}) collective-permute-start(f32[1,256]{1,0:T(1,128)S(1)} %get-tuple-element.117.r0), channel_id=1, source_target_pairs={{0,2},{2,0},{4,6},{6,4},{1,3},{3,1},{5,7},{7,5},{8,10},{10,8},{12,... | collective-permute-start | bytes 3080 | tf_op jit(solution)/shard_map/ppermute | solution.py:639
  94.6 3.9 %collective-permute-start.26 = (f32[1,256]{1,0:T(1,128)S(1)}, f32[1,256]{1,0:T(1,128)S(1)}, u32[]{:S(2)}, u32[]{:S(2)}) collective-permute-start(f32[1,256]{1,0:T(1,128)S(1)} %get-tuple-element.117.r0), channel_id=1, source_target_pairs={{0,4},{2,6},{4,0},{6,2},{1,5},{3,7},{5,1},{7,3},{8,12},{10,14},{12... | collective-permute-start | bytes 3080 | tf_op jit(solution)/shard_map/ppermute | solution.py:639
  99.8 9.7 %collective-permute-start.29 = (f32[8,128]{1,0:T(8,128)S(1)}, f32[8,128]{1,0:T(8,128)S(1)}, u32[]{:S(2)}, u32[]{:S(2)}) collective-permute-start(f32[8,128]{1,0:T(8,128)S(1)} %get-tuple-element.120), channel_id=1, source_target_pairs={{0,1},{1,0},{2,3},{3,2},{4,5},{5,4},{6,7},{7,6},{8,9},{9,8},{10,11... | collective-permute-start | bytes 12296 | tf_op jit(solution)/shard_map/ppermute | solution.py:635
  102.9 6.7 %collective-permute-start.30 = (f32[8,128]{1,0:T(8,128)S(1)}, f32[8,128]{1,0:T(8,128)S(1)}, u32[]{:S(2)}, u32[]{:S(2)}) collective-permute-start(f32[8,128]{1,0:T(8,128)S(1)} %get-tuple-element.121), channel_id=1, source_target_pairs={{0,248},{8,16},{16,8},{24,32},{32,24},{40,48},{48,40},{56,64},{64,... | collective-permute-start | bytes 12296 | tf_op jit(solution)/shard_map/ppermute | solution.py:635
  103.7 5.8 %collective-permute-start.31 = (f32[8,128]{1,0:T(8,128)S(1)}, f32[8,128]{1,0:T(8,128)S(1)}, u32[]{:S(2)}, u32[]{:S(2)}) collective-permute-start(f32[8,128]{1,0:T(8,128)S(1)} %get-tuple-element.122), channel_id=1, source_target_pairs={{0,2},{2,0},{4,6},{6,4},{1,3},{3,1},{5,7},{7,5},{8,10},{10,8},{12,... | collective-permute-start | bytes 12296 | tf_op jit(solution)/shard_map/ppermute | solution.py:635
  104.8 4.8 %collective-permute-start.32 = (f32[8,128]{1,0:T(8,128)S(1)}, f32[8,128]{1,0:T(8,128)S(1)}, u32[]{:S(2)}, u32[]{:S(2)}) collective-permute-start(f32[8,128]{1,0:T(8,128)S(1)} %get-tuple-element.123), channel_id=1, source_target_pairs={{0,6},{2,4},{4,2},{6,0},{1,7},{3,5},{5,3},{7,1},{8,14},{10,12},{12... | collective-permute-start | bytes 12296 | tf_op jit(solution)/shard_map/ppermute | solution.py:635
  111.6 7.2 %collective-permute-start.34 = (f32[8,128]{1,0:T(8,128)S(1)}, f32[8,128]{1,0:T(8,128)S(1)}, u32[]{:S(2)}, u32[]{:S(2)}) collective-permute-start(f32[8,128]{1,0:T(8,128)S(1)} %get-tuple-element.127), channel_id=1, source_target_pairs={{0,1},{1,0},{2,3},{3,2},{4,5},{5,4},{6,7},{7,6},{8,9},{9,8},{10,11... | collective-permute-start | bytes 12296 | tf_op jit(solution)/shard_map/ppermute | solution.py:635
  112.5 6.2 %collective-permute-start.35 = (f32[8,128]{1,0:T(8,128)S(1)}, f32[8,128]{1,0:T(8,128)S(1)}, u32[]{:S(2)}, u32[]{:S(2)}) collective-permute-start(f32[8,128]{1,0:T(8,128)S(1)} %get-tuple-element.128), channel_id=1, source_target_pairs={{0,248},{8,16},{16,8},{24,32},{32,24},{40,48},{48,40},{56,64},{64,... | collective-permute-start | bytes 12296 | tf_op jit(solution)/shard_map/ppermute | solution.py:635
  113.9 4.8 %collective-permute-start.36 = (f32[8,128]{1,0:T(8,128)S(1)}, f32[8,128]{1,0:T(8,128)S(1)}, u32[]{:S(2)}, u32[]{:S(2)}) collective-permute-start(f32[8,128]{1,0:T(8,128)S(1)} %get-tuple-element.129), channel_id=1, source_target_pairs={{0,2},{2,0},{4,6},{6,4},{1,3},{3,1},{5,7},{7,5},{8,10},{10,8},{12,... | collective-permute-start | bytes 12296 | tf_op jit(solution)/shard_map/ppermute | solution.py:635
  113.9 4.9 %collective-permute-start.37 = (f32[8,128]{1,0:T(8,128)S(1)}, f32[8,128]{1,0:T(8,128)S(1)}, u32[]{:S(2)}, u32[]{:S(2)}) collective-permute-start(f32[8,128]{1,0:T(8,128)S(1)} %get-tuple-element.130), channel_id=1, source_target_pairs={{0,6},{2,4},{4,2},{6,0},{1,7},{3,5},{5,3},{7,1},{8,14},{10,12},{12... | collective-permute-start | bytes 12296 | tf_op jit(solution)/shard_map/ppermute | solution.py:635
  (31 other events, 245.4 us)

commit v2 on v1

--- a/solution.py
+++ b/solution.py
@@ -23,6 +23,9 @@
 AXES = ("passage", "span", "radial")
 NEIGH, ORIENT, TAGS, GROUP, PLACE = 0, 6, 12, 18, 19
 HIGHEST = lax.Precision.HIGHEST
+GROWN = 3 * NODES + 6 * 2 * FACE
+LAID = 6 * 8 * FACE
+CONSTS = ((0, 80, 256), (80, 8, 256), (88, 8, 256), (96, 24, 96), (120, 32, 96), (152, 32, 24))
 F32 = jnp.float32
 
 
@@ -109,23 +112,21 @@
     restrict = np.zeros((NODES, WIDE), np.float32)
     restrict[:, :KC] = np.tile(rtab.T, (1, CG * VARS))
     lay = np.einsum("aob,fbk->foak", turn, place[:, 0]).reshape(6 * 8 * FACE, NODES)
-    own_lanes = np.zeros((RW, ROWS), np.float32)
-    for row in range(RW):
-        v = row % STRIDE
+    tile = np.zeros((80, 256), np.float32)
+    for col in range(256):
+        kind, v = col // RW % 2, col % STRIDE
         if v < VARS:
-            own_lanes[row, v * NODES : (v + 1) * NODES] = 1.0
-    tile = np.zeros((80, 6 * 256), np.float32)
-    colcode = np.full((8, 6 * 256), -100.0, np.float32)
+            tile[kind * 40 + v * 8 : kind * 40 + v * 8 + 6, col] = 1.0
+    code = np.full((8, 256), -100.0, np.float32)
+    sign = np.ones((8, 256), np.float32)
     for face in range(6):
         axis = face // 2
         for place_id, source in enumerate(SOURCES[axis]):
             for col in range(2 * RW):
                 kind, n, v = col // RW, col // STRIDE % ELEMS, col % STRIDE
-                lane = face * 256 + place_id * 2 * RW + col
-                if v < VARS:
-                    tile[kind * 40 + v * 8 + face, lane] = 1.0
-                colcode[0, lane] = source * ELEMS + n
-                colcode[1, lane] = (-1.0 if v == 1 + axis else 1.0) * (-1.0 if kind else 1.0)
+                lane = place_id * 2 * RW + col
+                code[face, lane] = source * ELEMS + n
+                sign[face, lane] = (-1.0 if v == 1 + axis else 1.0) * (-1.0 if kind else 1.0)
     rows = np.zeros((RW, 24), np.float32)
     for e in range(ELEMS):
         for u in range(VARS):
@@ -137,17 +138,15 @@
         if v < VARS:
             vtile[axis * 8 + v, col] = 1.0
         vmask[n * STRIDE : (n + 1) * STRIDE, col] = 1.0
+    consts = np.zeros((184, 256), np.float32)
+    for (row, count, lanes), part in zip(CONSTS, (tile, code, sign, vtile, vmask, rows)):
+        consts[row : row + count, :lanes] = part
     return dict(
-        de=stacked(de),
-        lay=lay.astype(jnp.bfloat16),
-        restrict=stacked(restrict),
-        spread=stacked(np.ascontiguousarray(restrict.T)),
-        own_lanes=own_lanes,
-        tile=tile,
-        colcode=colcode,
-        rows=rows,
-        vtile=vtile,
-        vmask=vmask,
+        consts=consts,
+        rise=np.concatenate([stacked(de), stacked(restrict)], axis=1),
+        lay=np.concatenate(
+            [lay.astype(jnp.bfloat16), stacked(np.ascontiguousarray(restrict.T))], axis=0
+        ),
     )
 
 
@@ -188,8 +187,8 @@
     return jnp.concatenate(pieces, axis=0)
 
 
-def coarse_row(member, restrict, vector):
-    return jnp.sum(member * dot(left_stack(vector), restrict), axis=0, keepdims=True)
+def coarse_row(member, rise_ref, vector):
+    return jnp.sum(member * dot(left_stack(vector), rise_ref[:, GROWN:]), axis=0, keepdims=True)
 
 
 def scalar_row(scalars):
@@ -205,29 +204,26 @@
     return [sums[:, i : i + 1] for i in range(count)]
 
 
-def coarse_values(coarse, cinv_ref, member_ref, spread_ref):
-    solved = lax.dot_general(
-        left_stack(coarse[:, :KC]),
-        cinv_ref[...],
-        (((1,), (1,)), ((), ())),
-        preferred_element_type=F32,
-    )
+def coarse_values(coarse, cinv_ref, member_ref, lay_ref):
+    solved = dot(left_stack(coarse[:, :KC]), cinv_ref[...])
     solved = jnp.concatenate([solved, jnp.zeros((1, WIDE - KC), F32)], axis=1)
-    return dot(left_stack(member_ref[...] * solved), spread_ref[...])
-
-
-def apply_blocks(turned_ref, own_lanes, parts):
+    return dot(left_stack(member_ref[...] * solved), lay_ref[LAID:, :])
+
+
+def apply_blocks(turned_ref, parts):
+    row = lax.broadcasted_iota(jnp.int32, (RW, ROWS), 0) % STRIDE
+    own_lanes = lax.broadcasted_iota(jnp.int32, (RW, ROWS), 1) // NODES == row
     stacked = []
     for part in parts:
         pair = jnp.concatenate([part, part], axis=1)
-        stacked.append(jnp.concatenate([pair, pair, part], axis=1) * own_lanes)
+        stacked.append(jnp.where(own_lanes, jnp.concatenate([pair, pair, part], axis=1), 0.0))
     pieces = []
     for e in range(ELEMS):
         rows = [part[e * STRIDE : (e + 1) * STRIDE] for part in stacked]
         rows = jnp.concatenate(rows, axis=0) if len(rows) > 1 else rows[0]
         out = dot(rows.astype(jnp.bfloat16), turned_ref[e])
         pieces.append(jnp.broadcast_to(jnp.sum(out, axis=0, keepdims=True), (STRIDE, ROWS)))
-    full = jnp.concatenate(pieces, axis=0) * own_lanes
+    full = jnp.where(own_lanes, jnp.concatenate(pieces, axis=0), 0.0)
     half = full[:, :128] + full[:, 128:256]
     return half[:, :NODES] + half[:, NODES:] + full[:, 256:]
 
@@ -261,17 +257,24 @@
 
 
 def unpack(tile):
-    return [copies(tile, e * 2 + kind) for kind in range(2) for e in range(ELEMS)]
-
-
-def write_sends(ints_ref, grown, send_refs):
-    p_odd, s_odd, r = ints_ref[0, PLACE] % 2, ints_ref[1, PLACE] % 2, ints_ref[2, PLACE]
+    slot = lax.broadcasted_iota(jnp.int32, tile.shape, 1) // FACE
+    level = [tile]
+    for bit in (1, 2, 4):
+        upper = slot & bit != 0
+        without = [jnp.where(upper, pltpu.roll(a, bit * FACE, 1), a) for a in level]
+        only = [jnp.where(upper, a, pltpu.roll(a, 128 - bit * FACE, 1)) for a in level]
+        level = without + only
+    return [level[e * 2 + kind] for kind in range(2) for e in range(ELEMS)]
+
+
+def write_sends(odd_ref, grown, send_refs):
+    p_odd, s_odd, r = (odd_ref[i * STRIDE : (i + 1) * STRIDE, :] > 0.5 for i in range(3))
     faces = [pack(grown, f) for f in range(6)]
-    send_refs[0][...] = jnp.where(r == 0, faces[5], faces[4])
-    send_refs[1][...] = jnp.where(p_odd == 0, faces[0], faces[1])
-    send_refs[2][...] = jnp.where(s_odd == 0, faces[3], faces[2])
-    send_refs[3][...] = jnp.where(s_odd == 0, faces[2], faces[3])
-    send_refs[4][...] = jnp.where(p_odd == 0, faces[1], faces[0])
+    send_refs[0][...] = jnp.where(r, faces[4], faces[5])
+    send_refs[1][...] = jnp.where(p_odd, faces[1], faces[0])
+    send_refs[2][...] = jnp.where(s_odd, faces[2], faces[3])
+    send_refs[3][...] = jnp.where(s_odd, faces[3], faces[2])
+    send_refs[4][...] = jnp.where(p_odd, faces[0], faces[1])
 
 
 def place_terms(groups, omask_ref, lay_ref, first_face):
@@ -282,7 +285,7 @@
         laid += [terms[:RW], terms[RW:]]
     laid = jnp.concatenate(laid, axis=1)
     high, low = halves(laid)
-    out = dot(jnp.concatenate([high, low], axis=0), lay_ref[first_face * 8 * FACE :, :])
+    out = dot(jnp.concatenate([high, low], axis=0), lay_ref[first_face * 8 * FACE : LAID, :])
     return out[:RW] + out[RW:]
 
 
@@ -299,7 +302,7 @@
     table_ref[...] = jnp.broadcast_to(scalar_row([total(rs * rs)]), table_ref.shape)
 
 
-def prepare_kernel(rs_ref, mass_ref, ints_ref, restrict_ref, x_ref, massw_ref, member_ref, row_ref):
+def prepare_kernel(rs_ref, mass_ref, ints_ref, rise_ref, x_ref, massw_ref, member_ref, odd_ref, row_ref):
     x_ref[...] = jnp.zeros_like(x_ref)
     massw_ref[...] = jnp.zeros_like(massw_ref)
     for e in range(ELEMS):
@@ -310,7 +313,10 @@
             massw_ref[row : row + 1, :] = mass_ref[e : e + 1, lanes]
     member = member_mask(ints_ref)
     member_ref[...] = member
-    row_ref[...] = coarse_row(member, restrict_ref[...], x_ref[...])
+    row_ref[...] = coarse_row(member, rise_ref, x_ref[...])
+    for i in range(3):
+        odd = (ints_ref[i, PLACE] % 2).astype(F32)
+        odd_ref[i * STRIDE : (i + 1) * STRIDE, :] = jnp.full((STRIDE, 128), odd, F32)
 
 
 def setup_kernel(
@@ -319,11 +325,7 @@
     flux_ref,
     visc_ref,
     blocks_ref,
-    rows_ref,
-    tile_ref,
-    colcode_ref,
-    vtile_ref,
-    vmask_ref,
+    consts_ref,
     cinv_ref,
     rem0_ref,
     rem1_ref,
@@ -347,17 +349,23 @@
         for v in range(VARS):
             coef_ref[here, v * 8 : v * 8 + 6] = flux_ref[u, v]
             coef_ref[here, 40 + v * 8 : 40 + v * 8 + 6] = visc_ref[u, v]
-    coef = exact_dot(rows_ref[...], coef_ref[...])
-    vmat_ref[...] = right_factor(exact_dot(coef[:, 80:104], vtile_ref[...]) * vmask_ref[...])
-    cinv3_ref[...] = right_factor(cinv_ref[0, 0])
+    tile, codes, wall_signs, vtile, vmask, expand = (
+        consts_ref[a : a + n, :lanes] for a, n, lanes in CONSTS
+    )
+    coef = exact_dot(expand, coef_ref[...])
+    vmat_ref[...] = right_factor(exact_dot(coef[:, 80:104], vtile) * vmask)
+    turned = cinv_ref[0, 0].T
+    high, low = halves(turned)
+    cinv3_ref[...] = jnp.concatenate([high, high, low], axis=0)
     for e in range(ELEMS):
         turned_ref[e] = blocks_ref[e].T
-    spread = exact_dot(coef[:, :80], tile_ref[...])
+    face_lane = lax.broadcasted_iota(jnp.int32, (RW, 80), 1) % 8
+    coef = [jnp.where(face_lane == f, coef[:, :80], 0.0) for f in range(6)]
+    spread = exact_dot(jnp.concatenate(coef, axis=0), tile)
     lane = lax.broadcasted_iota(jnp.int32, (STRIDE, 8 * FACE), 1)
     for f in range(6):
-        cols = slice(f * 256, (f + 1) * 256)
-        colcode = jnp.broadcast_to(colcode_ref[0:1, cols], (STRIDE, 256))
-        signs = jnp.broadcast_to(colcode_ref[1:2, cols], (STRIDE, 256))
+        colcode = jnp.broadcast_to(codes[f : f + 1], (STRIDE, 256))
+        signs = jnp.broadcast_to(wall_signs[f : f + 1], (STRIDE, 256))
         for e in range(ELEMS):
             near = ints_ref[e, NEIGH + f]
             tag = ints_ref[e, TAGS + f]
@@ -380,7 +388,7 @@
                 code = jnp.where(tag == 0, code, jnp.where(tag == 1, wall_code, -1))
                 turn_code = jnp.where(tag == 0, turn_code, 0)
             rows = slice(f * RW + e * STRIDE, f * RW + (e + 1) * STRIDE)
-            values = spread[e * STRIDE : (e + 1) * STRIDE, cols]
+            values = spread[rows]
             values = jnp.where(tag == 1, values * signs, values)
             amat_ref[rows, :] = jnp.where(colcode == code.astype(F32), -values, 0.0)
             omask_ref[rows, :] = jnp.where(lane // FACE == turn_code, 1.0, 0.0)
@@ -397,23 +405,23 @@
     return jnp.concatenate([high, high, values - high], axis=1).astype(jnp.bfloat16)
 
 
-def coarse_kernel(r0, r1, r2, r3, cinv, member, spread, coarse_ref):
+def coarse_kernel(r0, r1, r2, r3, cinv, member, lay, coarse_ref):
     coarse = (r0[...] + r1[...]) + (r2[...] + r3[...])
-    coarse_ref[...] = coarse_values(coarse, cinv, member, spread)
-
-
-def blocks_kernel(x, blocks, own, out_ref):
-    out_ref[...] = apply_blocks(blocks, own[...], two_parts(x[...]))
-
-
-def finish_first(ints, first, de, first_ref, grown_ref, sends):
+    coarse_ref[...] = coarse_values(coarse, cinv, member, lay)
+
+
+def blocks_kernel(x, blocks, out_ref):
+    out_ref[...] = apply_blocks(blocks, two_parts(x[...]))
+
+
+def finish_first(odd, first, rise, first_ref, grown_ref, sends):
     first_ref[...] = first
-    grown = dot(left_stack(first), de[...])
+    grown = dot(left_stack(first), rise[:, :GROWN])
     grown_ref[...] = grown
-    write_sends(ints, grown, sends)
-
-
-def first0_kernel(ints, table, x, coarse, blocks, own, de, *outs):
+    write_sends(odd, grown, sends)
+
+
+def first0_kernel(odd, table, x, coarse, blocks, rise, *outs):
     z_ref, coarse_ref, scal_ref, first_ref, grown_ref, *sends = outs
     beta = jnp.sqrt(read_scalars(table, 1)[0])
     z = x[...] / beta
@@ -421,11 +429,11 @@
     scal_ref[...] = jnp.broadcast_to(beta, scal_ref.shape)
     scaled = coarse[...] / beta
     coarse_ref[...] = scaled
-    first = apply_blocks(blocks, own[...], rounded(z)) + scaled
-    finish_first(ints, first, de, first_ref, grown_ref, sends)
-
-
-def first1_kernel(ints, table, x, coarse, b0, coarse0, blocks, own, de, *outs):
+    first = apply_blocks(blocks, rounded(z)) + scaled
+    finish_first(odd, first, rise, first_ref, grown_ref, sends)
+
+
+def first1_kernel(odd, table, x, coarse, b0, coarse0, blocks, rise, *outs):
     z_ref, scal_ref, first_ref, grown_ref, *sends = outs
     h00, square = read_scalars(table, 2)
     h10 = jnp.sqrt(jnp.maximum(square - h00 * h00, 1e-7 * square))
@@ -434,15 +442,15 @@
     row = lax.broadcasted_iota(jnp.int32, scal_ref.shape, 0)
     scal_ref[...] = jnp.where(row == 0, h00, jnp.where(row == 1, h10, square))
     scaled = (coarse[...] - h00 * coarse0[...]) / h10
-    first = apply_blocks(blocks, own[...], rounded(z)) + scaled
-    finish_first(ints, first, de, first_ref, grown_ref, sends)
-
-
-def first2_kernel(ints, r0, r1, r2, r3, fine, cinv, member, spread, de, *outs):
+    first = apply_blocks(blocks, rounded(z)) + scaled
+    finish_first(odd, first, rise, first_ref, grown_ref, sends)
+
+
+def first2_kernel(odd, r0, r1, r2, r3, fine, cinv, member, lay, rise, *outs):
     first_ref, grown_ref, *sends = outs
     coarse = (r0[...] + r1[...]) + (r2[...] + r3[...])
-    first = fine[...] + coarse_values(coarse, cinv, member, spread)
-    finish_first(ints, first, de, first_ref, grown_ref, sends)
+    first = fine[...] + coarse_values(coarse, cinv, member, lay)
+    finish_first(odd, first, rise, first_ref, grown_ref, sends)
 
 
 def local_kernel(x, grown_ref, mass, vmat, loc1, loc2, omask, lay, out_ref):
@@ -462,17 +470,17 @@
 
 
 def second_kernel(step, *refs):
-    ints, z, first, local = refs[:4]
+    odd, z, first, local = refs[:4]
     recv = refs[4:9]
-    rem, omask, lay, blocks, own, de = refs[9:12], *refs[12:17]
-    search_ref, grown_ref, *sends = refs[17:]
+    rem, omask, lay, blocks, rise = refs[9:12], *refs[12:16]
+    search_ref, grown_ref, *sends = refs[16:]
     defect = z[...] - (local[...] + halo_part(recv, rem, omask, lay))
     parts = two_parts(defect) if step == 2 else rounded(defect)
-    search = first[...] + apply_blocks(blocks, own[...], parts)
+    search = first[...] + apply_blocks(blocks, parts)
     search_ref[...] = search
-    grown = dot(left_stack(search), de[...])
+    grown = dot(left_stack(search), rise[:, :GROWN])
     grown_ref[...] = grown
-    write_sends(ints, grown, sends)
+    write_sends(odd, grown, sends)
 
 
 def third_kernel(step, *refs):
@@ -481,10 +489,10 @@
     rem, omask, lay = refs[6:9], refs[9], refs[10]
     mapped = local[...] + halo_part(recv, rem, omask, lay)
     if step == 0:
-        member, restrict, b0, w_ref, table_ref, row_ref = refs[11:]
+        member, rise, b0, w_ref, table_ref, row_ref = refs[11:]
         scalars = [total(mapped * b0[...]), total(mapped * mapped)]
     elif step == 1:
-        member, restrict, w_ref, row_ref = refs[11:]
+        member, rise, w_ref, row_ref = refs[11:]
     else:
         b0, b1, w1, w_ref, table_ref = refs[11:]
         scalars = [total(w1[...] * b[...]) for b in (b0, b1, w1)]
@@ -494,7 +502,7 @@
     if step != 1:
         table_ref[...] = jnp.broadcast_to(scalar_row(scalars), table_ref.shape)
     if step != 2:
-        row_ref[...] = coarse_row(member[...], restrict[...], mapped)
+        row_ref[...] = coarse_row(member[...], rise, mapped)
 
 
 def inverse_sqrt(value):
@@ -640,7 +648,7 @@
         ]
 
     vec = (RW, NODES)
-    grow = (RW, t["de"].shape[1])
+    grow = (RW, GROWN)
     send = (STRIDE, 128)
     table_shape = (devices, 128)
 
@@ -649,11 +657,11 @@
 
     (table,) = call(start_kernel, "start", (right_side,), [table_shape], raw=(0,))
     table = lax.all_to_all(table, AXES, 0, 0, tiled=True)
-    x, massw, member, row = call(
+    x, massw, member, odd, row = call(
         prepare_kernel,
         "prepare",
-        (right_side, mass, ints, t["restrict"]),
-        [vec, vec, (RW, WIDE), (1, WIDE)],
+        (right_side, mass, ints, t["rise"]),
+        [vec, vec, (RW, WIDE), (3 * STRIDE, 128), (1, WIDE)],
         smem=(2,),
         raw=(0, 1, 3),
     )
@@ -668,11 +676,7 @@
             flux_t,
             visc_t,
             block_inverse,
-            t["rows"],
-            t["tile"],
-            t["colcode"],
-            t["vtile"],
-            t["vmask"],
+            t["consts"],
             coarse_inverse,
         ),
         [
@@ -683,11 +687,11 @@
             pair,
             (6 * RW, 8 * FACE),
             half_floats(RW, 9 * RW),
-            half_floats(KC, 3 * KC),
+            half_floats(3 * KC, KC),
             half_floats(*block_inverse.shape),
         ],
         smem=(0,),
-        raw=tuple(range(1, 11)),
+        raw=tuple(range(1, 7)),
         scratch=[(24, 104), (6 * RW, 256)],
     )
     remote = (rem0, rem1, rem2, omask, t["lay"])
@@ -696,8 +700,8 @@
     def local_part(vector, grown, step):
         return call(local_kernel, "local%d" % step, (vector, grown) + near, [vec])[0]
 
-    coarse_tables = (cinv3, member, t["spread"])
-    tail = (turned, t["own_lanes"], t["de"])
+    coarse_tables = (cinv3, member, t["lay"])
+    tail = (turned, t["rise"])
     basis, search, images, scalars = [], [], [], []
     coarse0 = None
     outs = [vec, grow] + [send] * 5
@@ -708,29 +712,26 @@
             z, coarse0, scal, first, grown, *sends = call(
                 first0_kernel,
                 "first0",
-                (ints, table, x, coarse) + tail,
+                (odd, table, x, coarse) + tail,
                 [vec, vec, (8, 128)] + outs,
-                smem=(0,),
             )
             scalars.append(scal)
         elif step == 1:
             z, scal, first, grown, *sends = call(
                 first1_kernel,
                 "first1",
-                (ints, table, images[0], coarse, basis[0], coarse0) + tail,
+                (odd, table, images[0], coarse, basis[0], coarse0) + tail,
                 [vec, (8, 128)] + outs,
-                smem=(0,),
             )
             scalars.append(scal)
         else:
             z = images[1]
-            (fine,) = call(blocks_kernel, "fine", (z, turned, t["own_lanes"]), [vec])
+            (fine,) = call(blocks_kernel, "fine", (z, turned), [vec])
             first, grown, *sends = call(
                 first2_kernel,
                 "first2",
-                (ints, *rows, fine, *coarse_tables, t["de"]),
+                (odd, *rows, fine, *coarse_tables, t["rise"]),
                 outs,
-                smem=(0,),
             )
         basis.append(z)
         recv = exchange(sends)
@@ -738,9 +739,8 @@
         direction, grown, *sends = call(
             with_step(second_kernel, step),
             "second%d" % step,
-            (ints, z, first, local, *recv) + remote + tail,
+            (odd, z, first, local, *recv) + remote + tail,
             outs,
-            smem=(0,),
         )
         search.append(direction)
         recv = exchange(sends)
@@ -751,13 +751,13 @@
             image, table, row = call(
                 kernel,
                 "third0",
-                args + (member, t["restrict"], basis[0]),
+                args + (member, t["rise"], basis[0]),
                 [vec, table_shape, (1, WIDE)],
             )
             table = lax.all_to_all(table, AXES, 0, 0, tiled=True)
             rows = span_rows(row)
         elif step == 1:
-            image, row = call(kernel, "third1", args + (member, t["restrict"]), [vec, (1, WIDE)])
+            image, row = call(kernel, "third1", args + (member, t["rise"]), [vec, (1, WIDE)])
             rows = span_rows(row)
         else:
             image, table = call(kernel, "third2", args + tuple(basis), [vec, table_shape])

time: 144 us -> 139 us (0.965)
  Pallas kernels: 20.7 us -> 17.3 us
    pallas_call x22, Pallas kernels: 20.7 us -> 17.3 us  [call(): pl.pallas_call(kernel, name=name, out_shape=[shape_of(out) for out in out...]
    ppermute x30, starting transfers between devices: 39.4 us -> 37.9 us  [exchange(): return [lax.ppermute(x, axis, way) for x, (axis, way) in zip(sends, ways)]]
    unnamed x44 -> x30, local copies, waits for them, and re-layouts: 3.46 us -> 2.74 us
  transfers between devices with their start and end apart: 41 -> 41, of which waited for: 14 -> 15; matrix products, arithmetic and copies ran while one was open for 0% -> 0% of each run, Pallas kernels for 5% -> 5%
where the time goes in v2:
time: 139 us
  starting transfers between devices  75.7 us (54%)
  blocking collectives  22.7 us (16%)
  waiting for transfers between devices  19.3 us (14%)
  Pallas kernels  17.3 us (12%)
  local copies, waits for them, and re-layouts  3.03 us (2%)
    ppermute x30, starting transfers between devices, exchange(): return [lax.ppermute(x, axis, way) for x, (axis, way) in zip(sends, ways)]  37.9 us
    all_to_all x2, starting transfers between devices, body(): table = lax.all_to_all(table, AXES, 0, 0, tiled=True)  26.6 us
    all_to_all x1, blocking collectives, body(): table = lax.all_to_all(table, AXES, 0, 0, tiled=True)  22.7 us
    pallas_call x22, Pallas kernels, call(): pl.pallas_call(kernel, name=name, out_shape=[shape_of(out) for out in out...  17.3 us
    ppermute x9, starting transfers between devices, span_rows(): lax.ppermute(row, 'span', [(i, i ^ k) for i in range(n_span)])  11.2 us
    all_to_all x2, waiting for transfers between devices, body(): table = lax.all_to_all(table, AXES, 0, 0, tiled=True)  9.39 us
    ppermute x9, waiting for transfers between devices, span_rows(): lax.ppermute(row, 'span', [(i, i ^ k) for i in range(n_span)])  5.07 us
    ppermute x30, waiting for transfers between devices, exchange(): return [lax.ppermute(x, axis, way) for x, (axis, way) in zip(sends, ways)]  4.88 us
  transfers between devices with their start and end apart: 41, of which 15 were waited for; matrix products, arithmetic and copies ran while one was open for 0% of the time, Pallas kernels for 5%

profile of v2, /device:TPU:1, one launch (start us, length us, event | category | flops | bytes accessed | tf_op | source)
XLA Modules:
  0.0 139.2 jit_solution(12352838981814298395)
XLA Ops:
  2.2 15.7 %all-to-all-start = ((f32[256,1,128]{2,1,0:T(1,128)}), f32[256,1,128]{2,1,0:T(1,128)S(1)}, u32[]{:S(2)}, u32[]{:S(2)}) async-start(f32[256,1,128]{2,1,0:T(1,128)} %bitcast.7), calls=%async_computation | async-start | bytes 262144 | tf_op jit(solution)/shard_map/all_to_all | solution.py:659
  19.2 1.5 %collective-permute-start.2 = (f32[1,256]{1,0:T(1,128)S(1)}, f32[1,256]{1,0:T(1,128)S(1)}, u32[]{:S(2)}, u32[]{:S(2)}) collective-permute-start(f32[1,256]{1,0:T(1,128)S(1)} %get-tuple-element.72.r0), channel_id=1, source_target_pairs={{0,2},{2,0},{4,6},{6,4},{1,3},{3,1},{5,7},{7,5},{8,10},{10,8},{12,... | collective-permute-start | bytes 3080 | tf_op jit(solution)/shard_map/ppermute | solution.py:647
  20.6 1.8 %collective-permute-start.1 = (f32[1,256]{1,0:T(1,128)S(1)}, f32[1,256]{1,0:T(1,128)S(1)}, u32[]{:S(2)}, u32[]{:S(2)}) collective-permute-start(f32[1,256]{1,0:T(1,128)S(1)} %get-tuple-element.72.r0), channel_id=1, source_target_pairs={{0,6},{2,4},{4,2},{6,0},{1,7},{3,5},{5,3},{7,1},{8,14},{10,12},{12... | collective-permute-start | bytes 3080 | tf_op jit(solution)/shard_map/ppermute | solution.py:647
  25.1 1.4 %setup.1 = (bf16[64,384]{1,0:T(8,128)(2,1)S(1)}, bf16[64,384]{1,0:T(8,128)(2,1)S(1)}, bf16[64,192]{1,0:T(8,128)(2,1)S(1)}, bf16[64,384]{1,0:T(8,128)(2,1)S(1)}, ...) custom-call(s32[4,20]{1,0:T(4,128)S(1)} %concatenate.3.ints_ref, ...), custom_call_target="tpu_custom_call" | custom-call | tf_op jit(solution)/shard_map/setup/pallas_call | solution.py:582
  26.9 4.0 %all-to-all-done = f32[256,1,128]{2,1,0:T(1,128)S(1)} async-done(((f32[256,1,128]{2,1,0:T(1,128)}), f32[256,1,128]{2,1,0:T(1,128)S(1)}, u32[]{:S(2)}, u32[]{:S(2)}) %all-to-all-start) | async-done | bytes 131104 | tf_op jit(solution)/shard_map/all_to_all | solution.py:659
  32.4 1.9 %collective-permute-start.4 = (f32[8,128]{1,0:T(8,128)S(1)}, f32[8,128]{1,0:T(8,128)S(1)}, u32[]{:S(2)}, u32[]{:S(2)}) collective-permute-start(f32[8,128]{1,0:T(8,128)S(1)} %get-tuple-element.85), channel_id=1, source_target_pairs={{0,248},{8,16},{16,8},{24,32},{32,24},{40,48},{48,40},{56,64},{64,... | collective-permute-start | bytes 12296 | tf_op jit(solution)/shard_map/ppermute | solution.py:643
  35.8 2.4 %collective-permute-start.7 = (f32[8,128]{1,0:T(8,128)S(1)}, f32[8,128]{1,0:T(8,128)S(1)}, u32[]{:S(2)}, u32[]{:S(2)}) collective-permute-start(f32[8,128]{1,0:T(8,128)S(1)} %get-tuple-element.88), channel_id=1, source_target_pairs={{0,8},{8,0},{16,24},{24,16},{32,40},{40,32},{48,56},{56,48},{64,72... | collective-permute-start | bytes 12296 | tf_op jit(solution)/shard_map/ppermute | solution.py:643
  40.3 1.8 %collective-permute-start.8 = (f32[8,128]{1,0:T(8,128)S(1)}, f32[8,128]{1,0:T(8,128)S(1)}, u32[]{:S(2)}, u32[]{:S(2)}) collective-permute-start(f32[8,128]{1,0:T(8,128)S(1)} %get-tuple-element.94), channel_id=1, source_target_pairs={{0,1},{1,0},{2,3},{3,2},{4,5},{5,4},{6,7},{7,6},{8,9},{9,8},{10,11... | collective-permute-start | bytes 12296 | tf_op jit(solution)/shard_map/ppermute | solution.py:643
  42.1 1.3 collective-permute-start.9
  44.1 2.3 %collective-permute-start.12 = (f32[8,128]{1,0:T(8,128)S(1)}, f32[8,128]{1,0:T(8,128)S(1)}, u32[]{:S(2)}, u32[]{:S(2)}) collective-permute-start(f32[8,128]{1,0:T(8,128)S(1)} %get-tuple-element.98), channel_id=1, source_target_pairs={{0,8},{8,0},{16,24},{24,16},{32,40},{40,32},{48,56},{56,48},{64,72... | collective-permute-start | bytes 12296 | tf_op jit(solution)/shard_map/ppermute | solution.py:643
  47.2 1.4 third0.1
  48.6 11.0 %all-to-all-start.1 = ((f32[256,1,128]{2,1,0:T(1,128)}), f32[256,1,128]{2,1,0:T(1,128)S(1)}, u32[]{:S(2)}, u32[]{:S(2)}) async-start(f32[256,1,128]{2,1,0:T(1,128)} %bitcast.13), calls=%async_computation.1 | async-start | bytes 262144 | tf_op jit(solution)/shard_map/all_to_all | solution.py:757
  59.5 1.5 %collective-permute-start.15 = (f32[1,256]{1,0:T(1,128)S(1)}, f32[1,256]{1,0:T(1,128)S(1)}, u32[]{:S(2)}, u32[]{:S(2)}) collective-permute-start(f32[1,256]{1,0:T(1,128)S(1)} %get-tuple-element.101.r0), channel_id=1, source_target_pairs={{0,2},{2,0},{4,6},{6,4},{1,3},{3,1},{5,7},{7,5},{8,10},{10,8},{12,... | collective-permute-start | bytes 3080 | tf_op jit(solution)/shard_map/ppermute | solution.py:647
  61.0 1.8 %collective-permute-start.14 = (f32[1,256]{1,0:T(1,128)S(1)}, f32[1,256]{1,0:T(1,128)S(1)}, u32[]{:S(2)}, u32[]{:S(2)}) collective-permute-start(f32[1,256]{1,0:T(1,128)S(1)} %get-tuple-element.101.r0), channel_id=1, source_target_pairs={{0,6},{2,4},{4,2},{6,0},{1,7},{3,5},{5,3},{7,1},{8,14},{10,12},{12... | collective-permute-start | bytes 3080 | tf_op jit(solution)/shard_map/ppermute | solution.py:647
  64.6 2.1 %collective-permute-done.13.r1 = f32[1,256]{1,0:T(1,128)S(1)} collective-permute-done((f32[1,256]{1,0:T(1,128)S(1)}, f32[1,256]{1,0:T(1,128)S(1)}, u32[]{:S(2)}, u32[]{:S(2)}) %collective-permute-start.13) | collective-permute-done | bytes 1056 | tf_op jit(solution)/shard_map/ppermute | solution.py:647
  67.1 5.4 %all-to-all-done.1 = f32[256,1,128]{2,1,0:T(1,128)S(1)} async-done(((f32[256,1,128]{2,1,0:T(1,128)}), f32[256,1,128]{2,1,0:T(1,128)S(1)}, u32[]{:S(2)}, u32[]{:S(2)}) %all-to-all-start.1) | async-done | bytes 131104 | tf_op jit(solution)/shard_map/all_to_all | solution.py:757
  74.1 1.9 %collective-permute-start.17 = (f32[8,128]{1,0:T(8,128)S(1)}, f32[8,128]{1,0:T(8,128)S(1)}, u32[]{:S(2)}, u32[]{:S(2)}) collective-permute-start(f32[8,128]{1,0:T(8,128)S(1)} %get-tuple-element.107), channel_id=1, source_target_pairs={{0,248},{8,16},{16,8},{24,32},{32,24},{40,48},{48,40},{56,64},{64,... | collective-permute-start | bytes 12296 | tf_op jit(solution)/shard_map/ppermute | solution.py:643
  78.6 1.5 %collective-permute-done.19.refs_7_ = f32[8,128]{1,0:T(8,128)S(1)} collective-permute-done((f32[8,128]{1,0:T(8,128)S(1)}, f32[8,128]{1,0:T(8,128)S(1)}, u32[]{:S(2)}, u32[]{:S(2)}) %collective-permute-start.19) | collective-permute-done | bytes 4128 | tf_op jit(solution)/shard_map/ppermute | solution.py:643
  81.3 1.6 %collective-permute-start.21 = (f32[8,128]{1,0:T(8,128)S(1)}, f32[8,128]{1,0:T(8,128)S(1)}, u32[]{:S(2)}, u32[]{:S(2)}) collective-permute-start(f32[8,128]{1,0:T(8,128)S(1)} %get-tuple-element.113), channel_id=1, source_target_pairs={{0,1},{1,0},{2,3},{3,2},{4,5},{5,4},{6,7},{7,6},{8,9},{9,8},{10,11... | collective-permute-start | bytes 12296 | tf_op jit(solution)/shard_map/ppermute | solution.py:643
  83.0 2.2 %collective-permute-start.22 = (f32[8,128]{1,0:T(8,128)S(1)}, f32[8,128]{1,0:T(8,128)S(1)}, u32[]{:S(2)}, u32[]{:S(2)}) collective-permute-start(f32[8,128]{1,0:T(8,128)S(1)} %get-tuple-element.114), channel_id=1, source_target_pairs={{0,248},{8,16},{16,8},{24,32},{32,24},{40,48},{48,40},{56,64},{64,... | collective-permute-start | bytes 12296 | tf_op jit(solution)/shard_map/ppermute | solution.py:643
  85.8 1.3 collective-permute-start.25
  91.2 1.7 %collective-permute-start.26 = (f32[1,256]{1,0:T(1,128)S(1)}, f32[1,256]{1,0:T(1,128)S(1)}, u32[]{:S(2)}, u32[]{:S(2)}) collective-permute-start(f32[1,256]{1,0:T(1,128)S(1)} %get-tuple-element.119.r0), channel_id=1, source_target_pairs={{0,4},{2,6},{4,0},{6,2},{1,5},{3,7},{5,1},{7,3},{8,12},{10,14},{12... | collective-permute-start | bytes 3080 | tf_op jit(solution)/shard_map/ppermute | solution.py:647
  93.8 1.3 collective-permute-done.26.r1
  95.8 3.0 %collective-permute-start.29 = (f32[8,128]{1,0:T(8,128)S(1)}, f32[8,128]{1,0:T(8,128)S(1)}, u32[]{:S(2)}, u32[]{:S(2)}) collective-permute-start(f32[8,128]{1,0:T(8,128)S(1)} %get-tuple-element.122), channel_id=1, source_target_pairs={{0,1},{1,0},{2,3},{3,2},{4,5},{5,4},{6,7},{7,6},{8,9},{9,8},{10,11... | collective-permute-start | bytes 12296 | tf_op jit(solution)/shard_map/ppermute | solution.py:643
  100.6 2.0 %collective-permute-start.32 = (f32[8,128]{1,0:T(8,128)S(1)}, f32[8,128]{1,0:T(8,128)S(1)}, u32[]{:S(2)}, u32[]{:S(2)}) collective-permute-start(f32[8,128]{1,0:T(8,128)S(1)} %get-tuple-element.125), channel_id=1, source_target_pairs={{0,6},{2,4},{4,2},{6,0},{1,7},{3,5},{5,3},{7,1},{8,14},{10,12},{12... | collective-permute-start | bytes 12296 | tf_op jit(solution)/shard_map/ppermute | solution.py:643
  102.6 2.3 %collective-permute-start.33 = (f32[8,128]{1,0:T(8,128)S(1)}, f32[8,128]{1,0:T(8,128)S(1)}, u32[]{:S(2)}, u32[]{:S(2)}) collective-permute-start(f32[8,128]{1,0:T(8,128)S(1)} %get-tuple-element.126), channel_id=1, source_target_pairs={{0,8},{8,0},{16,24},{24,16},{32,40},{40,32},{48,56},{56,48},{64,72... | collective-permute-start | bytes 12296 | tf_op jit(solution)/shard_map/ppermute | solution.py:643
  105.7 1.2 second2.1
  107.8 1.4 %collective-permute-start.35 = (f32[8,128]{1,0:T(8,128)S(1)}, f32[8,128]{1,0:T(8,128)S(1)}, u32[]{:S(2)}, u32[]{:S(2)}) collective-permute-start(f32[8,128]{1,0:T(8,128)S(1)} %get-tuple-element.130), channel_id=1, source_target_pairs={{0,248},{8,16},{16,8},{24,32},{32,24},{40,48},{48,40},{56,64},{64,... | collective-permute-start | bytes 12296 | tf_op jit(solution)/shard_map/ppermute | solution.py:643
  109.3 1.7 %collective-permute-start.37 = (f32[8,128]{1,0:T(8,128)S(1)}, f32[8,128]{1,0:T(8,128)S(1)}, u32[]{:S(2)}, u32[]{:S(2)}) collective-permute-start(f32[8,128]{1,0:T(8,128)S(1)} %get-tuple-element.132), channel_id=1, source_target_pairs={{0,6},{2,4},{4,2},{6,0},{1,7},{3,5},{5,3},{7,1},{8,14},{10,12},{12... | collective-permute-start | bytes 12296 | tf_op jit(solution)/shard_map/ppermute | solution.py:643
  111.0 2.6 %collective-permute-start.38 = (f32[8,128]{1,0:T(8,128)S(1)}, f32[8,128]{1,0:T(8,128)S(1)}, u32[]{:S(2)}, u32[]{:S(2)}) collective-permute-start(f32[8,128]{1,0:T(8,128)S(1)} %get-tuple-element.133), channel_id=1, source_target_pairs={{0,8},{8,0},{16,24},{24,16},{32,40},{40,32},{48,56},{56,48},{64,72... | collective-permute-start | bytes 12296 | tf_op jit(solution)/shard_map/ppermute | solution.py:643
  115.1 22.7 %all_to_all.33 = f32[256,1,128]{2,1,0:T(1,128)S(1)} all-to-all(f32[256,1,128]{2,1,0:T(1,128)S(1)} %bitcast.25), channel_id=1, replica_groups=mesh['passage'=32,'span'=4,'radial'=2] {'passage','span','radial'}, dimensions={0} | all-to-all | bytes 262144 | tf_op jit(solution)/shard_map/all_to_all | solution.py:764
  137.7 1.4 %final.1 = (f32[4,320]{1,0:T(4,128)}, f32[4,320]{1,0:T(4,128)}) custom-call(f32[256,128]{1,0:T(8,128)S(1)} %bitcast.22, f32[8,128]{1,0:T(8,128)S(1)} %get-tuple-element.135.scal0, f32[8,128]{1,0:T(8,128)S(1)} %get-tuple-element.136.scal1, f32[32,64]{1,0:T(8,128)S(1)} %get-tuple-element.71.x, f32[32,64]{1,0:T(8,128)S(1)} %get-tuple-element.92.x.s0, ...), custom_call_target="tpu_custom_call" | custom-call | tf_op jit(solution)/shard_map/final/pallas_call | solution.py:582
  (107 shorter events, 31.1 us)
Async XLA Ops:
  2.2 28.7 %all-to-all-start = ((f32[256,1,128]{2,1,0:T(1,128)}), f32[256,1,128]{2,1,0:T(1,128)S(1)}, u32[]{:S(2)}, u32[]{:S(2)}) async-start(f32[256,1,128]{2,1,0:T(1,128)} %bitcast.7), calls=%async_computation | async-start | bytes 262144 | tf_op jit(solution)/shard_map/all_to_all | solution.py:659
  19.2 7.3 %collective-permute-start.2 = (f32[1,256]{1,0:T(1,128)S(1)}, f32[1,256]{1,0:T(1,128)S(1)}, u32[]{:S(2)}, u32[]{:S(2)}) collective-permute-start(f32[1,256]{1,0:T(1,128)S(1)} %get-tuple-element.72.r0), channel_id=1, source_target_pairs={{0,2},{2,0},{4,6},{6,4},{1,3},{3,1},{5,7},{7,5},{8,10},{10,8},{12,... | collective-permute-start | bytes 3080 | tf_op jit(solution)/shard_map/ppermute | solution.py:647
  20.6 5.8 %collective-permute-start.1 = (f32[1,256]{1,0:T(1,128)S(1)}, f32[1,256]{1,0:T(1,128)S(1)}, u32[]{:S(2)}, u32[]{:S(2)}) collective-permute-start(f32[1,256]{1,0:T(1,128)S(1)} %get-tuple-element.72.r0), channel_id=1, source_target_pairs={{0,6},{2,4},{4,2},{6,0},{1,7},{3,5},{5,3},{7,1},{8,14},{10,12},{12... | collective-permute-start | bytes 3080 | tf_op jit(solution)/shard_map/ppermute | solution.py:647
  22.4 4.0 %collective-permute-start = (f32[1,256]{1,0:T(1,128)S(1)}, f32[1,256]{1,0:T(1,128)S(1)}, u32[]{:S(2)}, u32[]{:S(2)}) collective-permute-start(f32[1,256]{1,0:T(1,128)S(1)} %get-tuple-element.72.r0), channel_id=1, source_target_pairs={{0,4},{2,6},{4,0},{6,2},{1,5},{3,7},{5,1},{7,3},{8,12},{10,14},{12... | collective-permute-start | bytes 3080 | tf_op jit(solution)/shard_map/ppermute | solution.py:647
  31.6 7.1 %collective-permute-start.3 = (f32[8,128]{1,0:T(8,128)S(1)}, f32[8,128]{1,0:T(8,128)S(1)}, u32[]{:S(2)}, u32[]{:S(2)}) collective-permute-start(f32[8,128]{1,0:T(8,128)S(1)} %get-tuple-element.84), channel_id=1, source_target_pairs={{0,1},{1,0},{2,3},{3,2},{4,5},{5,4},{6,7},{7,6},{8,9},{9,8},{10,11... | collective-permute-start | bytes 12296 | tf_op jit(solution)/shard_map/ppermute | solution.py:643
  32.4 6.4 %collective-permute-start.4 = (f32[8,128]{1,0:T(8,128)S(1)}, f32[8,128]{1,0:T(8,128)S(1)}, u32[]{:S(2)}, u32[]{:S(2)}) collective-permute-start(f32[8,128]{1,0:T(8,128)S(1)} %get-tuple-element.85), channel_id=1, source_target_pairs={{0,248},{8,16},{16,8},{24,32},{32,24},{40,48},{48,40},{56,64},{64,... | collective-permute-start | bytes 12296 | tf_op jit(solution)/shard_map/ppermute | solution.py:643
  34.3 4.5 %collective-permute-start.5 = (f32[8,128]{1,0:T(8,128)S(1)}, f32[8,128]{1,0:T(8,128)S(1)}, u32[]{:S(2)}, u32[]{:S(2)}) collective-permute-start(f32[8,128]{1,0:T(8,128)S(1)} %get-tuple-element.86), channel_id=1, source_target_pairs={{0,2},{2,0},{4,6},{6,4},{1,3},{3,1},{5,7},{7,5},{8,10},{10,8},{12,... | collective-permute-start | bytes 12296 | tf_op jit(solution)/shard_map/ppermute | solution.py:643
  34.6 4.2 %collective-permute-start.6 = (f32[8,128]{1,0:T(8,128)S(1)}, f32[8,128]{1,0:T(8,128)S(1)}, u32[]{:S(2)}, u32[]{:S(2)}) collective-permute-start(f32[8,128]{1,0:T(8,128)S(1)} %get-tuple-element.87), channel_id=1, source_target_pairs={{0,6},{2,4},{4,2},{6,0},{1,7},{3,5},{5,3},{7,1},{8,14},{10,12},{12... | collective-permute-start | bytes 12296 | tf_op jit(solution)/shard_map/ppermute | solution.py:643
  40.3 6.6 %collective-permute-start.8 = (f32[8,128]{1,0:T(8,128)S(1)}, f32[8,128]{1,0:T(8,128)S(1)}, u32[]{:S(2)}, u32[]{:S(2)}) collective-permute-start(f32[8,128]{1,0:T(8,128)S(1)} %get-tuple-element.94), channel_id=1, source_target_pairs={{0,1},{1,0},{2,3},{3,2},{4,5},{5,4},{6,7},{7,6},{8,9},{9,8},{10,11... | collective-permute-start | bytes 12296 | tf_op jit(solution)/shard_map/ppermute | solution.py:643
  42.1 4.8 %collective-permute-start.9 = (f32[8,128]{1,0:T(8,128)S(1)}, f32[8,128]{1,0:T(8,128)S(1)}, u32[]{:S(2)}, u32[]{:S(2)}) collective-permute-start(f32[8,128]{1,0:T(8,128)S(1)} %get-tuple-element.95), channel_id=1, source_target_pairs={{0,248},{8,16},{16,8},{24,32},{32,24},{40,48},{48,40},{56,64},{64,... | collective-permute-start | bytes 12296 | tf_op jit(solution)/shard_map/ppermute | solution.py:643
  43.4 3.5 %collective-permute-start.10 = (f32[8,128]{1,0:T(8,128)S(1)}, f32[8,128]{1,0:T(8,128)S(1)}, u32[]{:S(2)}, u32[]{:S(2)}) collective-permute-start(f32[8,128]{1,0:T(8,128)S(1)} %get-tuple-element.96), channel_id=1, source_target_pairs={{0,2},{2,0},{4,6},{6,4},{1,3},{3,1},{5,7},{7,5},{8,10},{10,8},{12,... | collective-permute-start | bytes 12296 | tf_op jit(solution)/shard_map/ppermute | solution.py:643
  43.4 3.7 %collective-permute-start.11 = (f32[8,128]{1,0:T(8,128)S(1)}, f32[8,128]{1,0:T(8,128)S(1)}, u32[]{:S(2)}, u32[]{:S(2)}) collective-permute-start(f32[8,128]{1,0:T(8,128)S(1)} %get-tuple-element.97), channel_id=1, source_target_pairs={{0,6},{2,4},{4,2},{6,0},{1,7},{3,5},{5,3},{7,1},{8,14},{10,12},{12... | collective-permute-start | bytes 12296 | tf_op jit(solution)/shard_map/ppermute | solution.py:643
  48.6 23.9 %all-to-all-start.1 = ((f32[256,1,128]{2,1,0:T(1,128)}), f32[256,1,128]{2,1,0:T(1,128)S(1)}, u32[]{:S(2)}, u32[]{:S(2)}) async-start(f32[256,1,128]{2,1,0:T(1,128)} %bitcast.13), calls=%async_computation.1 | async-start | bytes 262144 | tf_op jit(solution)/shard_map/all_to_all | solution.py:757
  59.5 3.9 %collective-permute-start.15 = (f32[1,256]{1,0:T(1,128)S(1)}, f32[1,256]{1,0:T(1,128)S(1)}, u32[]{:S(2)}, u32[]{:S(2)}) collective-permute-start(f32[1,256]{1,0:T(1,128)S(1)} %get-tuple-element.101.r0), channel_id=1, source_target_pairs={{0,2},{2,0},{4,6},{6,4},{1,3},{3,1},{5,7},{7,5},{8,10},{10,8},{12,... | collective-permute-start | bytes 3080 | tf_op jit(solution)/shard_map/ppermute | solution.py:647
  61.0 3.6 %collective-permute-start.14 = (f32[1,256]{1,0:T(1,128)S(1)}, f32[1,256]{1,0:T(1,128)S(1)}, u32[]{:S(2)}, u32[]{:S(2)}) collective-permute-start(f32[1,256]{1,0:T(1,128)S(1)} %get-tuple-element.101.r0), channel_id=1, source_target_pairs={{0,6},{2,4},{4,2},{6,0},{1,7},{3,5},{5,3},{7,1},{8,14},{10,12},{12... | collective-permute-start | bytes 3080 | tf_op jit(solution)/shard_map/ppermute | solution.py:647
  62.8 3.9 %collective-permute-start.13 = (f32[1,256]{1,0:T(1,128)S(1)}, f32[1,256]{1,0:T(1,128)S(1)}, u32[]{:S(2)}, u32[]{:S(2)}) collective-permute-start(f32[1,256]{1,0:T(1,128)S(1)} %get-tuple-element.101.r0), channel_id=1, source_target_pairs={{0,4},{2,6},{4,0},{6,2},{1,5},{3,7},{5,1},{7,3},{8,12},{10,14},{12... | collective-permute-start | bytes 3080 | tf_op jit(solution)/shard_map/ppermute | solution.py:647
  73.4 4.1 %collective-permute-start.16 = (f32[8,128]{1,0:T(8,128)S(1)}, f32[8,128]{1,0:T(8,128)S(1)}, u32[]{:S(2)}, u32[]{:S(2)}) collective-permute-start(f32[8,128]{1,0:T(8,128)S(1)} %get-tuple-element.106), channel_id=1, source_target_pairs={{0,1},{1,0},{2,3},{3,2},{4,5},{5,4},{6,7},{7,6},{8,9},{9,8},{10,11... | collective-permute-start | bytes 12296 | tf_op jit(solution)/shard_map/ppermute | solution.py:643
  76.4 3.7 %collective-permute-start.19 = (f32[8,128]{1,0:T(8,128)S(1)}, f32[8,128]{1,0:T(8,128)S(1)}, u32[]{:S(2)}, u32[]{:S(2)}) collective-permute-start(f32[8,128]{1,0:T(8,128)S(1)} %get-tuple-element.109), channel_id=1, source_target_pairs={{0,6},{2,4},{4,2},{6,0},{1,7},{3,5},{5,3},{7,1},{8,14},{10,12},{12... | collective-permute-start | bytes 12296 | tf_op jit(solution)/shard_map/ppermute | solution.py:643
  81.3 6.4 %collective-permute-start.21 = (f32[8,128]{1,0:T(8,128)S(1)}, f32[8,128]{1,0:T(8,128)S(1)}, u32[]{:S(2)}, u32[]{:S(2)}) collective-permute-start(f32[8,128]{1,0:T(8,128)S(1)} %get-tuple-element.113), channel_id=1, source_target_pairs={{0,1},{1,0},{2,3},{3,2},{4,5},{5,4},{6,7},{7,6},{8,9},{9,8},{10,11... | collective-permute-start | bytes 12296 | tf_op jit(solution)/shard_map/ppermute | solution.py:643
  83.0 4.7 %collective-permute-start.22 = (f32[8,128]{1,0:T(8,128)S(1)}, f32[8,128]{1,0:T(8,128)S(1)}, u32[]{:S(2)}, u32[]{:S(2)}) collective-permute-start(f32[8,128]{1,0:T(8,128)S(1)} %get-tuple-element.114), channel_id=1, source_target_pairs={{0,248},{8,16},{16,8},{24,32},{32,24},{40,48},{48,40},{56,64},{64,... | collective-permute-start | bytes 12296 | tf_op jit(solution)/shard_map/ppermute | solution.py:643
  85.1 3.7 %collective-permute-start.24 = (f32[8,128]{1,0:T(8,128)S(1)}, f32[8,128]{1,0:T(8,128)S(1)}, u32[]{:S(2)}, u32[]{:S(2)}) collective-permute-start(f32[8,128]{1,0:T(8,128)S(1)} %get-tuple-element.116), channel_id=1, source_target_pairs={{0,6},{2,4},{4,2},{6,0},{1,7},{3,5},{5,3},{7,1},{8,14},{10,12},{12... | collective-permute-start | bytes 12296 | tf_op jit(solution)/shard_map/ppermute | solution.py:643
  89.6 3.7 %collective-permute-start.28 = (f32[1,256]{1,0:T(1,128)S(1)}, f32[1,256]{1,0:T(1,128)S(1)}, u32[]{:S(2)}, u32[]{:S(2)}) collective-permute-start(f32[1,256]{1,0:T(1,128)S(1)} %get-tuple-element.119.r0), channel_id=1, source_target_pairs={{0,2},{2,0},{4,6},{6,4},{1,3},{3,1},{5,7},{7,5},{8,10},{10,8},{12,... | collective-permute-start | bytes 3080 | tf_op jit(solution)/shard_map/ppermute | solution.py:647
  90.2 3.6 %collective-permute-start.27 = (f32[1,256]{1,0:T(1,128)S(1)}, f32[1,256]{1,0:T(1,128)S(1)}, u32[]{:S(2)}, u32[]{:S(2)}) collective-permute-start(f32[1,256]{1,0:T(1,128)S(1)} %get-tuple-element.119.r0), channel_id=1, source_target_pairs={{0,6},{2,4},{4,2},{6,0},{1,7},{3,5},{5,3},{7,1},{8,14},{10,12},{12... | collective-permute-start | bytes 3080 | tf_op jit(solution)/shard_map/ppermute | solution.py:647
  91.2 3.9 %collective-permute-start.26 = (f32[1,256]{1,0:T(1,128)S(1)}, f32[1,256]{1,0:T(1,128)S(1)}, u32[]{:S(2)}, u32[]{:S(2)}) collective-permute-start(f32[1,256]{1,0:T(1,128)S(1)} %get-tuple-element.119.r0), channel_id=1, source_target_pairs={{0,4},{2,6},{4,0},{6,2},{1,5},{3,7},{5,1},{7,3},{8,12},{10,14},{12... | collective-permute-start | bytes 3080 | tf_op jit(solution)/shard_map/ppermute | solution.py:647
  95.8 9.7 %collective-permute-start.29 = (f32[8,128]{1,0:T(8,128)S(1)}, f32[8,128]{1,0:T(8,128)S(1)}, u32[]{:S(2)}, u32[]{:S(2)}) collective-permute-start(f32[8,128]{1,0:T(8,128)S(1)} %get-tuple-element.122), channel_id=1, source_target_pairs={{0,1},{1,0},{2,3},{3,2},{4,5},{5,4},{6,7},{7,6},{8,9},{9,8},{10,11... | collective-permute-start | bytes 12296 | tf_op jit(solution)/shard_map/ppermute | solution.py:643
  98.7 6.7 %collective-permute-start.30 = (f32[8,128]{1,0:T(8,128)S(1)}, f32[8,128]{1,0:T(8,128)S(1)}, u32[]{:S(2)}, u32[]{:S(2)}) collective-permute-start(f32[8,128]{1,0:T(8,128)S(1)} %get-tuple-element.123), channel_id=1, source_target_pairs={{0,248},{8,16},{16,8},{24,32},{32,24},{40,48},{48,40},{56,64},{64,... | collective-permute-start | bytes 12296 | tf_op jit(solution)/shard_map/ppermute | solution.py:643
  99.6 5.9 %collective-permute-start.31 = (f32[8,128]{1,0:T(8,128)S(1)}, f32[8,128]{1,0:T(8,128)S(1)}, u32[]{:S(2)}, u32[]{:S(2)}) collective-permute-start(f32[8,128]{1,0:T(8,128)S(1)} %get-tuple-element.124), channel_id=1, source_target_pairs={{0,2},{2,0},{4,6},{6,4},{1,3},{3,1},{5,7},{7,5},{8,10},{10,8},{12,... | collective-permute-start | bytes 12296 | tf_op jit(solution)/shard_map/ppermute | solution.py:643
  100.6 4.8 %collective-permute-start.32 = (f32[8,128]{1,0:T(8,128)S(1)}, f32[8,128]{1,0:T(8,128)S(1)}, u32[]{:S(2)}, u32[]{:S(2)}) collective-permute-start(f32[8,128]{1,0:T(8,128)S(1)} %get-tuple-element.125), channel_id=1, source_target_pairs={{0,6},{2,4},{4,2},{6,0},{1,7},{3,5},{5,3},{7,1},{8,14},{10,12},{12... | collective-permute-start | bytes 12296 | tf_op jit(solution)/shard_map/ppermute | solution.py:643
  106.9 7.1 %collective-permute-start.34 = (f32[8,128]{1,0:T(8,128)S(1)}, f32[8,128]{1,0:T(8,128)S(1)}, u32[]{:S(2)}, u32[]{:S(2)}) collective-permute-start(f32[8,128]{1,0:T(8,128)S(1)} %get-tuple-element.129), channel_id=1, source_target_pairs={{0,1},{1,0},{2,3},{3,2},{4,5},{5,4},{6,7},{7,6},{8,9},{9,8},{10,11... | collective-permute-start | bytes 12296 | tf_op jit(solution)/shard_map/ppermute | solution.py:643
  107.8 6.2 %collective-permute-start.35 = (f32[8,128]{1,0:T(8,128)S(1)}, f32[8,128]{1,0:T(8,128)S(1)}, u32[]{:S(2)}, u32[]{:S(2)}) collective-permute-start(f32[8,128]{1,0:T(8,128)S(1)} %get-tuple-element.130), channel_id=1, source_target_pairs={{0,248},{8,16},{16,8},{24,32},{32,24},{40,48},{48,40},{56,64},{64,... | collective-permute-start | bytes 12296 | tf_op jit(solution)/shard_map/ppermute | solution.py:643
  109.3 4.8 %collective-permute-start.36 = (f32[8,128]{1,0:T(8,128)S(1)}, f32[8,128]{1,0:T(8,128)S(1)}, u32[]{:S(2)}, u32[]{:S(2)}) collective-permute-start(f32[8,128]{1,0:T(8,128)S(1)} %get-tuple-element.131), channel_id=1, source_target_pairs={{0,2},{2,0},{4,6},{6,4},{1,3},{3,1},{5,7},{7,5},{8,10},{10,8},{12,... | collective-permute-start | bytes 12296 | tf_op jit(solution)/shard_map/ppermute | solution.py:643
  109.3 4.8 %collective-permute-start.37 = (f32[8,128]{1,0:T(8,128)S(1)}, f32[8,128]{1,0:T(8,128)S(1)}, u32[]{:S(2)}, u32[]{:S(2)}) collective-permute-start(f32[8,128]{1,0:T(8,128)S(1)} %get-tuple-element.132), channel_id=1, source_target_pairs={{0,6},{2,4},{4,2},{6,0},{1,7},{3,5},{5,3},{7,1},{8,14},{10,12},{12... | collective-permute-start | bytes 12296 | tf_op jit(solution)/shard_map/ppermute | solution.py:643
  (24 other events, 181.6 us)

commit v3 on v2

--- a/solution.py
+++ b/solution.py
@@ -201,7 +201,7 @@
 
 def read_scalars(table_ref, count):
     sums = jnp.sum(table_ref[...], axis=0, keepdims=True)
-    return [sums[:, i : i + 1] for i in range(count)]
+    return [jnp.broadcast_to(sums[:, i : i + 1], (1, 128)) for i in range(count)]
 
 
 def coarse_values(coarse, cinv_ref, member_ref, lay_ref):
@@ -424,10 +424,10 @@
 def first0_kernel(odd, table, x, coarse, blocks, rise, *outs):
     z_ref, coarse_ref, scal_ref, first_ref, grown_ref, *sends = outs
     beta = jnp.sqrt(read_scalars(table, 1)[0])
-    z = x[...] / beta
+    z = x[...] / beta[:, :NODES]
     z_ref[...] = z
     scal_ref[...] = jnp.broadcast_to(beta, scal_ref.shape)
-    scaled = coarse[...] / beta
+    scaled = coarse[...] / beta[:, :NODES]
     coarse_ref[...] = scaled
     first = apply_blocks(blocks, rounded(z)) + scaled
     finish_first(odd, first, rise, first_ref, grown_ref, sends)
@@ -437,10 +437,11 @@
     z_ref, scal_ref, first_ref, grown_ref, *sends = outs
     h00, square = read_scalars(table, 2)
     h10 = jnp.sqrt(jnp.maximum(square - h00 * h00, 1e-7 * square))
+    for i, value in enumerate((h00, h10, square)):
+        scal_ref[i * STRIDE : (i + 1) * STRIDE, :] = jnp.broadcast_to(value, (STRIDE, 128))
+    h00, h10 = h00[:, :NODES], h10[:, :NODES]
     z = (x[...] - h00 * b0[...]) / h10
     z_ref[...] = z
-    row = lax.broadcasted_iota(jnp.int32, scal_ref.shape, 0)
-    scal_ref[...] = jnp.where(row == 0, h00, jnp.where(row == 1, h10, square))
     scaled = (coarse[...] - h00 * coarse0[...]) / h10
     first = apply_blocks(blocks, rounded(z)) + scaled
     finish_first(odd, first, rise, first_ref, grown_ref, sends)
@@ -536,10 +537,9 @@
 
 
 def final_kernel(table, scal0, scal1, x, s0, s1, s2, w0, w1, w2, update_ref, residual_ref):
-    sums = jnp.sum(table[...], axis=0, keepdims=True)
-    g0, g1, g2, q0, q1, qw, qq = [sums[:, i : i + 1] for i in range(7)]
-    beta = scal0[0:1, 0:1]
-    h00, h10, square0 = [scal1[i : i + 1, 0:1] for i in range(3)]
+    g0, g1, g2, q0, q1, qw, qq = read_scalars(table, 7)
+    beta = scal0[0:1, :]
+    h00, h10, square0 = [scal1[i * STRIDE : i * STRIDE + 1, :] for i in range(3)]
     h01, h11 = g0, g1
     squared = jnp.maximum(g2 - h01 * h01 - h11 * h11, 1e-7 * g2)
     inv21 = inverse_sqrt(squared)
@@ -560,6 +560,7 @@
     y2 = y2 * inv21
     y0 = y0 - y2 * h01
     y1 = y1 - y2 * h11
+    y0, y1, y2 = (y[:, :NODES] for y in (y0, y1, y2))
     update = y0 * s0[...] + y1 * s1[...] + y2 * s2[...]
     residual = x[...] - (y0 * w0[...] + y1 * w1[...] + y2 * w2[...])
     for e in range(ELEMS):
@@ -721,7 +722,7 @@
                 first1_kernel,
                 "first1",
                 (odd, table, images[0], coarse, basis[0], coarse0) + tail,
-                [vec, (8, 128)] + outs,
+                [vec, (3 * STRIDE, 128)] + outs,
             )
             scalars.append(scal)
         else:

time: 139 us -> 139 us (level)
  no operation moved by 1% of the time
where the time goes in v3:
time: 139 us
  starting transfers between devices  75.7 us (54%)
  blocking collectives  22.7 us (16%)
  waiting for transfers between devices  19.3 us (14%)
  Pallas kernels  16.7 us (12%)
  local copies, waits for them, and re-layouts  3.03 us (2%)
    ppermute x30, starting transfers between devices, exchange(): return [lax.ppermute(x, axis, way) for x, (axis, way) in zip(sends, ways)]  37.9 us
    all_to_all x2, starting transfers between devices, body(): table = lax.all_to_all(table, AXES, 0, 0, tiled=True)  26.6 us
    all_to_all x1, blocking collectives, body(): table = lax.all_to_all(table, AXES, 0, 0, tiled=True)  22.7 us
    pallas_call x22, Pallas kernels, call(): pl.pallas_call(kernel, name=name, out_shape=[shape_of(out) for out in out...  16.7 us
    ppermute x9, starting transfers between devices, span_rows(): lax.ppermute(row, 'span', [(i, i ^ k) for i in range(n_span)])  11.2 us
    all_to_all x2, waiting for transfers between devices, body(): table = lax.all_to_all(table, AXES, 0, 0, tiled=True)  9.39 us
    ppermute x9, waiting for transfers between devices, span_rows(): lax.ppermute(row, 'span', [(i, i ^ k) for i in range(n_span)])  5.07 us
    ppermute x30, waiting for transfers between devices, exchange(): return [lax.ppermute(x, axis, way) for x, (axis, way) in zip(sends, ways)]  4.88 us
  transfers between devices with their start and end apart: 41, of which 15 were waited for; matrix products, arithmetic and copies ran while one was open for 0% of the time, Pallas kernels for 5%

profile of v3, /device:TPU:1, one launch (start us, length us, event | category | flops | bytes accessed | tf_op | source)
XLA Modules:
  0.0 138.5 jit_solution(1767838018513632379)
XLA Ops:
  2.2 15.7 %all-to-all-start = ((f32[256,1,128]{2,1,0:T(1,128)}), f32[256,1,128]{2,1,0:T(1,128)S(1)}, u32[]{:S(2)}, u32[]{:S(2)}) async-start(f32[256,1,128]{2,1,0:T(1,128)} %bitcast.7), calls=%async_computation | async-start | bytes 262144 | tf_op jit(solution)/shard_map/all_to_all | solution.py:660
  19.2 1.5 %collective-permute-start.2 = (f32[1,256]{1,0:T(1,128)S(1)}, f32[1,256]{1,0:T(1,128)S(1)}, u32[]{:S(2)}, u32[]{:S(2)}) collective-permute-start(f32[1,256]{1,0:T(1,128)S(1)} %get-tuple-element.72.r0), channel_id=1, source_target_pairs={{0,2},{2,0},{4,6},{6,4},{1,3},{3,1},{5,7},{7,5},{8,10},{10,8},{12,... | collective-permute-start | bytes 3080 | tf_op jit(solution)/shard_map/ppermute | solution.py:648
  20.6 1.8 %collective-permute-start.1 = (f32[1,256]{1,0:T(1,128)S(1)}, f32[1,256]{1,0:T(1,128)S(1)}, u32[]{:S(2)}, u32[]{:S(2)}) collective-permute-start(f32[1,256]{1,0:T(1,128)S(1)} %get-tuple-element.72.r0), channel_id=1, source_target_pairs={{0,6},{2,4},{4,2},{6,0},{1,7},{3,5},{5,3},{7,1},{8,14},{10,12},{12... | collective-permute-start | bytes 3080 | tf_op jit(solution)/shard_map/ppermute | solution.py:648
  25.1 1.4 %setup.1 = (bf16[64,384]{1,0:T(8,128)(2,1)S(1)}, bf16[64,384]{1,0:T(8,128)(2,1)S(1)}, bf16[64,192]{1,0:T(8,128)(2,1)S(1)}, bf16[64,384]{1,0:T(8,128)(2,1)S(1)}, ...) custom-call(s32[4,20]{1,0:T(4,128)S(1)} %concatenate.3.ints_ref, ...), custom_call_target="tpu_custom_call" | custom-call | tf_op jit(solution)/shard_map/setup/pallas_call | solution.py:583
  26.9 4.0 %all-to-all-done = f32[256,1,128]{2,1,0:T(1,128)S(1)} async-done(((f32[256,1,128]{2,1,0:T(1,128)}), f32[256,1,128]{2,1,0:T(1,128)S(1)}, u32[]{:S(2)}, u32[]{:S(2)}) %all-to-all-start) | async-done | bytes 131104 | tf_op jit(solution)/shard_map/all_to_all | solution.py:660
  32.4 1.9 %collective-permute-start.4 = (f32[8,128]{1,0:T(8,128)S(1)}, f32[8,128]{1,0:T(8,128)S(1)}, u32[]{:S(2)}, u32[]{:S(2)}) collective-permute-start(f32[8,128]{1,0:T(8,128)S(1)} %get-tuple-element.85), channel_id=1, source_target_pairs={{0,248},{8,16},{16,8},{24,32},{32,24},{40,48},{48,40},{56,64},{64,... | collective-permute-start | bytes 12296 | tf_op jit(solution)/shard_map/ppermute | solution.py:644
  35.8 2.4 %collective-permute-start.7 = (f32[8,128]{1,0:T(8,128)S(1)}, f32[8,128]{1,0:T(8,128)S(1)}, u32[]{:S(2)}, u32[]{:S(2)}) collective-permute-start(f32[8,128]{1,0:T(8,128)S(1)} %get-tuple-element.88), channel_id=1, source_target_pairs={{0,8},{8,0},{16,24},{24,16},{32,40},{40,32},{48,56},{56,48},{64,72... | collective-permute-start | bytes 12296 | tf_op jit(solution)/shard_map/ppermute | solution.py:644
  40.3 1.8 %collective-permute-start.8 = (f32[8,128]{1,0:T(8,128)S(1)}, f32[8,128]{1,0:T(8,128)S(1)}, u32[]{:S(2)}, u32[]{:S(2)}) collective-permute-start(f32[8,128]{1,0:T(8,128)S(1)} %get-tuple-element.94), channel_id=1, source_target_pairs={{0,1},{1,0},{2,3},{3,2},{4,5},{5,4},{6,7},{7,6},{8,9},{9,8},{10,11... | collective-permute-start | bytes 12296 | tf_op jit(solution)/shard_map/ppermute | solution.py:644
  42.1 1.3 collective-permute-start.9
  44.1 2.3 %collective-permute-start.12 = (f32[8,128]{1,0:T(8,128)S(1)}, f32[8,128]{1,0:T(8,128)S(1)}, u32[]{:S(2)}, u32[]{:S(2)}) collective-permute-start(f32[8,128]{1,0:T(8,128)S(1)} %get-tuple-element.98), channel_id=1, source_target_pairs={{0,8},{8,0},{16,24},{24,16},{32,40},{40,32},{48,56},{56,48},{64,72... | collective-permute-start | bytes 12296 | tf_op jit(solution)/shard_map/ppermute | solution.py:644
  47.2 1.4 third0.1
  48.6 11.0 %all-to-all-start.1 = ((f32[256,1,128]{2,1,0:T(1,128)}), f32[256,1,128]{2,1,0:T(1,128)S(1)}, u32[]{:S(2)}, u32[]{:S(2)}) async-start(f32[256,1,128]{2,1,0:T(1,128)} %bitcast.13), calls=%async_computation.1 | async-start | bytes 262144 | tf_op jit(solution)/shard_map/all_to_all | solution.py:758
  59.5 1.5 %collective-permute-start.15 = (f32[1,256]{1,0:T(1,128)S(1)}, f32[1,256]{1,0:T(1,128)S(1)}, u32[]{:S(2)}, u32[]{:S(2)}) collective-permute-start(f32[1,256]{1,0:T(1,128)S(1)} %get-tuple-element.101.r0), channel_id=1, source_target_pairs={{0,2},{2,0},{4,6},{6,4},{1,3},{3,1},{5,7},{7,5},{8,10},{10,8},{12,... | collective-permute-start | bytes 3080 | tf_op jit(solution)/shard_map/ppermute | solution.py:648
  61.0 1.8 %collective-permute-start.14 = (f32[1,256]{1,0:T(1,128)S(1)}, f32[1,256]{1,0:T(1,128)S(1)}, u32[]{:S(2)}, u32[]{:S(2)}) collective-permute-start(f32[1,256]{1,0:T(1,128)S(1)} %get-tuple-element.101.r0), channel_id=1, source_target_pairs={{0,6},{2,4},{4,2},{6,0},{1,7},{3,5},{5,3},{7,1},{8,14},{10,12},{12... | collective-permute-start | bytes 3080 | tf_op jit(solution)/shard_map/ppermute | solution.py:648
  64.6 2.1 %collective-permute-done.13.r1 = f32[1,256]{1,0:T(1,128)S(1)} collective-permute-done((f32[1,256]{1,0:T(1,128)S(1)}, f32[1,256]{1,0:T(1,128)S(1)}, u32[]{:S(2)}, u32[]{:S(2)}) %collective-permute-start.13) | collective-permute-done | bytes 1056 | tf_op jit(solution)/shard_map/ppermute | solution.py:648
  67.1 5.4 %all-to-all-done.1 = f32[256,1,128]{2,1,0:T(1,128)S(1)} async-done(((f32[256,1,128]{2,1,0:T(1,128)}), f32[256,1,128]{2,1,0:T(1,128)S(1)}, u32[]{:S(2)}, u32[]{:S(2)}) %all-to-all-start.1) | async-done | bytes 131104 | tf_op jit(solution)/shard_map/all_to_all | solution.py:758
  74.0 1.9 %collective-permute-start.17 = (f32[8,128]{1,0:T(8,128)S(1)}, f32[8,128]{1,0:T(8,128)S(1)}, u32[]{:S(2)}, u32[]{:S(2)}) collective-permute-start(f32[8,128]{1,0:T(8,128)S(1)} %get-tuple-element.107), channel_id=1, source_target_pairs={{0,248},{8,16},{16,8},{24,32},{32,24},{40,48},{48,40},{56,64},{64,... | collective-permute-start | bytes 12296 | tf_op jit(solution)/shard_map/ppermute | solution.py:644
  78.5 1.5 %collective-permute-done.19.refs_7_ = f32[8,128]{1,0:T(8,128)S(1)} collective-permute-done((f32[8,128]{1,0:T(8,128)S(1)}, f32[8,128]{1,0:T(8,128)S(1)}, u32[]{:S(2)}, u32[]{:S(2)}) %collective-permute-start.19) | collective-permute-done | bytes 4128 | tf_op jit(solution)/shard_map/ppermute | solution.py:644
  80.0 1.2 second1.1
  81.2 1.6 %collective-permute-start.21 = (f32[8,128]{1,0:T(8,128)S(1)}, f32[8,128]{1,0:T(8,128)S(1)}, u32[]{:S(2)}, u32[]{:S(2)}) collective-permute-start(f32[8,128]{1,0:T(8,128)S(1)} %get-tuple-element.113), channel_id=1, source_target_pairs={{0,1},{1,0},{2,3},{3,2},{4,5},{5,4},{6,7},{7,6},{8,9},{9,8},{10,11... | collective-permute-start | bytes 12296 | tf_op jit(solution)/shard_map/ppermute | solution.py:644
  82.9 2.2 %collective-permute-start.22 = (f32[8,128]{1,0:T(8,128)S(1)}, f32[8,128]{1,0:T(8,128)S(1)}, u32[]{:S(2)}, u32[]{:S(2)}) collective-permute-start(f32[8,128]{1,0:T(8,128)S(1)} %get-tuple-element.114), channel_id=1, source_target_pairs={{0,248},{8,16},{16,8},{24,32},{32,24},{40,48},{48,40},{56,64},{64,... | collective-permute-start | bytes 12296 | tf_op jit(solution)/shard_map/ppermute | solution.py:644
  85.7 1.3 collective-permute-start.25
  91.1 1.7 %collective-permute-start.26 = (f32[1,256]{1,0:T(1,128)S(1)}, f32[1,256]{1,0:T(1,128)S(1)}, u32[]{:S(2)}, u32[]{:S(2)}) collective-permute-start(f32[1,256]{1,0:T(1,128)S(1)} %get-tuple-element.119.r0), channel_id=1, source_target_pairs={{0,4},{2,6},{4,0},{6,2},{1,5},{3,7},{5,1},{7,3},{8,12},{10,14},{12... | collective-permute-start | bytes 3080 | tf_op jit(solution)/shard_map/ppermute | solution.py:648
  93.7 1.3 collective-permute-done.26.r1
  95.7 3.0 %collective-permute-start.29 = (f32[8,128]{1,0:T(8,128)S(1)}, f32[8,128]{1,0:T(8,128)S(1)}, u32[]{:S(2)}, u32[]{:S(2)}) collective-permute-start(f32[8,128]{1,0:T(8,128)S(1)} %get-tuple-element.122), channel_id=1, source_target_pairs={{0,1},{1,0},{2,3},{3,2},{4,5},{5,4},{6,7},{7,6},{8,9},{9,8},{10,11... | collective-permute-start | bytes 12296 | tf_op jit(solution)/shard_map/ppermute | solution.py:644
  100.5 2.0 %collective-permute-start.32 = (f32[8,128]{1,0:T(8,128)S(1)}, f32[8,128]{1,0:T(8,128)S(1)}, u32[]{:S(2)}, u32[]{:S(2)}) collective-permute-start(f32[8,128]{1,0:T(8,128)S(1)} %get-tuple-element.125), channel_id=1, source_target_pairs={{0,6},{2,4},{4,2},{6,0},{1,7},{3,5},{5,3},{7,1},{8,14},{10,12},{12... | collective-permute-start | bytes 12296 | tf_op jit(solution)/shard_map/ppermute | solution.py:644
  102.5 2.3 %collective-permute-start.33 = (f32[8,128]{1,0:T(8,128)S(1)}, f32[8,128]{1,0:T(8,128)S(1)}, u32[]{:S(2)}, u32[]{:S(2)}) collective-permute-start(f32[8,128]{1,0:T(8,128)S(1)} %get-tuple-element.126), channel_id=1, source_target_pairs={{0,8},{8,0},{16,24},{24,16},{32,40},{40,32},{48,56},{56,48},{64,72... | collective-permute-start | bytes 12296 | tf_op jit(solution)/shard_map/ppermute | solution.py:644
  105.6 1.2 second2.1
  107.7 1.4 %collective-permute-start.35 = (f32[8,128]{1,0:T(8,128)S(1)}, f32[8,128]{1,0:T(8,128)S(1)}, u32[]{:S(2)}, u32[]{:S(2)}) collective-permute-start(f32[8,128]{1,0:T(8,128)S(1)} %get-tuple-element.130), channel_id=1, source_target_pairs={{0,248},{8,16},{16,8},{24,32},{32,24},{40,48},{48,40},{56,64},{64,... | collective-permute-start | bytes 12296 | tf_op jit(solution)/shard_map/ppermute | solution.py:644
  109.2 1.7 %collective-permute-start.37 = (f32[8,128]{1,0:T(8,128)S(1)}, f32[8,128]{1,0:T(8,128)S(1)}, u32[]{:S(2)}, u32[]{:S(2)}) collective-permute-start(f32[8,128]{1,0:T(8,128)S(1)} %get-tuple-element.132), channel_id=1, source_target_pairs={{0,6},{2,4},{4,2},{6,0},{1,7},{3,5},{5,3},{7,1},{8,14},{10,12},{12... | collective-permute-start | bytes 12296 | tf_op jit(solution)/shard_map/ppermute | solution.py:644
  110.9 2.6 %collective-permute-start.38 = (f32[8,128]{1,0:T(8,128)S(1)}, f32[8,128]{1,0:T(8,128)S(1)}, u32[]{:S(2)}, u32[]{:S(2)}) collective-permute-start(f32[8,128]{1,0:T(8,128)S(1)} %get-tuple-element.133), channel_id=1, source_target_pairs={{0,8},{8,0},{16,24},{24,16},{32,40},{40,32},{48,56},{56,48},{64,72... | collective-permute-start | bytes 12296 | tf_op jit(solution)/shard_map/ppermute | solution.py:644
  115.0 22.7 %all_to_all.33 = f32[256,1,128]{2,1,0:T(1,128)S(1)} all-to-all(f32[256,1,128]{2,1,0:T(1,128)S(1)} %bitcast.25), channel_id=1, replica_groups=mesh['passage'=32,'span'=4,'radial'=2] {'passage','span','radial'}, dimensions={0} | all-to-all | bytes 262144 | tf_op jit(solution)/shard_map/all_to_all | solution.py:765
  (107 shorter events, 30.7 us)
Async XLA Ops:
  2.2 28.7 %all-to-all-start = ((f32[256,1,128]{2,1,0:T(1,128)}), f32[256,1,128]{2,1,0:T(1,128)S(1)}, u32[]{:S(2)}, u32[]{:S(2)}) async-start(f32[256,1,128]{2,1,0:T(1,128)} %bitcast.7), calls=%async_computation | async-start | bytes 262144 | tf_op jit(solution)/shard_map/all_to_all | solution.py:660
  19.2 7.3 %collective-permute-start.2 = (f32[1,256]{1,0:T(1,128)S(1)}, f32[1,256]{1,0:T(1,128)S(1)}, u32[]{:S(2)}, u32[]{:S(2)}) collective-permute-start(f32[1,256]{1,0:T(1,128)S(1)} %get-tuple-element.72.r0), channel_id=1, source_target_pairs={{0,2},{2,0},{4,6},{6,4},{1,3},{3,1},{5,7},{7,5},{8,10},{10,8},{12,... | collective-permute-start | bytes 3080 | tf_op jit(solution)/shard_map/ppermute | solution.py:648
  20.6 5.8 %collective-permute-start.1 = (f32[1,256]{1,0:T(1,128)S(1)}, f32[1,256]{1,0:T(1,128)S(1)}, u32[]{:S(2)}, u32[]{:S(2)}) collective-permute-start(f32[1,256]{1,0:T(1,128)S(1)} %get-tuple-element.72.r0), channel_id=1, source_target_pairs={{0,6},{2,4},{4,2},{6,0},{1,7},{3,5},{5,3},{7,1},{8,14},{10,12},{12... | collective-permute-start | bytes 3080 | tf_op jit(solution)/shard_map/ppermute | solution.py:648
  22.4 4.0 %collective-permute-start = (f32[1,256]{1,0:T(1,128)S(1)}, f32[1,256]{1,0:T(1,128)S(1)}, u32[]{:S(2)}, u32[]{:S(2)}) collective-permute-start(f32[1,256]{1,0:T(1,128)S(1)} %get-tuple-element.72.r0), channel_id=1, source_target_pairs={{0,4},{2,6},{4,0},{6,2},{1,5},{3,7},{5,1},{7,3},{8,12},{10,14},{12... | collective-permute-start | bytes 3080 | tf_op jit(solution)/shard_map/ppermute | solution.py:648
  31.6 7.1 %collective-permute-start.3 = (f32[8,128]{1,0:T(8,128)S(1)}, f32[8,128]{1,0:T(8,128)S(1)}, u32[]{:S(2)}, u32[]{:S(2)}) collective-permute-start(f32[8,128]{1,0:T(8,128)S(1)} %get-tuple-element.84), channel_id=1, source_target_pairs={{0,1},{1,0},{2,3},{3,2},{4,5},{5,4},{6,7},{7,6},{8,9},{9,8},{10,11... | collective-permute-start | bytes 12296 | tf_op jit(solution)/shard_map/ppermute | solution.py:644
  32.4 6.4 %collective-permute-start.4 = (f32[8,128]{1,0:T(8,128)S(1)}, f32[8,128]{1,0:T(8,128)S(1)}, u32[]{:S(2)}, u32[]{:S(2)}) collective-permute-start(f32[8,128]{1,0:T(8,128)S(1)} %get-tuple-element.85), channel_id=1, source_target_pairs={{0,248},{8,16},{16,8},{24,32},{32,24},{40,48},{48,40},{56,64},{64,... | collective-permute-start | bytes 12296 | tf_op jit(solution)/shard_map/ppermute | solution.py:644
  34.3 4.5 %collective-permute-start.5 = (f32[8,128]{1,0:T(8,128)S(1)}, f32[8,128]{1,0:T(8,128)S(1)}, u32[]{:S(2)}, u32[]{:S(2)}) collective-permute-start(f32[8,128]{1,0:T(8,128)S(1)} %get-tuple-element.86), channel_id=1, source_target_pairs={{0,2},{2,0},{4,6},{6,4},{1,3},{3,1},{5,7},{7,5},{8,10},{10,8},{12,... | collective-permute-start | bytes 12296 | tf_op jit(solution)/shard_map/ppermute | solution.py:644
  34.6 4.2 %collective-permute-start.6 = (f32[8,128]{1,0:T(8,128)S(1)}, f32[8,128]{1,0:T(8,128)S(1)}, u32[]{:S(2)}, u32[]{:S(2)}) collective-permute-start(f32[8,128]{1,0:T(8,128)S(1)} %get-tuple-element.87), channel_id=1, source_target_pairs={{0,6},{2,4},{4,2},{6,0},{1,7},{3,5},{5,3},{7,1},{8,14},{10,12},{12... | collective-permute-start | bytes 12296 | tf_op jit(solution)/shard_map/ppermute | solution.py:644
  40.3 6.6 %collective-permute-start.8 = (f32[8,128]{1,0:T(8,128)S(1)}, f32[8,128]{1,0:T(8,128)S(1)}, u32[]{:S(2)}, u32[]{:S(2)}) collective-permute-start(f32[8,128]{1,0:T(8,128)S(1)} %get-tuple-element.94), channel_id=1, source_target_pairs={{0,1},{1,0},{2,3},{3,2},{4,5},{5,4},{6,7},{7,6},{8,9},{9,8},{10,11... | collective-permute-start | bytes 12296 | tf_op jit(solution)/shard_map/ppermute | solution.py:644
  42.1 4.8 %collective-permute-start.9 = (f32[8,128]{1,0:T(8,128)S(1)}, f32[8,128]{1,0:T(8,128)S(1)}, u32[]{:S(2)}, u32[]{:S(2)}) collective-permute-start(f32[8,128]{1,0:T(8,128)S(1)} %get-tuple-element.95), channel_id=1, source_target_pairs={{0,248},{8,16},{16,8},{24,32},{32,24},{40,48},{48,40},{56,64},{64,... | collective-permute-start | bytes 12296 | tf_op jit(solution)/shard_map/ppermute | solution.py:644
  43.4 3.5 %collective-permute-start.10 = (f32[8,128]{1,0:T(8,128)S(1)}, f32[8,128]{1,0:T(8,128)S(1)}, u32[]{:S(2)}, u32[]{:S(2)}) collective-permute-start(f32[8,128]{1,0:T(8,128)S(1)} %get-tuple-element.96), channel_id=1, source_target_pairs={{0,2},{2,0},{4,6},{6,4},{1,3},{3,1},{5,7},{7,5},{8,10},{10,8},{12,... | collective-permute-start | bytes 12296 | tf_op jit(solution)/shard_map/ppermute | solution.py:644
  43.4 3.7 %collective-permute-start.11 = (f32[8,128]{1,0:T(8,128)S(1)}, f32[8,128]{1,0:T(8,128)S(1)}, u32[]{:S(2)}, u32[]{:S(2)}) collective-permute-start(f32[8,128]{1,0:T(8,128)S(1)} %get-tuple-element.97), channel_id=1, source_target_pairs={{0,6},{2,4},{4,2},{6,0},{1,7},{3,5},{5,3},{7,1},{8,14},{10,12},{12... | collective-permute-start | bytes 12296 | tf_op jit(solution)/shard_map/ppermute | solution.py:644
  48.6 23.9 %all-to-all-start.1 = ((f32[256,1,128]{2,1,0:T(1,128)}), f32[256,1,128]{2,1,0:T(1,128)S(1)}, u32[]{:S(2)}, u32[]{:S(2)}) async-start(f32[256,1,128]{2,1,0:T(1,128)} %bitcast.13), calls=%async_computation.1 | async-start | bytes 262144 | tf_op jit(solution)/shard_map/all_to_all | solution.py:758
  59.5 3.9 %collective-permute-start.15 = (f32[1,256]{1,0:T(1,128)S(1)}, f32[1,256]{1,0:T(1,128)S(1)}, u32[]{:S(2)}, u32[]{:S(2)}) collective-permute-start(f32[1,256]{1,0:T(1,128)S(1)} %get-tuple-element.101.r0), channel_id=1, source_target_pairs={{0,2},{2,0},{4,6},{6,4},{1,3},{3,1},{5,7},{7,5},{8,10},{10,8},{12,... | collective-permute-start | bytes 3080 | tf_op jit(solution)/shard_map/ppermute | solution.py:648
  61.0 3.6 %collective-permute-start.14 = (f32[1,256]{1,0:T(1,128)S(1)}, f32[1,256]{1,0:T(1,128)S(1)}, u32[]{:S(2)}, u32[]{:S(2)}) collective-permute-start(f32[1,256]{1,0:T(1,128)S(1)} %get-tuple-element.101.r0), channel_id=1, source_target_pairs={{0,6},{2,4},{4,2},{6,0},{1,7},{3,5},{5,3},{7,1},{8,14},{10,12},{12... | collective-permute-start | bytes 3080 | tf_op jit(solution)/shard_map/ppermute | solution.py:648
  62.8 3.9 %collective-permute-start.13 = (f32[1,256]{1,0:T(1,128)S(1)}, f32[1,256]{1,0:T(1,128)S(1)}, u32[]{:S(2)}, u32[]{:S(2)}) collective-permute-start(f32[1,256]{1,0:T(1,128)S(1)} %get-tuple-element.101.r0), channel_id=1, source_target_pairs={{0,4},{2,6},{4,0},{6,2},{1,5},{3,7},{5,1},{7,3},{8,12},{10,14},{12... | collective-permute-start | bytes 3080 | tf_op jit(solution)/shard_map/ppermute | solution.py:648
  73.3 4.1 %collective-permute-start.16 = (f32[8,128]{1,0:T(8,128)S(1)}, f32[8,128]{1,0:T(8,128)S(1)}, u32[]{:S(2)}, u32[]{:S(2)}) collective-permute-start(f32[8,128]{1,0:T(8,128)S(1)} %get-tuple-element.106), channel_id=1, source_target_pairs={{0,1},{1,0},{2,3},{3,2},{4,5},{5,4},{6,7},{7,6},{8,9},{9,8},{10,11... | collective-permute-start | bytes 12296 | tf_op jit(solution)/shard_map/ppermute | solution.py:644
  76.3 3.7 %collective-permute-start.19 = (f32[8,128]{1,0:T(8,128)S(1)}, f32[8,128]{1,0:T(8,128)S(1)}, u32[]{:S(2)}, u32[]{:S(2)}) collective-permute-start(f32[8,128]{1,0:T(8,128)S(1)} %get-tuple-element.109), channel_id=1, source_target_pairs={{0,6},{2,4},{4,2},{6,0},{1,7},{3,5},{5,3},{7,1},{8,14},{10,12},{12... | collective-permute-start | bytes 12296 | tf_op jit(solution)/shard_map/ppermute | solution.py:644
  81.2 6.4 %collective-permute-start.21 = (f32[8,128]{1,0:T(8,128)S(1)}, f32[8,128]{1,0:T(8,128)S(1)}, u32[]{:S(2)}, u32[]{:S(2)}) collective-permute-start(f32[8,128]{1,0:T(8,128)S(1)} %get-tuple-element.113), channel_id=1, source_target_pairs={{0,1},{1,0},{2,3},{3,2},{4,5},{5,4},{6,7},{7,6},{8,9},{9,8},{10,11... | collective-permute-start | bytes 12296 | tf_op jit(solution)/shard_map/ppermute | solution.py:644
  82.9 4.7 %collective-permute-start.22 = (f32[8,128]{1,0:T(8,128)S(1)}, f32[8,128]{1,0:T(8,128)S(1)}, u32[]{:S(2)}, u32[]{:S(2)}) collective-permute-start(f32[8,128]{1,0:T(8,128)S(1)} %get-tuple-element.114), channel_id=1, source_target_pairs={{0,248},{8,16},{16,8},{24,32},{32,24},{40,48},{48,40},{56,64},{64,... | collective-permute-start | bytes 12296 | tf_op jit(solution)/shard_map/ppermute | solution.py:644
  85.0 3.7 %collective-permute-start.24 = (f32[8,128]{1,0:T(8,128)S(1)}, f32[8,128]{1,0:T(8,128)S(1)}, u32[]{:S(2)}, u32[]{:S(2)}) collective-permute-start(f32[8,128]{1,0:T(8,128)S(1)} %get-tuple-element.116), channel_id=1, source_target_pairs={{0,6},{2,4},{4,2},{6,0},{1,7},{3,5},{5,3},{7,1},{8,14},{10,12},{12... | collective-permute-start | bytes 12296 | tf_op jit(solution)/shard_map/ppermute | solution.py:644
  89.5 3.7 %collective-permute-start.28 = (f32[1,256]{1,0:T(1,128)S(1)}, f32[1,256]{1,0:T(1,128)S(1)}, u32[]{:S(2)}, u32[]{:S(2)}) collective-permute-start(f32[1,256]{1,0:T(1,128)S(1)} %get-tuple-element.119.r0), channel_id=1, source_target_pairs={{0,2},{2,0},{4,6},{6,4},{1,3},{3,1},{5,7},{7,5},{8,10},{10,8},{12,... | collective-permute-start | bytes 3080 | tf_op jit(solution)/shard_map/ppermute | solution.py:648
  90.1 3.6 %collective-permute-start.27 = (f32[1,256]{1,0:T(1,128)S(1)}, f32[1,256]{1,0:T(1,128)S(1)}, u32[]{:S(2)}, u32[]{:S(2)}) collective-permute-start(f32[1,256]{1,0:T(1,128)S(1)} %get-tuple-element.119.r0), channel_id=1, source_target_pairs={{0,6},{2,4},{4,2},{6,0},{1,7},{3,5},{5,3},{7,1},{8,14},{10,12},{12... | collective-permute-start | bytes 3080 | tf_op jit(solution)/shard_map/ppermute | solution.py:648
  91.1 3.9 %collective-permute-start.26 = (f32[1,256]{1,0:T(1,128)S(1)}, f32[1,256]{1,0:T(1,128)S(1)}, u32[]{:S(2)}, u32[]{:S(2)}) collective-permute-start(f32[1,256]{1,0:T(1,128)S(1)} %get-tuple-element.119.r0), channel_id=1, source_target_pairs={{0,4},{2,6},{4,0},{6,2},{1,5},{3,7},{5,1},{7,3},{8,12},{10,14},{12... | collective-permute-start | bytes 3080 | tf_op jit(solution)/shard_map/ppermute | solution.py:648
  95.7 9.7 %collective-permute-start.29 = (f32[8,128]{1,0:T(8,128)S(1)}, f32[8,128]{1,0:T(8,128)S(1)}, u32[]{:S(2)}, u32[]{:S(2)}) collective-permute-start(f32[8,128]{1,0:T(8,128)S(1)} %get-tuple-element.122), channel_id=1, source_target_pairs={{0,1},{1,0},{2,3},{3,2},{4,5},{5,4},{6,7},{7,6},{8,9},{9,8},{10,11... | collective-permute-start | bytes 12296 | tf_op jit(solution)/shard_map/ppermute | solution.py:644
  98.6 6.7 %collective-permute-start.30 = (f32[8,128]{1,0:T(8,128)S(1)}, f32[8,128]{1,0:T(8,128)S(1)}, u32[]{:S(2)}, u32[]{:S(2)}) collective-permute-start(f32[8,128]{1,0:T(8,128)S(1)} %get-tuple-element.123), channel_id=1, source_target_pairs={{0,248},{8,16},{16,8},{24,32},{32,24},{40,48},{48,40},{56,64},{64,... | collective-permute-start | bytes 12296 | tf_op jit(solution)/shard_map/ppermute | solution.py:644
  99.5 5.9 %collective-permute-start.31 = (f32[8,128]{1,0:T(8,128)S(1)}, f32[8,128]{1,0:T(8,128)S(1)}, u32[]{:S(2)}, u32[]{:S(2)}) collective-permute-start(f32[8,128]{1,0:T(8,128)S(1)} %get-tuple-element.124), channel_id=1, source_target_pairs={{0,2},{2,0},{4,6},{6,4},{1,3},{3,1},{5,7},{7,5},{8,10},{10,8},{12,... | collective-permute-start | bytes 12296 | tf_op jit(solution)/shard_map/ppermute | solution.py:644
  100.5 4.8 %collective-permute-start.32 = (f32[8,128]{1,0:T(8,128)S(1)}, f32[8,128]{1,0:T(8,128)S(1)}, u32[]{:S(2)}, u32[]{:S(2)}) collective-permute-start(f32[8,128]{1,0:T(8,128)S(1)} %get-tuple-element.125), channel_id=1, source_target_pairs={{0,6},{2,4},{4,2},{6,0},{1,7},{3,5},{5,3},{7,1},{8,14},{10,12},{12... | collective-permute-start | bytes 12296 | tf_op jit(solution)/shard_map/ppermute | solution.py:644
  106.8 7.1 %collective-permute-start.34 = (f32[8,128]{1,0:T(8,128)S(1)}, f32[8,128]{1,0:T(8,128)S(1)}, u32[]{:S(2)}, u32[]{:S(2)}) collective-permute-start(f32[8,128]{1,0:T(8,128)S(1)} %get-tuple-element.129), channel_id=1, source_target_pairs={{0,1},{1,0},{2,3},{3,2},{4,5},{5,4},{6,7},{7,6},{8,9},{9,8},{10,11... | collective-permute-start | bytes 12296 | tf_op jit(solution)/shard_map/ppermute | solution.py:644
  107.7 6.2 %collective-permute-start.35 = (f32[8,128]{1,0:T(8,128)S(1)}, f32[8,128]{1,0:T(8,128)S(1)}, u32[]{:S(2)}, u32[]{:S(2)}) collective-permute-start(f32[8,128]{1,0:T(8,128)S(1)} %get-tuple-element.130), channel_id=1, source_target_pairs={{0,248},{8,16},{16,8},{24,32},{32,24},{40,48},{48,40},{56,64},{64,... | collective-permute-start | bytes 12296 | tf_op jit(solution)/shard_map/ppermute | solution.py:644
  109.2 4.8 %collective-permute-start.36 = (f32[8,128]{1,0:T(8,128)S(1)}, f32[8,128]{1,0:T(8,128)S(1)}, u32[]{:S(2)}, u32[]{:S(2)}) collective-permute-start(f32[8,128]{1,0:T(8,128)S(1)} %get-tuple-element.131), channel_id=1, source_target_pairs={{0,2},{2,0},{4,6},{6,4},{1,3},{3,1},{5,7},{7,5},{8,10},{10,8},{12,... | collective-permute-start | bytes 12296 | tf_op jit(solution)/shard_map/ppermute | solution.py:644
  109.2 4.8 %collective-permute-start.37 = (f32[8,128]{1,0:T(8,128)S(1)}, f32[8,128]{1,0:T(8,128)S(1)}, u32[]{:S(2)}, u32[]{:S(2)}) collective-permute-start(f32[8,128]{1,0:T(8,128)S(1)} %get-tuple-element.132), channel_id=1, source_target_pairs={{0,6},{2,4},{4,2},{6,0},{1,7},{3,5},{5,3},{7,1},{8,14},{10,12},{12... | collective-permute-start | bytes 12296 | tf_op jit(solution)/shard_map/ppermute | solution.py:644
  (24 other events, 181.6 us)

commit v4 on v3

--- a/solution.py
+++ b/solution.py
@@ -230,11 +230,6 @@
 
 def rounded(values):
     return [values.astype(jnp.bfloat16).astype(F32)]
-
-
-def two_parts(values):
-    high = values.astype(jnp.bfloat16).astype(F32)
-    return [high, values - high]
 
 
 def face_of(grown, face):
@@ -410,10 +405,6 @@
     coarse_ref[...] = coarse_values(coarse, cinv, member, lay)
 
 
-def blocks_kernel(x, blocks, out_ref):
-    out_ref[...] = apply_blocks(blocks, two_parts(x[...]))
-
-
 def finish_first(odd, first, rise, first_ref, grown_ref, sends):
     first_ref[...] = first
     grown = dot(left_stack(first), rise[:, :GROWN])
@@ -433,24 +424,25 @@
     finish_first(odd, first, rise, first_ref, grown_ref, sends)
 
 
-def first1_kernel(odd, table, x, coarse, b0, coarse0, blocks, rise, *outs):
-    z_ref, scal_ref, first_ref, grown_ref, *sends = outs
-    h00, square = read_scalars(table, 2)
-    h10 = jnp.sqrt(jnp.maximum(square - h00 * h00, 1e-7 * square))
-    for i, value in enumerate((h00, h10, square)):
+def next_kernel(step, odd, table, x, coarse, *refs):
+    basis, coarses, refs = refs[:step], refs[step : 2 * step], refs[2 * step :]
+    blocks, rise, z_ref, coarse_ref, scal_ref, first_ref, grown_ref, *sends = refs
+    *coeffs, square = read_scalars(table, step + 1)
+    rest = square
+    for h in coeffs:
+        rest = rest - h * h
+    height = jnp.sqrt(jnp.maximum(rest, 1e-7 * square))
+    for i, value in enumerate((*coeffs, height)):
         scal_ref[i * STRIDE : (i + 1) * STRIDE, :] = jnp.broadcast_to(value, (STRIDE, 128))
-    h00, h10 = h00[:, :NODES], h10[:, :NODES]
-    z = (x[...] - h00 * b0[...]) / h10
+    z, scaled = x[...], coarse[...]
+    for h, vector, known in zip(coeffs, basis, coarses):
+        z = z - h[:, :NODES] * vector[...]
+        scaled = scaled - h[:, :NODES] * known[...]
+    z = z / height[:, :NODES]
+    scaled = scaled / height[:, :NODES]
     z_ref[...] = z
-    scaled = (coarse[...] - h00 * coarse0[...]) / h10
+    coarse_ref[...] = scaled
     first = apply_blocks(blocks, rounded(z)) + scaled
-    finish_first(odd, first, rise, first_ref, grown_ref, sends)
-
-
-def first2_kernel(odd, r0, r1, r2, r3, fine, cinv, member, lay, rise, *outs):
-    first_ref, grown_ref, *sends = outs
-    coarse = (r0[...] + r1[...]) + (r2[...] + r3[...])
-    first = fine[...] + coarse_values(coarse, cinv, member, lay)
     finish_first(odd, first, rise, first_ref, grown_ref, sends)
 
 
@@ -470,14 +462,13 @@
     out_ref[...] = result + place_terms(groups, omask, lay, 2)
 
 
-def second_kernel(step, *refs):
+def second_kernel(*refs):
     odd, z, first, local = refs[:4]
     recv = refs[4:9]
     rem, omask, lay, blocks, rise = refs[9:12], *refs[12:16]
     search_ref, grown_ref, *sends = refs[16:]
     defect = z[...] - (local[...] + halo_part(recv, rem, omask, lay))
-    parts = two_parts(defect) if step == 2 else rounded(defect)
-    search = first[...] + apply_blocks(blocks, parts)
+    search = first[...] + apply_blocks(blocks, rounded(defect))
     search_ref[...] = search
     grown = dot(left_stack(search), rise[:, :GROWN])
     grown_ref[...] = grown
@@ -489,21 +480,14 @@
     recv = refs[1:6]
     rem, omask, lay = refs[6:9], refs[9], refs[10]
     mapped = local[...] + halo_part(recv, rem, omask, lay)
-    if step == 0:
-        member, rise, b0, w_ref, table_ref, row_ref = refs[11:]
-        scalars = [total(mapped * b0[...]), total(mapped * mapped)]
-    elif step == 1:
-        member, rise, w_ref, row_ref = refs[11:]
+    if step == 2:
+        *basis, w_ref, table_ref = refs[11:]
     else:
-        b0, b1, w1, w_ref, table_ref = refs[11:]
-        scalars = [total(w1[...] * b[...]) for b in (b0, b1, w1)]
-        scalars += [total(mapped * b[...]) for b in (b0, b1, w1)]
-        scalars += [total(mapped * mapped)]
+        member, rise, *basis, w_ref, table_ref, row_ref = refs[11:]
+        row_ref[...] = coarse_row(member[...], rise, mapped)
+    scalars = [total(mapped * b[...]) for b in basis] + [total(mapped * mapped)]
     w_ref[...] = mapped
-    if step != 1:
-        table_ref[...] = jnp.broadcast_to(scalar_row(scalars), table_ref.shape)
-    if step != 2:
-        row_ref[...] = coarse_row(member[...], rise, mapped)
+    table_ref[...] = jnp.broadcast_to(scalar_row(scalars), table_ref.shape)
 
 
 def inverse_sqrt(value):
@@ -536,31 +520,15 @@
     return weights
 
 
-def final_kernel(table, scal0, scal1, x, s0, s1, s2, w0, w1, w2, update_ref, residual_ref):
-    g0, g1, g2, q0, q1, qw, qq = read_scalars(table, 7)
+def final_kernel(table, scal0, scal1, scal2, x, s0, s1, s2, w0, w1, w2, update_ref, residual_ref):
+    h02, h12, h22, square = read_scalars(table, 4)
     beta = scal0[0:1, :]
-    h00, h10, square0 = [scal1[i * STRIDE : i * STRIDE + 1, :] for i in range(3)]
-    h01, h11 = g0, g1
-    squared = jnp.maximum(g2 - h01 * h01 - h11 * h11, 1e-7 * g2)
-    inv21 = inverse_sqrt(squared)
-    h21 = squared * inv21
-    cross = h00 * h01 + h10 * h11
-    h02 = (q0 - h01 * h00 - h11 * h01) * inv21
-    h12 = (q1 - h01 * h10 - h11 * h11) * inv21
-    with_w1 = (qw - h01 * cross - h11 * g2) * inv21
-    h22 = (with_w1 - h01 * h02 - h11 * h12) * inv21
-    with_w0 = h00 * q0 + h10 * q1
-    square = qq + h01 * h01 * square0 + h11 * h11 * g2
-    square = square - 2.0 * (h01 * with_w0 + h11 * qw - h01 * h11 * cross)
-    square = square * inv21 * inv21
+    h00, h10 = [scal1[i * STRIDE : i * STRIDE + 1, :] for i in range(2)]
+    h01, h11, h21 = [scal2[i * STRIDE : i * STRIDE + 1, :] for i in range(3)]
     h32 = jnp.sqrt(jnp.maximum(square - h02 * h02 - h12 * h12 - h22 * h22, 1e-7 * square))
     zero = jnp.zeros_like(beta)
     hess = [[h00, h01, h02], [h10, h11, h12], [zero, h21, h22], [zero, zero, h32]]
-    y0, y1, y2 = least_squares(hess, beta)
-    y2 = y2 * inv21
-    y0 = y0 - y2 * h01
-    y1 = y1 - y2 * h11
-    y0, y1, y2 = (y[:, :NODES] for y in (y0, y1, y2))
+    y0, y1, y2 = (y[:, :NODES] for y in least_squares(hess, beta))
     update = y0 * s0[...] + y1 * s1[...] + y2 * s2[...]
     residual = x[...] - (y0 * w0[...] + y1 * w1[...] + y2 * w2[...])
     for e in range(ELEMS):
@@ -703,42 +671,27 @@
 
     coarse_tables = (cinv3, member, t["lay"])
     tail = (turned, t["rise"])
-    basis, search, images, scalars = [], [], [], []
-    coarse0 = None
+    basis, search, images, scalars, coarses = [], [], [], [], []
     outs = [vec, grow] + [send] * 5
     for step in range(3):
-        if step < 2:
-            (coarse,) = call(coarse_kernel, "coarse%d" % step, (*rows, *coarse_tables), [vec])
+        (coarse,) = call(coarse_kernel, "coarse%d" % step, (*rows, *coarse_tables), [vec])
         if step == 0:
-            z, coarse0, scal, first, grown, *sends = call(
-                first0_kernel,
-                "first0",
-                (odd, table, x, coarse) + tail,
-                [vec, vec, (8, 128)] + outs,
-            )
-            scalars.append(scal)
-        elif step == 1:
-            z, scal, first, grown, *sends = call(
-                first1_kernel,
-                "first1",
-                (odd, table, images[0], coarse, basis[0], coarse0) + tail,
-                [vec, (3 * STRIDE, 128)] + outs,
-            )
-            scalars.append(scal)
+            kernel, args = first0_kernel, (odd, table, x, coarse)
         else:
-            z = images[1]
-            (fine,) = call(blocks_kernel, "fine", (z, turned), [vec])
-            first, grown, *sends = call(
-                first2_kernel,
-                "first2",
-                (odd, *rows, fine, *coarse_tables, t["rise"]),
-                outs,
-            )
+            kernel, args = with_step(next_kernel, step), (odd, table, images[-1], coarse)
+        z, scaled, scal, first, grown, *sends = call(
+            kernel,
+            "first%d" % step,
+            (*args, *basis, *coarses, *tail),
+            [vec, vec, ((8, 16, 24)[step], 128)] + outs,
+        )
         basis.append(z)
+        coarses.append(scaled)
+        scalars.append(scal)
         recv = exchange(sends)
         local = local_part(first, grown, step)
         direction, grown, *sends = call(
-            with_step(second_kernel, step),
+            second_kernel,
             "second%d" % step,
             (odd, z, first, local, *recv) + remote + tail,
             outs,
@@ -748,21 +701,17 @@
         local = local_part(direction, grown, step)
         kernel = with_step(third_kernel, step)
         args = (local, *recv) + remote
-        if step == 0:
+        if step < 2:
             image, table, row = call(
                 kernel,
-                "third0",
-                args + (member, t["rise"], basis[0]),
+                "third%d" % step,
+                args + (member, t["rise"], *basis),
                 [vec, table_shape, (1, WIDE)],
             )
-            table = lax.all_to_all(table, AXES, 0, 0, tiled=True)
-            rows = span_rows(row)
-        elif step == 1:
-            image, row = call(kernel, "third1", args + (member, t["rise"]), [vec, (1, WIDE)])
             rows = span_rows(row)
         else:
             image, table = call(kernel, "third2", args + tuple(basis), [vec, table_shape])
-            table = lax.all_to_all(table, AXES, 0, 0, tiled=True)
+        table = lax.all_to_all(table, AXES, 0, 0, tiled=True)
         images.append(image)
 
     update, residual = call(

time: 139 us -> 153 us (1.10)
  waiting for transfers between devices: 19.3 us -> 32 us
    all_to_all x2 -> x3, starting transfers between devices: 26.6 us -> 33.7 us  [body(): table = lax.all_to_all(table, AXES, 0, 0, tiled=True)]
    ppermute x30, starting transfers between devices: 37.9 us -> 31.6 us  [exchange(): return [lax.ppermute(x, axis, way) for x, (axis, way) in zip(sends, ways)]]
    all_to_all x2 -> x3, waiting for transfers between devices: 9.39 us -> 15.4 us  [body(): table = lax.all_to_all(table, AXES, 0, 0, tiled=True)]
    ppermute x30, waiting for transfers between devices: 4.88 us -> 10.4 us  [exchange(): return [lax.ppermute(x, axis, way) for x, (axis, way) in zip(sends, ways)]]
  transfers between devices with their start and end apart: 41 -> 42, of which waited for: 15 -> 16; matrix products, arithmetic and copies ran while one was open for 0% -> 0% of each run, Pallas kernels for 5% -> 4%
where the time goes in v4:
time: 153 us; the launch traced here: 152 us
  starting transfers between devices  76.8 us (50%)
  waiting for transfers between devices  32 us (21%)
  blocking collectives  22 us (14%)
  Pallas kernels  17.5 us (11%)
  local copies, waits for them, and re-layouts  3.03 us (2%)
    all_to_all x3, starting transfers between devices, body(): table = lax.all_to_all(table, AXES, 0, 0, tiled=True)  33.7 us
    ppermute x30, starting transfers between devices, exchange(): return [lax.ppermute(x, axis, way) for x, (axis, way) in zip(sends, ways)]  31.6 us
    all_to_all x1, blocking collectives, body(): table = lax.all_to_all(table, AXES, 0, 0, tiled=True)  22 us
    pallas_call x22, Pallas kernels, call(): pl.pallas_call(kernel, name=name, out_shape=[shape_of(out) for out in out...  17.5 us
    all_to_all x3, waiting for transfers between devices, body(): table = lax.all_to_all(table, AXES, 0, 0, tiled=True)  15.4 us
    ppermute x9, starting transfers between devices, span_rows(): lax.ppermute(row, 'span', [(i, i ^ k) for i in range(n_span)])  11.6 us
    ppermute x30, waiting for transfers between devices, exchange(): return [lax.ppermute(x, axis, way) for x, (axis, way) in zip(sends, ways)]  10.4 us
    ppermute x9, waiting for transfers between devices, span_rows(): lax.ppermute(row, 'span', [(i, i ^ k) for i in range(n_span)])  6.09 us
  transfers between devices with their start and end apart: 42, of which 16 were waited for; matrix products, arithmetic and copies ran while one was open for 0% of the time, Pallas kernels for 4%

profile of v4, /device:TPU:1, one launch (start us, length us, event | category | flops | bytes accessed | tf_op | source)
XLA Modules:
  0.0 152.4 jit_solution(8411244028765227895)
XLA Ops:
  2.2 15.7 %all-to-all-start = ((f32[256,1,128]{2,1,0:T(1,128)}), f32[256,1,128]{2,1,0:T(1,128)S(1)}, u32[]{:S(2)}, u32[]{:S(2)}) async-start(f32[256,1,128]{2,1,0:T(1,128)} %bitcast.7), calls=%async_computation | async-start | bytes 262144 | tf_op jit(solution)/shard_map/all_to_all | solution.py:628
  19.2 3.0 %collective-permute-start = (f32[1,256]{1,0:T(1,128)S(1)}, f32[1,256]{1,0:T(1,128)S(1)}, u32[]{:S(2)}, u32[]{:S(2)}) collective-permute-start(f32[1,256]{1,0:T(1,128)S(1)} %get-tuple-element.76.r0), channel_id=1, source_target_pairs={{0,4},{2,6},{4,0},{6,2},{1,5},{3,7},{5,1},{7,3},{8,12},{10,14},{12... | collective-permute-start | bytes 3080 | tf_op jit(solution)/shard_map/ppermute | solution.py:616
  25.0 1.4 setup.1
  26.8 4.0 %all-to-all-done = f32[256,1,128]{2,1,0:T(1,128)S(1)} async-done(((f32[256,1,128]{2,1,0:T(1,128)}), f32[256,1,128]{2,1,0:T(1,128)S(1)}, u32[]{:S(2)}, u32[]{:S(2)}) %all-to-all-start) | async-done | bytes 131104 | tf_op jit(solution)/shard_map/all_to_all | solution.py:628
  32.4 1.9 %collective-permute-start.4 = (f32[8,128]{1,0:T(8,128)S(1)}, f32[8,128]{1,0:T(8,128)S(1)}, u32[]{:S(2)}, u32[]{:S(2)}) collective-permute-start(f32[8,128]{1,0:T(8,128)S(1)} %get-tuple-element.89), channel_id=1, source_target_pairs={{0,248},{8,16},{16,8},{24,32},{32,24},{40,48},{48,40},{56,64},{64,... | collective-permute-start | bytes 12296 | tf_op jit(solution)/shard_map/ppermute | solution.py:612
  34.7 1.7 %collective-permute-start.6 = (f32[8,128]{1,0:T(8,128)S(1)}, f32[8,128]{1,0:T(8,128)S(1)}, u32[]{:S(2)}, u32[]{:S(2)}) collective-permute-start(f32[8,128]{1,0:T(8,128)S(1)} %get-tuple-element.91), channel_id=1, source_target_pairs={{0,6},{2,4},{4,2},{6,0},{1,7},{3,5},{5,3},{7,1},{8,14},{10,12},{12... | collective-permute-start | bytes 12296 | tf_op jit(solution)/shard_map/ppermute | solution.py:612
  36.4 2.4 %collective-permute-start.7 = (f32[8,128]{1,0:T(8,128)S(1)}, f32[8,128]{1,0:T(8,128)S(1)}, u32[]{:S(2)}, u32[]{:S(2)}) collective-permute-start(f32[8,128]{1,0:T(8,128)S(1)} %get-tuple-element.92), channel_id=1, source_target_pairs={{0,8},{8,0},{16,24},{24,16},{32,40},{40,32},{48,56},{56,48},{64,72... | collective-permute-start | bytes 12296 | tf_op jit(solution)/shard_map/ppermute | solution.py:612
  41.8 3.2 %collective-permute-start.12 = (f32[8,128]{1,0:T(8,128)S(1)}, f32[8,128]{1,0:T(8,128)S(1)}, u32[]{:S(2)}, u32[]{:S(2)}) collective-permute-start(f32[8,128]{1,0:T(8,128)S(1)} %get-tuple-element.102), channel_id=1, source_target_pairs={{0,8},{8,0},{16,24},{24,16},{32,40},{40,32},{48,56},{56,48},{64,72... | collective-permute-start | bytes 12296 | tf_op jit(solution)/shard_map/ppermute | solution.py:612
  45.0 1.8 %collective-permute-start.8 = (f32[8,128]{1,0:T(8,128)S(1)}, f32[8,128]{1,0:T(8,128)S(1)}, u32[]{:S(2)}, u32[]{:S(2)}) collective-permute-start(f32[8,128]{1,0:T(8,128)S(1)} %get-tuple-element.98), channel_id=1, source_target_pairs={{0,1},{1,0},{2,3},{3,2},{4,5},{5,4},{6,7},{7,6},{8,9},{9,8},{10,11... | collective-permute-start | bytes 12296 | tf_op jit(solution)/shard_map/ppermute | solution.py:612
  47.3 1.7 %collective-permute-done.8.refs_1_ = f32[8,128]{1,0:T(8,128)S(1)} collective-permute-done((f32[8,128]{1,0:T(8,128)S(1)}, f32[8,128]{1,0:T(8,128)S(1)}, u32[]{:S(2)}, u32[]{:S(2)}) %collective-permute-start.8) | collective-permute-done | bytes 4128 | tf_op jit(solution)/shard_map/ppermute | solution.py:612
  49.8 1.4 third0.1
  51.2 8.8 %all-to-all-start.1 = ((f32[256,1,128]{2,1,0:T(1,128)}), f32[256,1,128]{2,1,0:T(1,128)S(1)}, u32[]{:S(2)}, u32[]{:S(2)}) async-start(f32[256,1,128]{2,1,0:T(1,128)} %bitcast.13), calls=%async_computation.1 | async-start | bytes 262144 | tf_op jit(solution)/shard_map/all_to_all | solution.py:714
  60.0 3.0 %collective-permute-start.13 = (f32[1,256]{1,0:T(1,128)S(1)}, f32[1,256]{1,0:T(1,128)S(1)}, u32[]{:S(2)}, u32[]{:S(2)}) collective-permute-start(f32[1,256]{1,0:T(1,128)S(1)} %get-tuple-element.105.r0), channel_id=1, source_target_pairs={{0,4},{2,6},{4,0},{6,2},{1,5},{3,7},{5,1},{7,3},{8,12},{10,14},{12... | collective-permute-start | bytes 3080 | tf_op jit(solution)/shard_map/ppermute | solution.py:616
  64.0 2.9 %collective-permute-done.14.r2 = f32[1,256]{1,0:T(1,128)S(1)} collective-permute-done((f32[1,256]{1,0:T(1,128)S(1)}, f32[1,256]{1,0:T(1,128)S(1)}, u32[]{:S(2)}, u32[]{:S(2)}) %collective-permute-start.14) | collective-permute-done | bytes 1056 | tf_op jit(solution)/shard_map/ppermute | solution.py:616
  67.3 5.7 %all-to-all-done.1 = f32[256,1,128]{2,1,0:T(1,128)S(1)} async-done(((f32[256,1,128]{2,1,0:T(1,128)}), f32[256,1,128]{2,1,0:T(1,128)S(1)}, u32[]{:S(2)}, u32[]{:S(2)}) %all-to-all-start.1) | async-done | bytes 131104 | tf_op jit(solution)/shard_map/all_to_all | solution.py:714
  74.5 1.9 %collective-permute-start.17 = (f32[8,128]{1,0:T(8,128)S(1)}, f32[8,128]{1,0:T(8,128)S(1)}, u32[]{:S(2)}, u32[]{:S(2)}) collective-permute-start(f32[8,128]{1,0:T(8,128)S(1)} %get-tuple-element.111), channel_id=1, source_target_pairs={{0,248},{8,16},{16,8},{24,32},{32,24},{40,48},{48,40},{56,64},{64,... | collective-permute-start | bytes 12296 | tf_op jit(solution)/shard_map/ppermute | solution.py:612
  79.0 1.8 %collective-permute-done.19.refs_7_ = f32[8,128]{1,0:T(8,128)S(1)} collective-permute-done((f32[8,128]{1,0:T(8,128)S(1)}, f32[8,128]{1,0:T(8,128)S(1)}, u32[]{:S(2)}, u32[]{:S(2)}) %collective-permute-start.19) | collective-permute-done | bytes 4128 | tf_op jit(solution)/shard_map/ppermute | solution.py:612
  82.0 1.3 collective-permute-start.21
  83.4 2.1 %collective-permute-start.22 = (f32[8,128]{1,0:T(8,128)S(1)}, f32[8,128]{1,0:T(8,128)S(1)}, u32[]{:S(2)}, u32[]{:S(2)}) collective-permute-start(f32[8,128]{1,0:T(8,128)S(1)} %get-tuple-element.118), channel_id=1, source_target_pairs={{0,248},{8,16},{16,8},{24,32},{32,24},{40,48},{48,40},{56,64},{64,... | collective-permute-start | bytes 12296 | tf_op jit(solution)/shard_map/ppermute | solution.py:612
  86.2 1.4 collective-permute-start.25
  89.2 1.4 third1.1
  90.5 9.1 %all-to-all-start.2 = ((f32[256,1,128]{2,1,0:T(1,128)}), f32[256,1,128]{2,1,0:T(1,128)S(1)}, u32[]{:S(2)}, u32[]{:S(2)}) async-start(f32[256,1,128]{2,1,0:T(1,128)} %bitcast.16), calls=%async_computation.2 | async-start | bytes 262144 | tf_op jit(solution)/shard_map/all_to_all | solution.py:714
  99.7 3.0 %collective-permute-start.26 = (f32[1,256]{1,0:T(1,128)S(1)}, f32[1,256]{1,0:T(1,128)S(1)}, u32[]{:S(2)}, u32[]{:S(2)}) collective-permute-start(f32[1,256]{1,0:T(1,128)S(1)} %get-tuple-element.124.r0), channel_id=1, source_target_pairs={{0,4},{2,6},{4,0},{6,2},{1,5},{3,7},{5,1},{7,3},{8,12},{10,14},{12... | collective-permute-start | bytes 3080 | tf_op jit(solution)/shard_map/ppermute | solution.py:616
  103.7 2.9 %collective-permute-done.27.r2 = f32[1,256]{1,0:T(1,128)S(1)} collective-permute-done((f32[1,256]{1,0:T(1,128)S(1)}, f32[1,256]{1,0:T(1,128)S(1)}, u32[]{:S(2)}, u32[]{:S(2)}) %collective-permute-start.27) | collective-permute-done | bytes 1056 | tf_op jit(solution)/shard_map/ppermute | solution.py:616
  107.0 5.7 %all-to-all-done.2 = f32[256,1,128]{2,1,0:T(1,128)S(1)} async-done(((f32[256,1,128]{2,1,0:T(1,128)}), f32[256,1,128]{2,1,0:T(1,128)S(1)}, u32[]{:S(2)}, u32[]{:S(2)}) %all-to-all-start.2) | async-done | bytes 131104 | tf_op jit(solution)/shard_map/all_to_all | solution.py:714
  114.3 1.9 %collective-permute-start.30 = (f32[8,128]{1,0:T(8,128)S(1)}, f32[8,128]{1,0:T(8,128)S(1)}, u32[]{:S(2)}, u32[]{:S(2)}) collective-permute-start(f32[8,128]{1,0:T(8,128)S(1)} %get-tuple-element.130), channel_id=1, source_target_pairs={{0,248},{8,16},{16,8},{24,32},{32,24},{40,48},{48,40},{56,64},{64,... | collective-permute-start | bytes 12296 | tf_op jit(solution)/shard_map/ppermute | solution.py:612
  118.7 1.8 %collective-permute-done.32.refs_7_ = f32[8,128]{1,0:T(8,128)S(1)} collective-permute-done((f32[8,128]{1,0:T(8,128)S(1)}, f32[8,128]{1,0:T(8,128)S(1)}, u32[]{:S(2)}, u32[]{:S(2)}) %collective-permute-start.32) | collective-permute-done | bytes 4128 | tf_op jit(solution)/shard_map/ppermute | solution.py:612
  120.6 1.2 second2.1
  121.8 1.3 collective-permute-start.34
  123.1 2.1 %collective-permute-start.35 = (f32[8,128]{1,0:T(8,128)S(1)}, f32[8,128]{1,0:T(8,128)S(1)}, u32[]{:S(2)}, u32[]{:S(2)}) collective-permute-start(f32[8,128]{1,0:T(8,128)S(1)} %get-tuple-element.137), channel_id=1, source_target_pairs={{0,248},{8,16},{16,8},{24,32},{32,24},{40,48},{48,40},{56,64},{64,... | collective-permute-start | bytes 12296 | tf_op jit(solution)/shard_map/ppermute | solution.py:612
  126.0 1.4 collective-permute-start.38
  129.6 22.0 %all_to_all.44 = f32[256,1,128]{2,1,0:T(1,128)S(1)} all-to-all(f32[256,1,128]{2,1,0:T(1,128)S(1)} %bitcast.30), channel_id=1, replica_groups=mesh['passage'=32,'span'=4,'radial'=2] {'passage','span','radial'}, dimensions={0} | all-to-all | bytes 262144 | tf_op jit(solution)/shard_map/all_to_all | solution.py:714
  (109 shorter events, 30.5 us)
Async XLA Ops:
  2.2 28.7 %all-to-all-start = ((f32[256,1,128]{2,1,0:T(1,128)}), f32[256,1,128]{2,1,0:T(1,128)S(1)}, u32[]{:S(2)}, u32[]{:S(2)}) async-start(f32[256,1,128]{2,1,0:T(1,128)} %bitcast.7), calls=%async_computation | async-start | bytes 262144 | tf_op jit(solution)/shard_map/all_to_all | solution.py:628
  19.2 7.3 %collective-permute-start = (f32[1,256]{1,0:T(1,128)S(1)}, f32[1,256]{1,0:T(1,128)S(1)}, u32[]{:S(2)}, u32[]{:S(2)}) collective-permute-start(f32[1,256]{1,0:T(1,128)S(1)} %get-tuple-element.76.r0), channel_id=1, source_target_pairs={{0,4},{2,6},{4,0},{6,2},{1,5},{3,7},{5,1},{7,3},{8,12},{10,14},{12... | collective-permute-start | bytes 3080 | tf_op jit(solution)/shard_map/ppermute | solution.py:616
  22.1 4.3 %collective-permute-start.1 = (f32[1,256]{1,0:T(1,128)S(1)}, f32[1,256]{1,0:T(1,128)S(1)}, u32[]{:S(2)}, u32[]{:S(2)}) collective-permute-start(f32[1,256]{1,0:T(1,128)S(1)} %get-tuple-element.76.r0), channel_id=1, source_target_pairs={{0,6},{2,4},{4,2},{6,0},{1,7},{3,5},{5,3},{7,1},{8,14},{10,12},{12... | collective-permute-start | bytes 3080 | tf_op jit(solution)/shard_map/ppermute | solution.py:616
  23.0 3.4 %collective-permute-start.2 = (f32[1,256]{1,0:T(1,128)S(1)}, f32[1,256]{1,0:T(1,128)S(1)}, u32[]{:S(2)}, u32[]{:S(2)}) collective-permute-start(f32[1,256]{1,0:T(1,128)S(1)} %get-tuple-element.76.r0), channel_id=1, source_target_pairs={{0,2},{2,0},{4,6},{6,4},{1,3},{3,1},{5,7},{7,5},{8,10},{10,8},{12,... | collective-permute-start | bytes 3080 | tf_op jit(solution)/shard_map/ppermute | solution.py:616
  31.6 7.7 %collective-permute-start.3 = (f32[8,128]{1,0:T(8,128)S(1)}, f32[8,128]{1,0:T(8,128)S(1)}, u32[]{:S(2)}, u32[]{:S(2)}) collective-permute-start(f32[8,128]{1,0:T(8,128)S(1)} %get-tuple-element.88), channel_id=1, source_target_pairs={{0,1},{1,0},{2,3},{3,2},{4,5},{5,4},{6,7},{7,6},{8,9},{9,8},{10,11... | collective-permute-start | bytes 12296 | tf_op jit(solution)/shard_map/ppermute | solution.py:612
  32.4 7.0 %collective-permute-start.4 = (f32[8,128]{1,0:T(8,128)S(1)}, f32[8,128]{1,0:T(8,128)S(1)}, u32[]{:S(2)}, u32[]{:S(2)}) collective-permute-start(f32[8,128]{1,0:T(8,128)S(1)} %get-tuple-element.89), channel_id=1, source_target_pairs={{0,248},{8,16},{16,8},{24,32},{32,24},{40,48},{48,40},{56,64},{64,... | collective-permute-start | bytes 12296 | tf_op jit(solution)/shard_map/ppermute | solution.py:612
  34.3 5.1 %collective-permute-start.5 = (f32[8,128]{1,0:T(8,128)S(1)}, f32[8,128]{1,0:T(8,128)S(1)}, u32[]{:S(2)}, u32[]{:S(2)}) collective-permute-start(f32[8,128]{1,0:T(8,128)S(1)} %get-tuple-element.90), channel_id=1, source_target_pairs={{0,2},{2,0},{4,6},{6,4},{1,3},{3,1},{5,7},{7,5},{8,10},{10,8},{12,... | collective-permute-start | bytes 12296 | tf_op jit(solution)/shard_map/ppermute | solution.py:612
  34.7 4.7 %collective-permute-start.6 = (f32[8,128]{1,0:T(8,128)S(1)}, f32[8,128]{1,0:T(8,128)S(1)}, u32[]{:S(2)}, u32[]{:S(2)}) collective-permute-start(f32[8,128]{1,0:T(8,128)S(1)} %get-tuple-element.91), channel_id=1, source_target_pairs={{0,6},{2,4},{4,2},{6,0},{1,7},{3,5},{5,3},{7,1},{8,14},{10,12},{12... | collective-permute-start | bytes 12296 | tf_op jit(solution)/shard_map/ppermute | solution.py:612
  40.9 6.4 %collective-permute-start.10 = (f32[8,128]{1,0:T(8,128)S(1)}, f32[8,128]{1,0:T(8,128)S(1)}, u32[]{:S(2)}, u32[]{:S(2)}) collective-permute-start(f32[8,128]{1,0:T(8,128)S(1)} %get-tuple-element.100), channel_id=1, source_target_pairs={{0,2},{2,0},{4,6},{6,4},{1,3},{3,1},{5,7},{7,5},{8,10},{10,8},{12,... | collective-permute-start | bytes 12296 | tf_op jit(solution)/shard_map/ppermute | solution.py:612
  40.9 6.4 %collective-permute-start.11 = (f32[8,128]{1,0:T(8,128)S(1)}, f32[8,128]{1,0:T(8,128)S(1)}, u32[]{:S(2)}, u32[]{:S(2)}) collective-permute-start(f32[8,128]{1,0:T(8,128)S(1)} %get-tuple-element.101), channel_id=1, source_target_pairs={{0,6},{2,4},{4,2},{6,0},{1,7},{3,5},{5,3},{7,1},{8,14},{10,12},{12... | collective-permute-start | bytes 12296 | tf_op jit(solution)/shard_map/ppermute | solution.py:612
  41.8 5.5 %collective-permute-start.12 = (f32[8,128]{1,0:T(8,128)S(1)}, f32[8,128]{1,0:T(8,128)S(1)}, u32[]{:S(2)}, u32[]{:S(2)}) collective-permute-start(f32[8,128]{1,0:T(8,128)S(1)} %get-tuple-element.102), channel_id=1, source_target_pairs={{0,8},{8,0},{16,24},{24,16},{32,40},{40,32},{48,56},{56,48},{64,72... | collective-permute-start | bytes 12296 | tf_op jit(solution)/shard_map/ppermute | solution.py:612
  45.0 4.0 %collective-permute-start.8 = (f32[8,128]{1,0:T(8,128)S(1)}, f32[8,128]{1,0:T(8,128)S(1)}, u32[]{:S(2)}, u32[]{:S(2)}) collective-permute-start(f32[8,128]{1,0:T(8,128)S(1)} %get-tuple-element.98), channel_id=1, source_target_pairs={{0,1},{1,0},{2,3},{3,2},{4,5},{5,4},{6,7},{7,6},{8,9},{9,8},{10,11... | collective-permute-start | bytes 12296 | tf_op jit(solution)/shard_map/ppermute | solution.py:612
  51.2 21.8 %all-to-all-start.1 = ((f32[256,1,128]{2,1,0:T(1,128)}), f32[256,1,128]{2,1,0:T(1,128)S(1)}, u32[]{:S(2)}, u32[]{:S(2)}) async-start(f32[256,1,128]{2,1,0:T(1,128)} %bitcast.13), calls=%async_computation.1 | async-start | bytes 262144 | tf_op jit(solution)/shard_map/all_to_all | solution.py:714
  60.0 4.0 %collective-permute-start.13 = (f32[1,256]{1,0:T(1,128)S(1)}, f32[1,256]{1,0:T(1,128)S(1)}, u32[]{:S(2)}, u32[]{:S(2)}) collective-permute-start(f32[1,256]{1,0:T(1,128)S(1)} %get-tuple-element.105.r0), channel_id=1, source_target_pairs={{0,4},{2,6},{4,0},{6,2},{1,5},{3,7},{5,1},{7,3},{8,12},{10,14},{12... | collective-permute-start | bytes 3080 | tf_op jit(solution)/shard_map/ppermute | solution.py:616
  63.0 3.9 %collective-permute-start.14 = (f32[1,256]{1,0:T(1,128)S(1)}, f32[1,256]{1,0:T(1,128)S(1)}, u32[]{:S(2)}, u32[]{:S(2)}) collective-permute-start(f32[1,256]{1,0:T(1,128)S(1)} %get-tuple-element.105.r0), channel_id=1, source_target_pairs={{0,6},{2,4},{4,2},{6,0},{1,7},{3,5},{5,3},{7,1},{8,14},{10,12},{12... | collective-permute-start | bytes 3080 | tf_op jit(solution)/shard_map/ppermute | solution.py:616
  73.8 4.2 %collective-permute-start.16 = (f32[8,128]{1,0:T(8,128)S(1)}, f32[8,128]{1,0:T(8,128)S(1)}, u32[]{:S(2)}, u32[]{:S(2)}) collective-permute-start(f32[8,128]{1,0:T(8,128)S(1)} %get-tuple-element.110), channel_id=1, source_target_pairs={{0,1},{1,0},{2,3},{3,2},{4,5},{5,4},{6,7},{7,6},{8,9},{9,8},{10,11... | collective-permute-start | bytes 12296 | tf_op jit(solution)/shard_map/ppermute | solution.py:612
  74.5 3.5 %collective-permute-start.17 = (f32[8,128]{1,0:T(8,128)S(1)}, f32[8,128]{1,0:T(8,128)S(1)}, u32[]{:S(2)}, u32[]{:S(2)}) collective-permute-start(f32[8,128]{1,0:T(8,128)S(1)} %get-tuple-element.111), channel_id=1, source_target_pairs={{0,248},{8,16},{16,8},{24,32},{32,24},{40,48},{48,40},{56,64},{64,... | collective-permute-start | bytes 12296 | tf_op jit(solution)/shard_map/ppermute | solution.py:612
  76.8 4.0 %collective-permute-start.19 = (f32[8,128]{1,0:T(8,128)S(1)}, f32[8,128]{1,0:T(8,128)S(1)}, u32[]{:S(2)}, u32[]{:S(2)}) collective-permute-start(f32[8,128]{1,0:T(8,128)S(1)} %get-tuple-element.113), channel_id=1, source_target_pairs={{0,6},{2,4},{4,2},{6,0},{1,7},{3,5},{5,3},{7,1},{8,14},{10,12},{12... | collective-permute-start | bytes 12296 | tf_op jit(solution)/shard_map/ppermute | solution.py:612
  77.1 3.7 %collective-permute-start.20 = (f32[8,128]{1,0:T(8,128)S(1)}, f32[8,128]{1,0:T(8,128)S(1)}, u32[]{:S(2)}, u32[]{:S(2)}) collective-permute-start(f32[8,128]{1,0:T(8,128)S(1)} %get-tuple-element.114), channel_id=1, source_target_pairs={{0,8},{8,0},{16,24},{24,16},{32,40},{40,32},{48,56},{56,48},{64,72... | collective-permute-start | bytes 12296 | tf_op jit(solution)/shard_map/ppermute | solution.py:612
  82.0 6.1 %collective-permute-start.21 = (f32[8,128]{1,0:T(8,128)S(1)}, f32[8,128]{1,0:T(8,128)S(1)}, u32[]{:S(2)}, u32[]{:S(2)}) collective-permute-start(f32[8,128]{1,0:T(8,128)S(1)} %get-tuple-element.117), channel_id=1, source_target_pairs={{0,1},{1,0},{2,3},{3,2},{4,5},{5,4},{6,7},{7,6},{8,9},{9,8},{10,11... | collective-permute-start | bytes 12296 | tf_op jit(solution)/shard_map/ppermute | solution.py:612
  83.4 4.7 %collective-permute-start.22 = (f32[8,128]{1,0:T(8,128)S(1)}, f32[8,128]{1,0:T(8,128)S(1)}, u32[]{:S(2)}, u32[]{:S(2)}) collective-permute-start(f32[8,128]{1,0:T(8,128)S(1)} %get-tuple-element.118), channel_id=1, source_target_pairs={{0,248},{8,16},{16,8},{24,32},{32,24},{40,48},{48,40},{56,64},{64,... | collective-permute-start | bytes 12296 | tf_op jit(solution)/shard_map/ppermute | solution.py:612
  85.5 3.7 %collective-permute-start.24 = (f32[8,128]{1,0:T(8,128)S(1)}, f32[8,128]{1,0:T(8,128)S(1)}, u32[]{:S(2)}, u32[]{:S(2)}) collective-permute-start(f32[8,128]{1,0:T(8,128)S(1)} %get-tuple-element.120), channel_id=1, source_target_pairs={{0,6},{2,4},{4,2},{6,0},{1,7},{3,5},{5,3},{7,1},{8,14},{10,12},{12... | collective-permute-start | bytes 12296 | tf_op jit(solution)/shard_map/ppermute | solution.py:612
  90.5 22.2 %all-to-all-start.2 = ((f32[256,1,128]{2,1,0:T(1,128)}), f32[256,1,128]{2,1,0:T(1,128)S(1)}, u32[]{:S(2)}, u32[]{:S(2)}) async-start(f32[256,1,128]{2,1,0:T(1,128)} %bitcast.16), calls=%async_computation.2 | async-start | bytes 262144 | tf_op jit(solution)/shard_map/all_to_all | solution.py:714
  99.7 4.0 %collective-permute-start.26 = (f32[1,256]{1,0:T(1,128)S(1)}, f32[1,256]{1,0:T(1,128)S(1)}, u32[]{:S(2)}, u32[]{:S(2)}) collective-permute-start(f32[1,256]{1,0:T(1,128)S(1)} %get-tuple-element.124.r0), channel_id=1, source_target_pairs={{0,4},{2,6},{4,0},{6,2},{1,5},{3,7},{5,1},{7,3},{8,12},{10,14},{12... | collective-permute-start | bytes 3080 | tf_op jit(solution)/shard_map/ppermute | solution.py:616
  102.7 3.9 %collective-permute-start.27 = (f32[1,256]{1,0:T(1,128)S(1)}, f32[1,256]{1,0:T(1,128)S(1)}, u32[]{:S(2)}, u32[]{:S(2)}) collective-permute-start(f32[1,256]{1,0:T(1,128)S(1)} %get-tuple-element.124.r0), channel_id=1, source_target_pairs={{0,6},{2,4},{4,2},{6,0},{1,7},{3,5},{5,3},{7,1},{8,14},{10,12},{12... | collective-permute-start | bytes 3080 | tf_op jit(solution)/shard_map/ppermute | solution.py:616
  113.6 4.2 %collective-permute-start.29 = (f32[8,128]{1,0:T(8,128)S(1)}, f32[8,128]{1,0:T(8,128)S(1)}, u32[]{:S(2)}, u32[]{:S(2)}) collective-permute-start(f32[8,128]{1,0:T(8,128)S(1)} %get-tuple-element.129), channel_id=1, source_target_pairs={{0,1},{1,0},{2,3},{3,2},{4,5},{5,4},{6,7},{7,6},{8,9},{9,8},{10,11... | collective-permute-start | bytes 12296 | tf_op jit(solution)/shard_map/ppermute | solution.py:612
  114.3 3.5 %collective-permute-start.30 = (f32[8,128]{1,0:T(8,128)S(1)}, f32[8,128]{1,0:T(8,128)S(1)}, u32[]{:S(2)}, u32[]{:S(2)}) collective-permute-start(f32[8,128]{1,0:T(8,128)S(1)} %get-tuple-element.130), channel_id=1, source_target_pairs={{0,248},{8,16},{16,8},{24,32},{32,24},{40,48},{48,40},{56,64},{64,... | collective-permute-start | bytes 12296 | tf_op jit(solution)/shard_map/ppermute | solution.py:612
  116.6 4.0 %collective-permute-start.32 = (f32[8,128]{1,0:T(8,128)S(1)}, f32[8,128]{1,0:T(8,128)S(1)}, u32[]{:S(2)}, u32[]{:S(2)}) collective-permute-start(f32[8,128]{1,0:T(8,128)S(1)} %get-tuple-element.132), channel_id=1, source_target_pairs={{0,6},{2,4},{4,2},{6,0},{1,7},{3,5},{5,3},{7,1},{8,14},{10,12},{12... | collective-permute-start | bytes 12296 | tf_op jit(solution)/shard_map/ppermute | solution.py:612
  116.8 3.7 %collective-permute-start.33 = (f32[8,128]{1,0:T(8,128)S(1)}, f32[8,128]{1,0:T(8,128)S(1)}, u32[]{:S(2)}, u32[]{:S(2)}) collective-permute-start(f32[8,128]{1,0:T(8,128)S(1)} %get-tuple-element.133), channel_id=1, source_target_pairs={{0,8},{8,0},{16,24},{24,16},{32,40},{40,32},{48,56},{56,48},{64,72... | collective-permute-start | bytes 12296 | tf_op jit(solution)/shard_map/ppermute | solution.py:612
  121.8 6.1 %collective-permute-start.34 = (f32[8,128]{1,0:T(8,128)S(1)}, f32[8,128]{1,0:T(8,128)S(1)}, u32[]{:S(2)}, u32[]{:S(2)}) collective-permute-start(f32[8,128]{1,0:T(8,128)S(1)} %get-tuple-element.136), channel_id=1, source_target_pairs={{0,1},{1,0},{2,3},{3,2},{4,5},{5,4},{6,7},{7,6},{8,9},{9,8},{10,11... | collective-permute-start | bytes 12296 | tf_op jit(solution)/shard_map/ppermute | solution.py:612
  123.1 4.7 %collective-permute-start.35 = (f32[8,128]{1,0:T(8,128)S(1)}, f32[8,128]{1,0:T(8,128)S(1)}, u32[]{:S(2)}, u32[]{:S(2)}) collective-permute-start(f32[8,128]{1,0:T(8,128)S(1)} %get-tuple-element.137), channel_id=1, source_target_pairs={{0,248},{8,16},{16,8},{24,32},{32,24},{40,48},{48,40},{56,64},{64,... | collective-permute-start | bytes 12296 | tf_op jit(solution)/shard_map/ppermute | solution.py:612
  125.3 3.7 %collective-permute-start.37 = (f32[8,128]{1,0:T(8,128)S(1)}, f32[8,128]{1,0:T(8,128)S(1)}, u32[]{:S(2)}, u32[]{:S(2)}) collective-permute-start(f32[8,128]{1,0:T(8,128)S(1)} %get-tuple-element.139), channel_id=1, source_target_pairs={{0,6},{2,4},{4,2},{6,0},{1,7},{3,5},{5,3},{7,1},{8,14},{10,12},{12... | collective-permute-start | bytes 12296 | tf_op jit(solution)/shard_map/ppermute | solution.py:612
  (25 other events, 182.1 us)

commit v5 on v3

--- a/solution.py
+++ b/solution.py
@@ -75,6 +75,14 @@
 
 
 def stacked(values):
+    high = values.astype(jnp.bfloat16)
+    rest = values - high.astype(np.float32)
+    mid = rest.astype(jnp.bfloat16)
+    low = (rest - mid.astype(np.float32)).astype(jnp.bfloat16)
+    return np.concatenate([high, high, high, mid, mid, low], axis=0)
+
+
+def short_stacked(values):
     high = values.astype(jnp.bfloat16)
     low = (values - high.astype(np.float32)).astype(jnp.bfloat16)
     return np.concatenate([high, high, low], axis=0)
@@ -143,9 +151,10 @@
         consts[row : row + count, :lanes] = part
     return dict(
         consts=consts,
-        rise=np.concatenate([stacked(de), stacked(restrict)], axis=1),
+        rise=stacked(de),
+        restrict=short_stacked(restrict),
         lay=np.concatenate(
-            [lay.astype(jnp.bfloat16), stacked(np.ascontiguousarray(restrict.T))], axis=0
+            [lay.astype(jnp.bfloat16), short_stacked(np.ascontiguousarray(restrict.T))], axis=0
         ),
     )
 
@@ -154,19 +163,31 @@
     return jnp.dot(a, b, precision=HIGHEST, preferred_element_type=F32)
 
 
-def halves(values):
-    high = values.astype(jnp.bfloat16)
-    return high, (values - high.astype(F32)).astype(jnp.bfloat16)
+def thirds(values):
+    high = values.astype(jnp.bfloat16).astype(F32)
+    rest = values - high
+    mid = rest.astype(jnp.bfloat16).astype(F32)
+    return high, mid, rest - mid
 
 
 def left_stack(values):
+    high, mid, low = thirds(values)
+    return jnp.concatenate([high, mid, low, high, mid, high], axis=1).astype(jnp.bfloat16)
+
+
+def short_stack(values):
     high = values.astype(jnp.bfloat16).astype(F32)
     return jnp.concatenate([high, values - high, high], axis=1).astype(jnp.bfloat16)
 
 
 def right_stack(values):
-    high, low = halves(values)
-    return jnp.concatenate([high, low, high], axis=0)
+    high, mid, low = (part.astype(jnp.bfloat16) for part in thirds(values))
+    return jnp.concatenate([high, mid, low, high, mid, high], axis=0)
+
+
+def right_factor(values):
+    high, mid, low = thirds(values)
+    return jnp.concatenate([high, high, high, mid, mid, low], axis=1).astype(jnp.bfloat16)
 
 
 def dot(a, b):
@@ -187,8 +208,8 @@
     return jnp.concatenate(pieces, axis=0)
 
 
-def coarse_row(member, rise_ref, vector):
-    return jnp.sum(member * dot(left_stack(vector), rise_ref[:, GROWN:]), axis=0, keepdims=True)
+def coarse_row(member, restrict_ref, vector):
+    return jnp.sum(member * dot(short_stack(vector), restrict_ref[...]), axis=0, keepdims=True)
 
 
 def scalar_row(scalars):
@@ -205,9 +226,9 @@
 
 
 def coarse_values(coarse, cinv_ref, member_ref, lay_ref):
-    solved = dot(left_stack(coarse[:, :KC]), cinv_ref[...])
+    solved = dot(short_stack(coarse[:, :KC]), cinv_ref[...])
     solved = jnp.concatenate([solved, jnp.zeros((1, WIDE - KC), F32)], axis=1)
-    return dot(left_stack(member_ref[...] * solved), lay_ref[LAID:, :])
+    return dot(short_stack(member_ref[...] * solved), lay_ref[LAID:, :])
 
 
 def apply_blocks(turned_ref, parts):
@@ -284,9 +305,8 @@
         terms = terms * omask_ref[base : base + 2 * RW, :]
         laid += [terms[:RW], terms[RW:]]
     laid = jnp.concatenate(laid, axis=1)
-    high, low = halves(laid)
-    out = dot(jnp.concatenate([high, low], axis=0), lay_ref[first_face * 8 * FACE : LAID, :])
-    return out[:RW] + out[RW:]
+    out = dot(jnp.concatenate(thirds(laid), axis=0).astype(jnp.bfloat16), lay_ref[first_face * 8 * FACE : LAID, :])
+    return out[:RW] + (out[RW : 2 * RW] + out[2 * RW :])
 
 
 def halo_part(recv, rem, omask_ref, lay_ref):
@@ -302,7 +322,7 @@
     table_ref[...] = jnp.broadcast_to(scalar_row([total(rs * rs)]), table_ref.shape)
 
 
-def prepare_kernel(rs_ref, mass_ref, ints_ref, rise_ref, x_ref, massw_ref, member_ref, odd_ref, row_ref):
+def prepare_kernel(rs_ref, mass_ref, ints_ref, restrict_ref, x_ref, massw_ref, member_ref, odd_ref, row_ref):
     x_ref[...] = jnp.zeros_like(x_ref)
     massw_ref[...] = jnp.zeros_like(massw_ref)
     for e in range(ELEMS):
@@ -313,7 +333,7 @@
             massw_ref[row : row + 1, :] = mass_ref[e : e + 1, lanes]
     member = member_mask(ints_ref)
     member_ref[...] = member
-    row_ref[...] = coarse_row(member, rise_ref, x_ref[...])
+    row_ref[...] = coarse_row(member, restrict_ref, x_ref[...])
     for i in range(3):
         odd = (ints_ref[i, PLACE] % 2).astype(F32)
         odd_ref[i * STRIDE : (i + 1) * STRIDE, :] = jnp.full((STRIDE, 128), odd, F32)
@@ -355,7 +375,8 @@
     coef = exact_dot(expand, coef_ref[...])
     vmat_ref[...] = right_factor(exact_dot(coef[:, 80:104], vtile) * vmask)
     turned = cinv_ref[0, 0].T
-    high, low = halves(turned)
+    high = turned.astype(jnp.bfloat16)
+    low = (turned - high.astype(F32)).astype(jnp.bfloat16)
     cinv3_ref[...] = jnp.concatenate([high, high, low], axis=0)
     for e in range(ELEMS):
         turned_ref[e] = blocks_ref[e].T
@@ -400,11 +421,6 @@
     loc2_ref[...] = right_factor(amat_ref[2 * one :, one : 3 * one])
 
 
-def right_factor(values):
-    high = values.astype(jnp.bfloat16).astype(F32)
-    return jnp.concatenate([high, high, values - high], axis=1).astype(jnp.bfloat16)
-
-
 def coarse_kernel(r0, r1, r2, r3, cinv, member, lay, coarse_ref):
     coarse = (r0[...] + r1[...]) + (r2[...] + r3[...])
     coarse_ref[...] = coarse_values(coarse, cinv, member, lay)
@@ -416,7 +432,7 @@
 
 def finish_first(odd, first, rise, first_ref, grown_ref, sends):
     first_ref[...] = first
-    grown = dot(left_stack(first), rise[:, :GROWN])
+    grown = dot(left_stack(first), rise[...])
     grown_ref[...] = grown
     write_sends(odd, grown, sends)
 
@@ -479,7 +495,7 @@
     parts = two_parts(defect) if step == 2 else rounded(defect)
     search = first[...] + apply_blocks(blocks, parts)
     search_ref[...] = search
-    grown = dot(left_stack(search), rise[:, :GROWN])
+    grown = dot(left_stack(search), rise[...])
     grown_ref[...] = grown
     write_sends(odd, grown, sends)
 
@@ -490,10 +506,10 @@
     rem, omask, lay = refs[6:9], refs[9], refs[10]
     mapped = local[...] + halo_part(recv, rem, omask, lay)
     if step == 0:
-        member, rise, b0, w_ref, table_ref, row_ref = refs[11:]
+        member, restrict, b0, w_ref, table_ref, row_ref = refs[11:]
         scalars = [total(mapped * b0[...]), total(mapped * mapped)]
     elif step == 1:
-        member, rise, w_ref, row_ref = refs[11:]
+        member, restrict, w_ref, row_ref = refs[11:]
     else:
         b0, b1, w1, w_ref, table_ref = refs[11:]
         scalars = [total(w1[...] * b[...]) for b in (b0, b1, w1)]
@@ -503,7 +519,7 @@
     if step != 1:
         table_ref[...] = jnp.broadcast_to(scalar_row(scalars), table_ref.shape)
     if step != 2:
-        row_ref[...] = coarse_row(member[...], rise, mapped)
+        row_ref[...] = coarse_row(member[...], restrict, mapped)
 
 
 def inverse_sqrt(value):
@@ -661,13 +677,13 @@
     x, massw, member, odd, row = call(
         prepare_kernel,
         "prepare",
-        (right_side, mass, ints, t["rise"]),
+        (right_side, mass, ints, t["restrict"]),
         [vec, vec, (RW, WIDE), (3 * STRIDE, 128), (1, WIDE)],
         smem=(2,),
         raw=(0, 1, 3),
     )
     rows = span_rows(row)
-    pair = half_floats(2 * RW, 3 * 4 * RW)
+    pair = half_floats(2 * RW, 6 * 4 * RW)
     rem0, rem1, rem2, loc1, loc2, omask, vmat, cinv3, turned = call(
         setup_kernel,
         "setup",
@@ -683,11 +699,11 @@
         [
             pair,
             pair,
-            half_floats(2 * RW, 3 * 2 * RW),
+            half_floats(2 * RW, 6 * 2 * RW),
             pair,
             pair,
             (6 * RW, 8 * FACE),
-            half_floats(RW, 9 * RW),
+            half_floats(RW, 18 * RW),
             half_floats(3 * KC, KC),
             half_floats(*block_inverse.shape),
         ],
@@ -752,13 +768,13 @@
             image, table, row = call(
                 kernel,
                 "third0",
-                args + (member, t["rise"], basis[0]),
+                args + (member, t["restrict"], basis[0]),
                 [vec, table_shape, (1, WIDE)],
             )
             table = lax.all_to_all(table, AXES, 0, 0, tiled=True)
             rows = span_rows(row)
         elif step == 1:
-            image, row = call(kernel, "third1", args + (member, t["rise"]), [vec, (1, WIDE)])
+            image, row = call(kernel, "third1", args + (member, t["restrict"]), [vec, (1, WIDE)])
             rows = span_rows(row)
         else:
             image, table = call(kernel, "third2", args + tuple(basis), [vec, table_shape])

time: 139 us -> 140 us (level)
  transfers between devices with their start and end apart: 41 -> 41, of which waited for: 15 -> 14; matrix products, arithmetic and copies ran while one was open for 0% -> 0% of each run, Pallas kernels for 5% -> 5%
where the time goes in v5:
time: 140 us; the launch traced here: 139 us
  starting transfers between devices  76.2 us (54%)
  blocking collectives  22.7 us (16%)
  waiting for transfers between devices  19.1 us (14%)
  Pallas kernels  17.2 us (12%)
  local copies, waits for them, and re-layouts  2.98 us (2%)
    ppermute x30, starting transfers between devices, exchange(): return [lax.ppermute(x, axis, way) for x, (axis, way) in zip(sends, ways)]  38.4 us
    all_to_all x2, starting transfers between devices, body(): table = lax.all_to_all(table, AXES, 0, 0, tiled=True)  26.6 us
    all_to_all x1, blocking collectives, body(): table = lax.all_to_all(table, AXES, 0, 0, tiled=True)  22.7 us
    pallas_call x22, Pallas kernels, call(): pl.pallas_call(kernel, name=name, out_shape=[shape_of(out) for out in out...  17.2 us
    ppermute x9, starting transfers between devices, span_rows(): lax.ppermute(row, 'span', [(i, i ^ k) for i in range(n_span)])  11.2 us
    all_to_all x2, waiting for transfers between devices, body(): table = lax.all_to_all(table, AXES, 0, 0, tiled=True)  9.38 us
    ppermute x30, waiting for transfers between devices, exchange(): return [lax.ppermute(x, axis, way) for x, (axis, way) in zip(sends, ways)]  4.95 us
    ppermute x9, waiting for transfers between devices, span_rows(): lax.ppermute(row, 'span', [(i, i ^ k) for i in range(n_span)])  4.75 us
  transfers between devices with their start and end apart: 41, of which 14 were waited for; matrix products, arithmetic and copies ran while one was open for 0% of the time, Pallas kernels for 5%

profile of v5, /device:TPU:1, one launch (start us, length us, event | category | flops | bytes accessed | tf_op | source)
XLA Modules:
  0.0 139.4 jit_solution(18320773663695276615)
XLA Ops:
  2.1 15.7 %all-to-all-start = ((f32[256,1,128]{2,1,0:T(1,128)}), f32[256,1,128]{2,1,0:T(1,128)S(1)}, u32[]{:S(2)}, u32[]{:S(2)}) async-start(f32[256,1,128]{2,1,0:T(1,128)} %bitcast.7), calls=%async_computation | async-start | bytes 262144 | tf_op jit(solution)/shard_map/all_to_all | solution.py:676
  19.1 1.5 %collective-permute-start.2 = (f32[1,256]{1,0:T(1,128)S(1)}, f32[1,256]{1,0:T(1,128)S(1)}, u32[]{:S(2)}, u32[]{:S(2)}) collective-permute-start(f32[1,256]{1,0:T(1,128)S(1)} %get-tuple-element.72.r0), channel_id=1, source_target_pairs={{0,2},{2,0},{4,6},{6,4},{1,3},{3,1},{5,7},{7,5},{8,10},{10,8},{12,... | collective-permute-start | bytes 3080 | tf_op jit(solution)/shard_map/ppermute | solution.py:664
  20.6 1.8 %collective-permute-start.1 = (f32[1,256]{1,0:T(1,128)S(1)}, f32[1,256]{1,0:T(1,128)S(1)}, u32[]{:S(2)}, u32[]{:S(2)}) collective-permute-start(f32[1,256]{1,0:T(1,128)S(1)} %get-tuple-element.72.r0), channel_id=1, source_target_pairs={{0,6},{2,4},{4,2},{6,0},{1,7},{3,5},{5,3},{7,1},{8,14},{10,12},{12... | collective-permute-start | bytes 3080 | tf_op jit(solution)/shard_map/ppermute | solution.py:664
  25.0 1.4 %setup.1 = (bf16[64,768]{1,0:T(8,128)(2,1)S(1)}, bf16[64,768]{1,0:T(8,128)(2,1)S(1)}, bf16[64,384]{1,0:T(8,128)(2,1)S(1)}, bf16[64,768]{1,0:T(8,128)(2,1)S(1)}, ...) custom-call(s32[4,20]{1,0:T(4,128)S(1)} %concatenate.3.ints_ref, ...), custom_call_target="tpu_custom_call" | custom-call | tf_op jit(solution)/shard_map/setup/pallas_call | solution.py:599
  26.8 4.0 %all-to-all-done = f32[256,1,128]{2,1,0:T(1,128)S(1)} async-done(((f32[256,1,128]{2,1,0:T(1,128)}), f32[256,1,128]{2,1,0:T(1,128)S(1)}, u32[]{:S(2)}, u32[]{:S(2)}) %all-to-all-start) | async-done | bytes 131104 | tf_op jit(solution)/shard_map/all_to_all | solution.py:676
  32.4 2.1 %collective-permute-start.4 = (f32[8,128]{1,0:T(8,128)S(1)}, f32[8,128]{1,0:T(8,128)S(1)}, u32[]{:S(2)}, u32[]{:S(2)}) collective-permute-start(f32[8,128]{1,0:T(8,128)S(1)} %get-tuple-element.85), channel_id=1, source_target_pairs={{0,248},{8,16},{16,8},{24,32},{32,24},{40,48},{48,40},{56,64},{64,... | collective-permute-start | bytes 12296 | tf_op jit(solution)/shard_map/ppermute | solution.py:660
  34.9 1.5 %collective-permute-start.6 = (f32[8,128]{1,0:T(8,128)S(1)}, f32[8,128]{1,0:T(8,128)S(1)}, u32[]{:S(2)}, u32[]{:S(2)}) collective-permute-start(f32[8,128]{1,0:T(8,128)S(1)} %get-tuple-element.87), channel_id=1, source_target_pairs={{0,6},{2,4},{4,2},{6,0},{1,7},{3,5},{5,3},{7,1},{8,14},{10,12},{12... | collective-permute-start | bytes 12296 | tf_op jit(solution)/shard_map/ppermute | solution.py:660
  36.4 2.4 %collective-permute-start.7 = (f32[8,128]{1,0:T(8,128)S(1)}, f32[8,128]{1,0:T(8,128)S(1)}, u32[]{:S(2)}, u32[]{:S(2)}) collective-permute-start(f32[8,128]{1,0:T(8,128)S(1)} %get-tuple-element.88), channel_id=1, source_target_pairs={{0,8},{8,0},{16,24},{24,16},{32,40},{40,32},{48,56},{56,48},{64,72... | collective-permute-start | bytes 12296 | tf_op jit(solution)/shard_map/ppermute | solution.py:660
  40.9 1.8 %collective-permute-start.8 = (f32[8,128]{1,0:T(8,128)S(1)}, f32[8,128]{1,0:T(8,128)S(1)}, u32[]{:S(2)}, u32[]{:S(2)}) collective-permute-start(f32[8,128]{1,0:T(8,128)S(1)} %get-tuple-element.94), channel_id=1, source_target_pairs={{0,1},{1,0},{2,3},{3,2},{4,5},{5,4},{6,7},{7,6},{8,9},{9,8},{10,11... | collective-permute-start | bytes 12296 | tf_op jit(solution)/shard_map/ppermute | solution.py:660
  44.2 2.9 %collective-permute-start.12 = (f32[8,128]{1,0:T(8,128)S(1)}, f32[8,128]{1,0:T(8,128)S(1)}, u32[]{:S(2)}, u32[]{:S(2)}) collective-permute-start(f32[8,128]{1,0:T(8,128)S(1)} %get-tuple-element.98), channel_id=1, source_target_pairs={{0,8},{8,0},{16,24},{24,16},{32,40},{40,32},{48,56},{56,48},{64,72... | collective-permute-start | bytes 12296 | tf_op jit(solution)/shard_map/ppermute | solution.py:660
  47.9 1.4 third0.1
  49.3 10.9 %all-to-all-start.1 = ((f32[256,1,128]{2,1,0:T(1,128)}), f32[256,1,128]{2,1,0:T(1,128)S(1)}, u32[]{:S(2)}, u32[]{:S(2)}) async-start(f32[256,1,128]{2,1,0:T(1,128)} %bitcast.13), calls=%async_computation.1 | async-start | bytes 262144 | tf_op jit(solution)/shard_map/all_to_all | solution.py:774
  60.2 1.5 %collective-permute-start.15 = (f32[1,256]{1,0:T(1,128)S(1)}, f32[1,256]{1,0:T(1,128)S(1)}, u32[]{:S(2)}, u32[]{:S(2)}) collective-permute-start(f32[1,256]{1,0:T(1,128)S(1)} %get-tuple-element.101.r0), channel_id=1, source_target_pairs={{0,2},{2,0},{4,6},{6,4},{1,3},{3,1},{5,7},{7,5},{8,10},{10,8},{12,... | collective-permute-start | bytes 3080 | tf_op jit(solution)/shard_map/ppermute | solution.py:664
  61.7 1.8 %collective-permute-start.14 = (f32[1,256]{1,0:T(1,128)S(1)}, f32[1,256]{1,0:T(1,128)S(1)}, u32[]{:S(2)}, u32[]{:S(2)}) collective-permute-start(f32[1,256]{1,0:T(1,128)S(1)} %get-tuple-element.101.r0), channel_id=1, source_target_pairs={{0,6},{2,4},{4,2},{6,0},{1,7},{3,5},{5,3},{7,1},{8,14},{10,12},{12... | collective-permute-start | bytes 3080 | tf_op jit(solution)/shard_map/ppermute | solution.py:664
  65.3 2.1 %collective-permute-done.13.r1 = f32[1,256]{1,0:T(1,128)S(1)} collective-permute-done((f32[1,256]{1,0:T(1,128)S(1)}, f32[1,256]{1,0:T(1,128)S(1)}, u32[]{:S(2)}, u32[]{:S(2)}) %collective-permute-start.13) | collective-permute-done | bytes 1056 | tf_op jit(solution)/shard_map/ppermute | solution.py:664
  67.8 5.4 %all-to-all-done.1 = f32[256,1,128]{2,1,0:T(1,128)S(1)} async-done(((f32[256,1,128]{2,1,0:T(1,128)}), f32[256,1,128]{2,1,0:T(1,128)S(1)}, u32[]{:S(2)}, u32[]{:S(2)}) %all-to-all-start.1) | async-done | bytes 131104 | tf_op jit(solution)/shard_map/all_to_all | solution.py:774
  74.8 2.0 %collective-permute-start.17 = (f32[8,128]{1,0:T(8,128)S(1)}, f32[8,128]{1,0:T(8,128)S(1)}, u32[]{:S(2)}, u32[]{:S(2)}) collective-permute-start(f32[8,128]{1,0:T(8,128)S(1)} %get-tuple-element.107), channel_id=1, source_target_pairs={{0,248},{8,16},{16,8},{24,32},{32,24},{40,48},{48,40},{56,64},{64,... | collective-permute-start | bytes 12296 | tf_op jit(solution)/shard_map/ppermute | solution.py:660
  79.3 1.5 %collective-permute-done.19.refs_7_ = f32[8,128]{1,0:T(8,128)S(1)} collective-permute-done((f32[8,128]{1,0:T(8,128)S(1)}, f32[8,128]{1,0:T(8,128)S(1)}, u32[]{:S(2)}, u32[]{:S(2)}) %collective-permute-start.19) | collective-permute-done | bytes 4128 | tf_op jit(solution)/shard_map/ppermute | solution.py:660
  80.8 1.2 second1.1
  82.0 1.7 %collective-permute-start.21 = (f32[8,128]{1,0:T(8,128)S(1)}, f32[8,128]{1,0:T(8,128)S(1)}, u32[]{:S(2)}, u32[]{:S(2)}) collective-permute-start(f32[8,128]{1,0:T(8,128)S(1)} %get-tuple-element.113), channel_id=1, source_target_pairs={{0,1},{1,0},{2,3},{3,2},{4,5},{5,4},{6,7},{7,6},{8,9},{9,8},{10,11... | collective-permute-start | bytes 12296 | tf_op jit(solution)/shard_map/ppermute | solution.py:660
  83.7 2.2 %collective-permute-start.22 = (f32[8,128]{1,0:T(8,128)S(1)}, f32[8,128]{1,0:T(8,128)S(1)}, u32[]{:S(2)}, u32[]{:S(2)}) collective-permute-start(f32[8,128]{1,0:T(8,128)S(1)} %get-tuple-element.114), channel_id=1, source_target_pairs={{0,248},{8,16},{16,8},{24,32},{32,24},{40,48},{48,40},{56,64},{64,... | collective-permute-start | bytes 12296 | tf_op jit(solution)/shard_map/ppermute | solution.py:660
  86.6 1.3 collective-permute-start.25
  88.5 1.4 %collective-permute-done.24.refs_4_ = f32[8,128]{1,0:T(8,128)S(1)} collective-permute-done((f32[8,128]{1,0:T(8,128)S(1)}, f32[8,128]{1,0:T(8,128)S(1)}, u32[]{:S(2)}, u32[]{:S(2)}) %collective-permute-start.24) | collective-permute-done | bytes 4128 | tf_op jit(solution)/shard_map/ppermute | solution.py:660
  92.0 2.1 %collective-permute-start.26 = (f32[1,256]{1,0:T(1,128)S(1)}, f32[1,256]{1,0:T(1,128)S(1)}, u32[]{:S(2)}, u32[]{:S(2)}) collective-permute-start(f32[1,256]{1,0:T(1,128)S(1)} %get-tuple-element.119.r0), channel_id=1, source_target_pairs={{0,4},{2,6},{4,0},{6,2},{1,5},{3,7},{5,1},{7,3},{8,12},{10,14},{12... | collective-permute-start | bytes 3080 | tf_op jit(solution)/shard_map/ppermute | solution.py:664
  96.6 2.8 %collective-permute-start.29 = (f32[8,128]{1,0:T(8,128)S(1)}, f32[8,128]{1,0:T(8,128)S(1)}, u32[]{:S(2)}, u32[]{:S(2)}) collective-permute-start(f32[8,128]{1,0:T(8,128)S(1)} %get-tuple-element.122), channel_id=1, source_target_pairs={{0,1},{1,0},{2,3},{3,2},{4,5},{5,4},{6,7},{7,6},{8,9},{9,8},{10,11... | collective-permute-start | bytes 12296 | tf_op jit(solution)/shard_map/ppermute | solution.py:660
  101.2 2.1 %collective-permute-start.32 = (f32[8,128]{1,0:T(8,128)S(1)}, f32[8,128]{1,0:T(8,128)S(1)}, u32[]{:S(2)}, u32[]{:S(2)}) collective-permute-start(f32[8,128]{1,0:T(8,128)S(1)} %get-tuple-element.125), channel_id=1, source_target_pairs={{0,6},{2,4},{4,2},{6,0},{1,7},{3,5},{5,3},{7,1},{8,14},{10,12},{12... | collective-permute-start | bytes 12296 | tf_op jit(solution)/shard_map/ppermute | solution.py:660
  103.3 2.2 %collective-permute-start.33 = (f32[8,128]{1,0:T(8,128)S(1)}, f32[8,128]{1,0:T(8,128)S(1)}, u32[]{:S(2)}, u32[]{:S(2)}) collective-permute-start(f32[8,128]{1,0:T(8,128)S(1)} %get-tuple-element.126), channel_id=1, source_target_pairs={{0,8},{8,0},{16,24},{24,16},{32,40},{40,32},{48,56},{56,48},{64,72... | collective-permute-start | bytes 12296 | tf_op jit(solution)/shard_map/ppermute | solution.py:660
  106.3 1.3 second2.1
  108.5 1.5 %collective-permute-start.35 = (f32[8,128]{1,0:T(8,128)S(1)}, f32[8,128]{1,0:T(8,128)S(1)}, u32[]{:S(2)}, u32[]{:S(2)}) collective-permute-start(f32[8,128]{1,0:T(8,128)S(1)} %get-tuple-element.130), channel_id=1, source_target_pairs={{0,248},{8,16},{16,8},{24,32},{32,24},{40,48},{48,40},{56,64},{64,... | collective-permute-start | bytes 12296 | tf_op jit(solution)/shard_map/ppermute | solution.py:660
  110.0 1.7 %collective-permute-start.37 = (f32[8,128]{1,0:T(8,128)S(1)}, f32[8,128]{1,0:T(8,128)S(1)}, u32[]{:S(2)}, u32[]{:S(2)}) collective-permute-start(f32[8,128]{1,0:T(8,128)S(1)} %get-tuple-element.132), channel_id=1, source_target_pairs={{0,6},{2,4},{4,2},{6,0},{1,7},{3,5},{5,3},{7,1},{8,14},{10,12},{12... | collective-permute-start | bytes 12296 | tf_op jit(solution)/shard_map/ppermute | solution.py:660
  111.7 2.5 %collective-permute-start.38 = (f32[8,128]{1,0:T(8,128)S(1)}, f32[8,128]{1,0:T(8,128)S(1)}, u32[]{:S(2)}, u32[]{:S(2)}) collective-permute-start(f32[8,128]{1,0:T(8,128)S(1)} %get-tuple-element.133), channel_id=1, source_target_pairs={{0,8},{8,0},{16,24},{24,16},{32,40},{40,32},{48,56},{56,48},{64,72... | collective-permute-start | bytes 12296 | tf_op jit(solution)/shard_map/ppermute | solution.py:660
  115.8 22.7 %all_to_all.33 = f32[256,1,128]{2,1,0:T(1,128)S(1)} all-to-all(f32[256,1,128]{2,1,0:T(1,128)S(1)} %bitcast.25), channel_id=1, replica_groups=mesh['passage'=32,'span'=4,'radial'=2] {'passage','span','radial'}, dimensions={0} | all-to-all | bytes 262144 | tf_op jit(solution)/shard_map/all_to_all | solution.py:781
  (109 shorter events, 30.0 us)
Async XLA Ops:
  2.1 28.7 %all-to-all-start = ((f32[256,1,128]{2,1,0:T(1,128)}), f32[256,1,128]{2,1,0:T(1,128)S(1)}, u32[]{:S(2)}, u32[]{:S(2)}) async-start(f32[256,1,128]{2,1,0:T(1,128)} %bitcast.7), calls=%async_computation | async-start | bytes 262144 | tf_op jit(solution)/shard_map/all_to_all | solution.py:676
  19.1 7.3 %collective-permute-start.2 = (f32[1,256]{1,0:T(1,128)S(1)}, f32[1,256]{1,0:T(1,128)S(1)}, u32[]{:S(2)}, u32[]{:S(2)}) collective-permute-start(f32[1,256]{1,0:T(1,128)S(1)} %get-tuple-element.72.r0), channel_id=1, source_target_pairs={{0,2},{2,0},{4,6},{6,4},{1,3},{3,1},{5,7},{7,5},{8,10},{10,8},{12,... | collective-permute-start | bytes 3080 | tf_op jit(solution)/shard_map/ppermute | solution.py:664
  20.6 5.9 %collective-permute-start.1 = (f32[1,256]{1,0:T(1,128)S(1)}, f32[1,256]{1,0:T(1,128)S(1)}, u32[]{:S(2)}, u32[]{:S(2)}) collective-permute-start(f32[1,256]{1,0:T(1,128)S(1)} %get-tuple-element.72.r0), channel_id=1, source_target_pairs={{0,6},{2,4},{4,2},{6,0},{1,7},{3,5},{5,3},{7,1},{8,14},{10,12},{12... | collective-permute-start | bytes 3080 | tf_op jit(solution)/shard_map/ppermute | solution.py:664
  22.3 4.1 %collective-permute-start = (f32[1,256]{1,0:T(1,128)S(1)}, f32[1,256]{1,0:T(1,128)S(1)}, u32[]{:S(2)}, u32[]{:S(2)}) collective-permute-start(f32[1,256]{1,0:T(1,128)S(1)} %get-tuple-element.72.r0), channel_id=1, source_target_pairs={{0,4},{2,6},{4,0},{6,2},{1,5},{3,7},{5,1},{7,3},{8,12},{10,14},{12... | collective-permute-start | bytes 3080 | tf_op jit(solution)/shard_map/ppermute | solution.py:664
  31.6 7.8 %collective-permute-start.3 = (f32[8,128]{1,0:T(8,128)S(1)}, f32[8,128]{1,0:T(8,128)S(1)}, u32[]{:S(2)}, u32[]{:S(2)}) collective-permute-start(f32[8,128]{1,0:T(8,128)S(1)} %get-tuple-element.84), channel_id=1, source_target_pairs={{0,1},{1,0},{2,3},{3,2},{4,5},{5,4},{6,7},{7,6},{8,9},{9,8},{10,11... | collective-permute-start | bytes 12296 | tf_op jit(solution)/shard_map/ppermute | solution.py:660
  32.4 7.0 %collective-permute-start.4 = (f32[8,128]{1,0:T(8,128)S(1)}, f32[8,128]{1,0:T(8,128)S(1)}, u32[]{:S(2)}, u32[]{:S(2)}) collective-permute-start(f32[8,128]{1,0:T(8,128)S(1)} %get-tuple-element.85), channel_id=1, source_target_pairs={{0,248},{8,16},{16,8},{24,32},{32,24},{40,48},{48,40},{56,64},{64,... | collective-permute-start | bytes 12296 | tf_op jit(solution)/shard_map/ppermute | solution.py:660
  34.5 4.9 %collective-permute-start.5 = (f32[8,128]{1,0:T(8,128)S(1)}, f32[8,128]{1,0:T(8,128)S(1)}, u32[]{:S(2)}, u32[]{:S(2)}) collective-permute-start(f32[8,128]{1,0:T(8,128)S(1)} %get-tuple-element.86), channel_id=1, source_target_pairs={{0,2},{2,0},{4,6},{6,4},{1,3},{3,1},{5,7},{7,5},{8,10},{10,8},{12,... | collective-permute-start | bytes 12296 | tf_op jit(solution)/shard_map/ppermute | solution.py:660
  34.9 4.6 %collective-permute-start.6 = (f32[8,128]{1,0:T(8,128)S(1)}, f32[8,128]{1,0:T(8,128)S(1)}, u32[]{:S(2)}, u32[]{:S(2)}) collective-permute-start(f32[8,128]{1,0:T(8,128)S(1)} %get-tuple-element.87), channel_id=1, source_target_pairs={{0,6},{2,4},{4,2},{6,0},{1,7},{3,5},{5,3},{7,1},{8,14},{10,12},{12... | collective-permute-start | bytes 12296 | tf_op jit(solution)/shard_map/ppermute | solution.py:660
  40.9 6.7 %collective-permute-start.8 = (f32[8,128]{1,0:T(8,128)S(1)}, f32[8,128]{1,0:T(8,128)S(1)}, u32[]{:S(2)}, u32[]{:S(2)}) collective-permute-start(f32[8,128]{1,0:T(8,128)S(1)} %get-tuple-element.94), channel_id=1, source_target_pairs={{0,1},{1,0},{2,3},{3,2},{4,5},{5,4},{6,7},{7,6},{8,9},{9,8},{10,11... | collective-permute-start | bytes 12296 | tf_op jit(solution)/shard_map/ppermute | solution.py:660
  42.8 4.9 %collective-permute-start.9 = (f32[8,128]{1,0:T(8,128)S(1)}, f32[8,128]{1,0:T(8,128)S(1)}, u32[]{:S(2)}, u32[]{:S(2)}) collective-permute-start(f32[8,128]{1,0:T(8,128)S(1)} %get-tuple-element.95), channel_id=1, source_target_pairs={{0,248},{8,16},{16,8},{24,32},{32,24},{40,48},{48,40},{56,64},{64,... | collective-permute-start | bytes 12296 | tf_op jit(solution)/shard_map/ppermute | solution.py:660
  43.5 4.1 %collective-permute-start.10 = (f32[8,128]{1,0:T(8,128)S(1)}, f32[8,128]{1,0:T(8,128)S(1)}, u32[]{:S(2)}, u32[]{:S(2)}) collective-permute-start(f32[8,128]{1,0:T(8,128)S(1)} %get-tuple-element.96), channel_id=1, source_target_pairs={{0,2},{2,0},{4,6},{6,4},{1,3},{3,1},{5,7},{7,5},{8,10},{10,8},{12,... | collective-permute-start | bytes 12296 | tf_op jit(solution)/shard_map/ppermute | solution.py:660
  43.5 4.1 %collective-permute-start.11 = (f32[8,128]{1,0:T(8,128)S(1)}, f32[8,128]{1,0:T(8,128)S(1)}, u32[]{:S(2)}, u32[]{:S(2)}) collective-permute-start(f32[8,128]{1,0:T(8,128)S(1)} %get-tuple-element.97), channel_id=1, source_target_pairs={{0,6},{2,4},{4,2},{6,0},{1,7},{3,5},{5,3},{7,1},{8,14},{10,12},{12... | collective-permute-start | bytes 12296 | tf_op jit(solution)/shard_map/ppermute | solution.py:660
  44.2 3.7 %collective-permute-start.12 = (f32[8,128]{1,0:T(8,128)S(1)}, f32[8,128]{1,0:T(8,128)S(1)}, u32[]{:S(2)}, u32[]{:S(2)}) collective-permute-start(f32[8,128]{1,0:T(8,128)S(1)} %get-tuple-element.98), channel_id=1, source_target_pairs={{0,8},{8,0},{16,24},{24,16},{32,40},{40,32},{48,56},{56,48},{64,72... | collective-permute-start | bytes 12296 | tf_op jit(solution)/shard_map/ppermute | solution.py:660
  49.3 23.9 %all-to-all-start.1 = ((f32[256,1,128]{2,1,0:T(1,128)}), f32[256,1,128]{2,1,0:T(1,128)S(1)}, u32[]{:S(2)}, u32[]{:S(2)}) async-start(f32[256,1,128]{2,1,0:T(1,128)} %bitcast.13), calls=%async_computation.1 | async-start | bytes 262144 | tf_op jit(solution)/shard_map/all_to_all | solution.py:774
  60.2 3.9 %collective-permute-start.15 = (f32[1,256]{1,0:T(1,128)S(1)}, f32[1,256]{1,0:T(1,128)S(1)}, u32[]{:S(2)}, u32[]{:S(2)}) collective-permute-start(f32[1,256]{1,0:T(1,128)S(1)} %get-tuple-element.101.r0), channel_id=1, source_target_pairs={{0,2},{2,0},{4,6},{6,4},{1,3},{3,1},{5,7},{7,5},{8,10},{10,8},{12,... | collective-permute-start | bytes 3080 | tf_op jit(solution)/shard_map/ppermute | solution.py:664
  61.7 3.6 %collective-permute-start.14 = (f32[1,256]{1,0:T(1,128)S(1)}, f32[1,256]{1,0:T(1,128)S(1)}, u32[]{:S(2)}, u32[]{:S(2)}) collective-permute-start(f32[1,256]{1,0:T(1,128)S(1)} %get-tuple-element.101.r0), channel_id=1, source_target_pairs={{0,6},{2,4},{4,2},{6,0},{1,7},{3,5},{5,3},{7,1},{8,14},{10,12},{12... | collective-permute-start | bytes 3080 | tf_op jit(solution)/shard_map/ppermute | solution.py:664
  63.5 3.9 %collective-permute-start.13 = (f32[1,256]{1,0:T(1,128)S(1)}, f32[1,256]{1,0:T(1,128)S(1)}, u32[]{:S(2)}, u32[]{:S(2)}) collective-permute-start(f32[1,256]{1,0:T(1,128)S(1)} %get-tuple-element.101.r0), channel_id=1, source_target_pairs={{0,4},{2,6},{4,0},{6,2},{1,5},{3,7},{5,1},{7,3},{8,12},{10,14},{12... | collective-permute-start | bytes 3080 | tf_op jit(solution)/shard_map/ppermute | solution.py:664
  74.0 4.2 %collective-permute-start.16 = (f32[8,128]{1,0:T(8,128)S(1)}, f32[8,128]{1,0:T(8,128)S(1)}, u32[]{:S(2)}, u32[]{:S(2)}) collective-permute-start(f32[8,128]{1,0:T(8,128)S(1)} %get-tuple-element.106), channel_id=1, source_target_pairs={{0,1},{1,0},{2,3},{3,2},{4,5},{5,4},{6,7},{7,6},{8,9},{9,8},{10,11... | collective-permute-start | bytes 12296 | tf_op jit(solution)/shard_map/ppermute | solution.py:660
  77.1 3.7 %collective-permute-start.19 = (f32[8,128]{1,0:T(8,128)S(1)}, f32[8,128]{1,0:T(8,128)S(1)}, u32[]{:S(2)}, u32[]{:S(2)}) collective-permute-start(f32[8,128]{1,0:T(8,128)S(1)} %get-tuple-element.109), channel_id=1, source_target_pairs={{0,6},{2,4},{4,2},{6,0},{1,7},{3,5},{5,3},{7,1},{8,14},{10,12},{12... | collective-permute-start | bytes 12296 | tf_op jit(solution)/shard_map/ppermute | solution.py:660
  82.0 6.4 %collective-permute-start.21 = (f32[8,128]{1,0:T(8,128)S(1)}, f32[8,128]{1,0:T(8,128)S(1)}, u32[]{:S(2)}, u32[]{:S(2)}) collective-permute-start(f32[8,128]{1,0:T(8,128)S(1)} %get-tuple-element.113), channel_id=1, source_target_pairs={{0,1},{1,0},{2,3},{3,2},{4,5},{5,4},{6,7},{7,6},{8,9},{9,8},{10,11... | collective-permute-start | bytes 12296 | tf_op jit(solution)/shard_map/ppermute | solution.py:660
  83.7 4.8 %collective-permute-start.22 = (f32[8,128]{1,0:T(8,128)S(1)}, f32[8,128]{1,0:T(8,128)S(1)}, u32[]{:S(2)}, u32[]{:S(2)}) collective-permute-start(f32[8,128]{1,0:T(8,128)S(1)} %get-tuple-element.114), channel_id=1, source_target_pairs={{0,248},{8,16},{16,8},{24,32},{32,24},{40,48},{48,40},{56,64},{64,... | collective-permute-start | bytes 12296 | tf_op jit(solution)/shard_map/ppermute | solution.py:660
  85.9 4.0 %collective-permute-start.24 = (f32[8,128]{1,0:T(8,128)S(1)}, f32[8,128]{1,0:T(8,128)S(1)}, u32[]{:S(2)}, u32[]{:S(2)}) collective-permute-start(f32[8,128]{1,0:T(8,128)S(1)} %get-tuple-element.116), channel_id=1, source_target_pairs={{0,6},{2,4},{4,2},{6,0},{1,7},{3,5},{5,3},{7,1},{8,14},{10,12},{12... | collective-permute-start | bytes 12296 | tf_op jit(solution)/shard_map/ppermute | solution.py:660
  90.7 3.7 %collective-permute-start.28 = (f32[1,256]{1,0:T(1,128)S(1)}, f32[1,256]{1,0:T(1,128)S(1)}, u32[]{:S(2)}, u32[]{:S(2)}) collective-permute-start(f32[1,256]{1,0:T(1,128)S(1)} %get-tuple-element.119.r0), channel_id=1, source_target_pairs={{0,2},{2,0},{4,6},{6,4},{1,3},{3,1},{5,7},{7,5},{8,10},{10,8},{12,... | collective-permute-start | bytes 3080 | tf_op jit(solution)/shard_map/ppermute | solution.py:664
  92.0 3.9 %collective-permute-start.26 = (f32[1,256]{1,0:T(1,128)S(1)}, f32[1,256]{1,0:T(1,128)S(1)}, u32[]{:S(2)}, u32[]{:S(2)}) collective-permute-start(f32[1,256]{1,0:T(1,128)S(1)} %get-tuple-element.119.r0), channel_id=1, source_target_pairs={{0,4},{2,6},{4,0},{6,2},{1,5},{3,7},{5,1},{7,3},{8,12},{10,14},{12... | collective-permute-start | bytes 3080 | tf_op jit(solution)/shard_map/ppermute | solution.py:664
  96.6 9.5 %collective-permute-start.29 = (f32[8,128]{1,0:T(8,128)S(1)}, f32[8,128]{1,0:T(8,128)S(1)}, u32[]{:S(2)}, u32[]{:S(2)}) collective-permute-start(f32[8,128]{1,0:T(8,128)S(1)} %get-tuple-element.122), channel_id=1, source_target_pairs={{0,1},{1,0},{2,3},{3,2},{4,5},{5,4},{6,7},{7,6},{8,9},{9,8},{10,11... | collective-permute-start | bytes 12296 | tf_op jit(solution)/shard_map/ppermute | solution.py:660
  99.3 6.7 %collective-permute-start.30 = (f32[8,128]{1,0:T(8,128)S(1)}, f32[8,128]{1,0:T(8,128)S(1)}, u32[]{:S(2)}, u32[]{:S(2)}) collective-permute-start(f32[8,128]{1,0:T(8,128)S(1)} %get-tuple-element.123), channel_id=1, source_target_pairs={{0,248},{8,16},{16,8},{24,32},{32,24},{40,48},{48,40},{56,64},{64,... | collective-permute-start | bytes 12296 | tf_op jit(solution)/shard_map/ppermute | solution.py:660
  100.2 5.9 %collective-permute-start.31 = (f32[8,128]{1,0:T(8,128)S(1)}, f32[8,128]{1,0:T(8,128)S(1)}, u32[]{:S(2)}, u32[]{:S(2)}) collective-permute-start(f32[8,128]{1,0:T(8,128)S(1)} %get-tuple-element.124), channel_id=1, source_target_pairs={{0,2},{2,0},{4,6},{6,4},{1,3},{3,1},{5,7},{7,5},{8,10},{10,8},{12,... | collective-permute-start | bytes 12296 | tf_op jit(solution)/shard_map/ppermute | solution.py:660
  101.2 4.9 %collective-permute-start.32 = (f32[8,128]{1,0:T(8,128)S(1)}, f32[8,128]{1,0:T(8,128)S(1)}, u32[]{:S(2)}, u32[]{:S(2)}) collective-permute-start(f32[8,128]{1,0:T(8,128)S(1)} %get-tuple-element.125), channel_id=1, source_target_pairs={{0,6},{2,4},{4,2},{6,0},{1,7},{3,5},{5,3},{7,1},{8,14},{10,12},{12... | collective-permute-start | bytes 12296 | tf_op jit(solution)/shard_map/ppermute | solution.py:660
  107.6 7.2 %collective-permute-start.34 = (f32[8,128]{1,0:T(8,128)S(1)}, f32[8,128]{1,0:T(8,128)S(1)}, u32[]{:S(2)}, u32[]{:S(2)}) collective-permute-start(f32[8,128]{1,0:T(8,128)S(1)} %get-tuple-element.129), channel_id=1, source_target_pairs={{0,1},{1,0},{2,3},{3,2},{4,5},{5,4},{6,7},{7,6},{8,9},{9,8},{10,11... | collective-permute-start | bytes 12296 | tf_op jit(solution)/shard_map/ppermute | solution.py:660
  108.5 6.3 %collective-permute-start.35 = (f32[8,128]{1,0:T(8,128)S(1)}, f32[8,128]{1,0:T(8,128)S(1)}, u32[]{:S(2)}, u32[]{:S(2)}) collective-permute-start(f32[8,128]{1,0:T(8,128)S(1)} %get-tuple-element.130), channel_id=1, source_target_pairs={{0,248},{8,16},{16,8},{24,32},{32,24},{40,48},{48,40},{56,64},{64,... | collective-permute-start | bytes 12296 | tf_op jit(solution)/shard_map/ppermute | solution.py:660
  110.0 4.8 %collective-permute-start.36 = (f32[8,128]{1,0:T(8,128)S(1)}, f32[8,128]{1,0:T(8,128)S(1)}, u32[]{:S(2)}, u32[]{:S(2)}) collective-permute-start(f32[8,128]{1,0:T(8,128)S(1)} %get-tuple-element.131), channel_id=1, source_target_pairs={{0,2},{2,0},{4,6},{6,4},{1,3},{3,1},{5,7},{7,5},{8,10},{10,8},{12,... | collective-permute-start | bytes 12296 | tf_op jit(solution)/shard_map/ppermute | solution.py:660
  110.0 4.8 %collective-permute-start.37 = (f32[8,128]{1,0:T(8,128)S(1)}, f32[8,128]{1,0:T(8,128)S(1)}, u32[]{:S(2)}, u32[]{:S(2)}) collective-permute-start(f32[8,128]{1,0:T(8,128)S(1)} %get-tuple-element.132), channel_id=1, source_target_pairs={{0,6},{2,4},{4,2},{6,0},{1,7},{3,5},{5,3},{7,1},{8,14},{10,12},{12... | collective-permute-start | bytes 12296 | tf_op jit(solution)/shard_map/ppermute | solution.py:660
  (25 other events, 206.2 us)

commit v6 on v5

--- a/solution.py
+++ b/solution.py
@@ -23,7 +23,7 @@
 AXES = ("passage", "span", "radial")
 NEIGH, ORIENT, TAGS, GROUP, PLACE = 0, 6, 12, 18, 19
 HIGHEST = lax.Precision.HIGHEST
-GROWN = 3 * NODES + 6 * 2 * FACE
+GROWN = 6 * 2 * FACE
 LAID = 6 * 8 * FACE
 CONSTS = ((0, 80, 256), (80, 8, 256), (88, 8, 256), (96, 24, 96), (120, 32, 96), (152, 32, 24))
 F32 = jnp.float32
@@ -102,7 +102,7 @@
         for face in range(6):
             axis = face // 2
             spot = others(node, axis)
-            base = 3 * NODES + face * 2 * FACE
+            base = 3 * NODES + (face - 2) % 6 * 2 * FACE
             de[node, base + FACE + spot] = dmat[layer_of(face), coords(node)[axis]]
             if coords(node)[axis] == layer_of(face):
                 de[node, base + spot] = 1.0
@@ -151,7 +151,8 @@
         consts[row : row + count, :lanes] = part
     return dict(
         consts=consts,
-        rise=stacked(de),
+        rise=stacked(de[:, 3 * NODES :]),
+        slope=stacked(de[:, : 3 * NODES]),
         restrict=short_stacked(restrict),
         lay=np.concatenate(
             [lay.astype(jnp.bfloat16), short_stacked(np.ascontiguousarray(restrict.T))], axis=0
@@ -259,7 +260,7 @@
 
 
 def face_of(grown, face):
-    base = 3 * NODES + face * 2 * FACE
+    base = (face - 2) % 6 * 2 * FACE
     return grown[:, base : base + 2 * FACE]
 
 
@@ -470,20 +471,23 @@
     finish_first(odd, first, rise, first_ref, grown_ref, sends)
 
 
-def local_kernel(x, grown_ref, mass, vmat, loc1, loc2, omask, lay, out_ref):
-    grown = grown_ref[...]
-    slopes = jnp.concatenate([grown[:, i * NODES : (i + 1) * NODES] for i in range(3)], axis=0)
+def local_kernel(x, grown_ref, mass, vmat, loc1, loc2, omask, lay, slope, out_ref):
+    tile = grown_ref[:, :128]
+    slopes = dot(left_stack(x[...]), slope[...])
+    slopes = jnp.concatenate([slopes[:, i * NODES : (i + 1) * NODES] for i in range(3)], axis=0)
     result = 1.5 * mass[...] * x[...] + dot(vmat[...], right_stack(slopes))
     groups = []
     for faces, mat in (((2, 3), loc1), ((4, 5), loc2)):
         pieces = []
         for f in faces:
-            base = 3 * NODES + f * 2 * FACE
-            tile = grown[:, base // 128 * 128 : base // 128 * 128 + 128]
-            slot = base % 128 // FACE
+            slot = (f - 2) * 2
             pieces += [copies(tile, slot), copies(tile, slot + 1)]
         groups.append(dot(mat[...], right_stack(jnp.concatenate(pieces, axis=0))))
     out_ref[...] = result + place_terms(groups, omask, lay, 2)
+
+
+def row_kernel(x, member, restrict, row_ref):
+    row_ref[...] = coarse_row(member[...], restrict, x[...])
 
 
 def second_kernel(step, *refs):
@@ -506,7 +510,7 @@
     rem, omask, lay = refs[6:9], refs[9], refs[10]
     mapped = local[...] + halo_part(recv, rem, omask, lay)
     if step == 0:
-        member, restrict, b0, w_ref, table_ref, row_ref = refs[11:]
+        b0, w_ref, table_ref = refs[11:]
         scalars = [total(mapped * b0[...]), total(mapped * mapped)]
     elif step == 1:
         member, restrict, w_ref, row_ref = refs[11:]
@@ -518,7 +522,7 @@
     w_ref[...] = mapped
     if step != 1:
         table_ref[...] = jnp.broadcast_to(scalar_row(scalars), table_ref.shape)
-    if step != 2:
+    if step == 1:
         row_ref[...] = coarse_row(member[...], restrict, mapped)
 
 
@@ -712,7 +716,7 @@
         scratch=[(24, 104), (6 * RW, 256)],
     )
     remote = (rem0, rem1, rem2, omask, t["lay"])
-    near = (massw, vmat, loc1, loc2, omask, t["lay"])
+    near = (massw, vmat, loc1, loc2, omask, t["lay"], t["slope"])
 
     def local_part(vector, grown, step):
         return call(local_kernel, "local%d" % step, (vector, grown) + near, [vec])[0]
@@ -765,13 +769,9 @@
         kernel = with_step(third_kernel, step)
         args = (local, *recv) + remote
         if step == 0:
-            image, table, row = call(
-                kernel,
-                "third0",
-                args + (member, t["restrict"], basis[0]),
-                [vec, table_shape, (1, WIDE)],
-            )
+            image, table = call(kernel, "third0", args + (basis[0],), [vec, table_shape])
             table = lax.all_to_all(table, AXES, 0, 0, tiled=True)
+            (row,) = call(row_kernel, "row0", (image, member, t["restrict"]), [(1, WIDE)])
             rows = span_rows(row)
         elif step == 1:
             image, row = call(kernel, "third1", args + (member, t["restrict"]), [vec, (1, WIDE)])

time: 140 us -> 139 us (level)
    pallas_call x22 -> x23, Pallas kernels: 17.2 us -> 18.3 us  [call(): pl.pallas_call(kernel, name=name, out_shape=[shape_of(out) for out in out...]
  transfers between devices with their start and end apart: 41 -> 41, of which waited for: 14 -> 14; matrix products, arithmetic and copies ran while one was open for 0% -> 0% of each run, Pallas kernels for 5% -> 6%
where the time goes in v6:
time: 139 us
  starting transfers between devices  75.5 us (54%)
  blocking collectives  22.2 us (16%)
  waiting for transfers between devices  18.6 us (13%)
  Pallas kernels  18.3 us (13%)
  local copies, waits for them, and re-layouts  2.98 us (2%)
    ppermute x30, starting transfers between devices, exchange(): return [lax.ppermute(x, axis, way) for x, (axis, way) in zip(sends, ways)]  38.1 us
    all_to_all x2, starting transfers between devices, body(): table = lax.all_to_all(table, AXES, 0, 0, tiled=True)  26.6 us
    all_to_all x1, blocking collectives, body(): table = lax.all_to_all(table, AXES, 0, 0, tiled=True)  22.2 us
    pallas_call x23, Pallas kernels, call(): pl.pallas_call(kernel, name=name, out_shape=[shape_of(out) for out in out...  18.3 us
    ppermute x9, starting transfers between devices, span_rows(): lax.ppermute(row, 'span', [(i, i ^ k) for i in range(n_span)])  10.8 us
    all_to_all x2, waiting for transfers between devices, body(): table = lax.all_to_all(table, AXES, 0, 0, tiled=True)  9.49 us
    ppermute x9, waiting for transfers between devices, span_rows(): lax.ppermute(row, 'span', [(i, i ^ k) for i in range(n_span)])  5.37 us
    ppermute x30, waiting for transfers between devices, exchange(): return [lax.ppermute(x, axis, way) for x, (axis, way) in zip(sends, ways)]  3.69 us
  transfers between devices with their start and end apart: 41, of which 14 were waited for; matrix products, arithmetic and copies ran while one was open for 0% of the time, Pallas kernels for 6%

profile of v6, /device:TPU:1, one launch (start us, length us, event | category | flops | bytes accessed | tf_op | source)
XLA Modules:
  0.0 138.7 jit_solution(2761216106734592552)
XLA Ops:
  2.2 15.7 %all-to-all-start = ((f32[256,1,128]{2,1,0:T(1,128)}), f32[256,1,128]{2,1,0:T(1,128)S(1)}, u32[]{:S(2)}, u32[]{:S(2)}) async-start(f32[256,1,128]{2,1,0:T(1,128)} %bitcast.7), calls=%async_computation | async-start | bytes 262144 | tf_op jit(solution)/shard_map/all_to_all | solution.py:680
  19.1 3.0 %collective-permute-start = (f32[1,256]{1,0:T(1,128)S(1)}, f32[1,256]{1,0:T(1,128)S(1)}, u32[]{:S(2)}, u32[]{:S(2)}) collective-permute-start(f32[1,256]{1,0:T(1,128)S(1)} %get-tuple-element.71.r0), channel_id=1, source_target_pairs={{0,4},{2,6},{4,0},{6,2},{1,5},{3,7},{5,1},{7,3},{8,12},{10,14},{12... | collective-permute-start | bytes 3080 | tf_op jit(solution)/shard_map/ppermute | solution.py:668
  23.0 1.2 copy-done.3
  25.0 1.4 %setup.1 = (bf16[64,768]{1,0:T(8,128)(2,1)S(1)}, bf16[64,768]{1,0:T(8,128)(2,1)S(1)}, bf16[64,384]{1,0:T(8,128)(2,1)S(1)}, bf16[64,768]{1,0:T(8,128)(2,1)S(1)}, ...) custom-call(s32[4,20]{1,0:T(4,128)S(1)} %concatenate.3.ints_ref, ...), custom_call_target="tpu_custom_call" | custom-call | tf_op jit(solution)/shard_map/setup/pallas_call | solution.py:603
  26.8 4.0 %all-to-all-done = f32[256,1,128]{2,1,0:T(1,128)S(1)} async-done(((f32[256,1,128]{2,1,0:T(1,128)}), f32[256,1,128]{2,1,0:T(1,128)S(1)}, u32[]{:S(2)}, u32[]{:S(2)}) %all-to-all-start) | async-done | bytes 131104 | tf_op jit(solution)/shard_map/all_to_all | solution.py:680
  32.4 1.9 %collective-permute-start.4 = (f32[8,128]{1,0:T(8,128)S(1)}, f32[8,128]{1,0:T(8,128)S(1)}, u32[]{:S(2)}, u32[]{:S(2)}) collective-permute-start(f32[8,128]{1,0:T(8,128)S(1)} %get-tuple-element.84), channel_id=1, source_target_pairs={{0,248},{8,16},{16,8},{24,32},{32,24},{40,48},{48,40},{56,64},{64,... | collective-permute-start | bytes 12296 | tf_op jit(solution)/shard_map/ppermute | solution.py:664
  35.1 1.9 %collective-permute-start.6 = (f32[8,128]{1,0:T(8,128)S(1)}, f32[8,128]{1,0:T(8,128)S(1)}, u32[]{:S(2)}, u32[]{:S(2)}) collective-permute-start(f32[8,128]{1,0:T(8,128)S(1)} %get-tuple-element.86), channel_id=1, source_target_pairs={{0,6},{2,4},{4,2},{6,0},{1,7},{3,5},{5,3},{7,1},{8,14},{10,12},{12... | collective-permute-start | bytes 12296 | tf_op jit(solution)/shard_map/ppermute | solution.py:664
  37.0 2.4 %collective-permute-start.7 = (f32[8,128]{1,0:T(8,128)S(1)}, f32[8,128]{1,0:T(8,128)S(1)}, u32[]{:S(2)}, u32[]{:S(2)}) collective-permute-start(f32[8,128]{1,0:T(8,128)S(1)} %get-tuple-element.87), channel_id=1, source_target_pairs={{0,8},{8,0},{16,24},{24,16},{32,40},{40,32},{48,56},{56,48},{64,72... | collective-permute-start | bytes 12296 | tf_op jit(solution)/shard_map/ppermute | solution.py:664
  40.2 1.3 second0.1
  41.5 1.8 %collective-permute-start.8 = (f32[8,128]{1,0:T(8,128)S(1)}, f32[8,128]{1,0:T(8,128)S(1)}, u32[]{:S(2)}, u32[]{:S(2)}) collective-permute-start(f32[8,128]{1,0:T(8,128)S(1)} %get-tuple-element.93), channel_id=1, source_target_pairs={{0,1},{1,0},{2,3},{3,2},{4,5},{5,4},{6,7},{7,6},{8,9},{9,8},{10,11... | collective-permute-start | bytes 12296 | tf_op jit(solution)/shard_map/ppermute | solution.py:664
  44.2 3.5 %collective-permute-start.12 = (f32[8,128]{1,0:T(8,128)S(1)}, f32[8,128]{1,0:T(8,128)S(1)}, u32[]{:S(2)}, u32[]{:S(2)}) collective-permute-start(f32[8,128]{1,0:T(8,128)S(1)} %get-tuple-element.97), channel_id=1, source_target_pairs={{0,8},{8,0},{16,24},{24,16},{32,40},{40,32},{48,56},{56,48},{64,72... | collective-permute-start | bytes 12296 | tf_op jit(solution)/shard_map/ppermute | solution.py:664
  48.5 1.4 third0.1
  49.8 11.0 %all-to-all-start.1 = ((f32[256,1,128]{2,1,0:T(1,128)}), f32[256,1,128]{2,1,0:T(1,128)S(1)}, u32[]{:S(2)}, u32[]{:S(2)}) async-start(f32[256,1,128]{2,1,0:T(1,128)} %bitcast.13), calls=%async_computation.1 | async-start | bytes 262144 | tf_op jit(solution)/shard_map/all_to_all | solution.py:773
  61.0 3.0 %collective-permute-start.13 = (f32[1,256]{1,0:T(1,128)S(1)}, f32[1,256]{1,0:T(1,128)S(1)}, u32[]{:S(2)}, u32[]{:S(2)}) collective-permute-start(f32[1,256]{1,0:T(1,128)S(1)} %row0.1.r0), channel_id=1, source_target_pairs={{0,4},{2,6},{4,0},{6,2},{1,5},{3,7},{5,1},{7,3},{8,12},{10,14},{12... | collective-permute-start | bytes 3080 | tf_op jit(solution)/shard_map/ppermute | solution.py:668
  65.0 2.9 %collective-permute-done.14.r2 = f32[1,256]{1,0:T(1,128)S(1)} collective-permute-done((f32[1,256]{1,0:T(1,128)S(1)}, f32[1,256]{1,0:T(1,128)S(1)}, u32[]{:S(2)}, u32[]{:S(2)}) %collective-permute-start.14) | collective-permute-done | bytes 1056 | tf_op jit(solution)/shard_map/ppermute | solution.py:668
  68.3 5.5 %all-to-all-done.1 = f32[256,1,128]{2,1,0:T(1,128)S(1)} async-done(((f32[256,1,128]{2,1,0:T(1,128)}), f32[256,1,128]{2,1,0:T(1,128)S(1)}, u32[]{:S(2)}, u32[]{:S(2)}) %all-to-all-start.1) | async-done | bytes 131104 | tf_op jit(solution)/shard_map/all_to_all | solution.py:773
  75.4 1.9 %collective-permute-start.17 = (f32[8,128]{1,0:T(8,128)S(1)}, f32[8,128]{1,0:T(8,128)S(1)}, u32[]{:S(2)}, u32[]{:S(2)}) collective-permute-start(f32[8,128]{1,0:T(8,128)S(1)} %get-tuple-element.105), channel_id=1, source_target_pairs={{0,248},{8,16},{16,8},{24,32},{32,24},{40,48},{48,40},{56,64},{64,... | collective-permute-start | bytes 12296 | tf_op jit(solution)/shard_map/ppermute | solution.py:664
  79.9 1.8 %collective-permute-done.19.refs_7_ = f32[8,128]{1,0:T(8,128)S(1)} collective-permute-done((f32[8,128]{1,0:T(8,128)S(1)}, f32[8,128]{1,0:T(8,128)S(1)}, u32[]{:S(2)}, u32[]{:S(2)}) %collective-permute-start.19) | collective-permute-done | bytes 4128 | tf_op jit(solution)/shard_map/ppermute | solution.py:664
  81.7 1.3 second1.1
  83.0 1.4 collective-permute-start.21
  84.4 2.1 %collective-permute-start.22 = (f32[8,128]{1,0:T(8,128)S(1)}, f32[8,128]{1,0:T(8,128)S(1)}, u32[]{:S(2)}, u32[]{:S(2)}) collective-permute-start(f32[8,128]{1,0:T(8,128)S(1)} %get-tuple-element.112), channel_id=1, source_target_pairs={{0,248},{8,16},{16,8},{24,32},{32,24},{40,48},{48,40},{56,64},{64,... | collective-permute-start | bytes 12296 | tf_op jit(solution)/shard_map/ppermute | solution.py:664
  87.2 1.4 collective-permute-start.25
  91.0 1.3 collective-permute-start.26
  92.3 1.7 %collective-permute-start.27 = (f32[1,256]{1,0:T(1,128)S(1)}, f32[1,256]{1,0:T(1,128)S(1)}, u32[]{:S(2)}, u32[]{:S(2)}) collective-permute-start(f32[1,256]{1,0:T(1,128)S(1)} %get-tuple-element.117.r0), channel_id=1, source_target_pairs={{0,6},{2,4},{4,2},{6,0},{1,7},{3,5},{5,3},{7,1},{8,14},{10,12},{12... | collective-permute-start | bytes 3080 | tf_op jit(solution)/shard_map/ppermute | solution.py:668
  97.4 2.0 %collective-permute-start.29 = (f32[8,128]{1,0:T(8,128)S(1)}, f32[8,128]{1,0:T(8,128)S(1)}, u32[]{:S(2)}, u32[]{:S(2)}) collective-permute-start(f32[8,128]{1,0:T(8,128)S(1)} %get-tuple-element.120), channel_id=1, source_target_pairs={{0,1},{1,0},{2,3},{3,2},{4,5},{5,4},{6,7},{7,6},{8,9},{9,8},{10,11... | collective-permute-start | bytes 12296 | tf_op jit(solution)/shard_map/ppermute | solution.py:664
  99.4 2.2 %collective-permute-start.30 = (f32[8,128]{1,0:T(8,128)S(1)}, f32[8,128]{1,0:T(8,128)S(1)}, u32[]{:S(2)}, u32[]{:S(2)}) collective-permute-start(f32[8,128]{1,0:T(8,128)S(1)} %get-tuple-element.121), channel_id=1, source_target_pairs={{0,248},{8,16},{16,8},{24,32},{32,24},{40,48},{48,40},{56,64},{64,... | collective-permute-start | bytes 12296 | tf_op jit(solution)/shard_map/ppermute | solution.py:664
  102.5 2.0 %collective-permute-start.33 = (f32[8,128]{1,0:T(8,128)S(1)}, f32[8,128]{1,0:T(8,128)S(1)}, u32[]{:S(2)}, u32[]{:S(2)}) collective-permute-start(f32[8,128]{1,0:T(8,128)S(1)} %get-tuple-element.124), channel_id=1, source_target_pairs={{0,8},{8,0},{16,24},{24,16},{32,40},{40,32},{48,56},{56,48},{64,72... | collective-permute-start | bytes 12296 | tf_op jit(solution)/shard_map/ppermute | solution.py:664
  105.3 1.3 second2.1
  106.6 1.7 %collective-permute-start.34 = (f32[8,128]{1,0:T(8,128)S(1)}, f32[8,128]{1,0:T(8,128)S(1)}, u32[]{:S(2)}, u32[]{:S(2)}) collective-permute-start(f32[8,128]{1,0:T(8,128)S(1)} %get-tuple-element.127), channel_id=1, source_target_pairs={{0,1},{1,0},{2,3},{3,2},{4,5},{5,4},{6,7},{7,6},{8,9},{9,8},{10,11... | collective-permute-start | bytes 12296 | tf_op jit(solution)/shard_map/ppermute | solution.py:664
  108.3 1.6 %collective-permute-start.35 = (f32[8,128]{1,0:T(8,128)S(1)}, f32[8,128]{1,0:T(8,128)S(1)}, u32[]{:S(2)}, u32[]{:S(2)}) collective-permute-start(f32[8,128]{1,0:T(8,128)S(1)} %get-tuple-element.128), channel_id=1, source_target_pairs={{0,248},{8,16},{16,8},{24,32},{32,24},{40,48},{48,40},{56,64},{64,... | collective-permute-start | bytes 12296 | tf_op jit(solution)/shard_map/ppermute | solution.py:664
  111.2 2.9 %collective-permute-start.38 = (f32[8,128]{1,0:T(8,128)S(1)}, f32[8,128]{1,0:T(8,128)S(1)}, u32[]{:S(2)}, u32[]{:S(2)}) collective-permute-start(f32[8,128]{1,0:T(8,128)S(1)} %get-tuple-element.131), channel_id=1, source_target_pairs={{0,8},{8,0},{16,24},{24,16},{32,40},{40,32},{48,56},{56,48},{64,72... | collective-permute-start | bytes 12296 | tf_op jit(solution)/shard_map/ppermute | solution.py:664
  115.7 22.2 %all_to_all.33 = f32[256,1,128]{2,1,0:T(1,128)S(1)} all-to-all(f32[256,1,128]{2,1,0:T(1,128)S(1)} %bitcast.25), channel_id=1, replica_groups=mesh['passage'=32,'span'=4,'radial'=2] {'passage','span','radial'}, dimensions={0} | all-to-all | bytes 262144 | tf_op jit(solution)/shard_map/all_to_all | solution.py:781
  (112 shorter events, 27.1 us)
Async XLA Ops:
  2.2 28.7 %all-to-all-start = ((f32[256,1,128]{2,1,0:T(1,128)}), f32[256,1,128]{2,1,0:T(1,128)S(1)}, u32[]{:S(2)}, u32[]{:S(2)}) async-start(f32[256,1,128]{2,1,0:T(1,128)} %bitcast.7), calls=%async_computation | async-start | bytes 262144 | tf_op jit(solution)/shard_map/all_to_all | solution.py:680
  19.1 7.3 %collective-permute-start = (f32[1,256]{1,0:T(1,128)S(1)}, f32[1,256]{1,0:T(1,128)S(1)}, u32[]{:S(2)}, u32[]{:S(2)}) collective-permute-start(f32[1,256]{1,0:T(1,128)S(1)} %get-tuple-element.71.r0), channel_id=1, source_target_pairs={{0,4},{2,6},{4,0},{6,2},{1,5},{3,7},{5,1},{7,3},{8,12},{10,14},{12... | collective-permute-start | bytes 3080 | tf_op jit(solution)/shard_map/ppermute | solution.py:668
  22.1 4.3 %collective-permute-start.1 = (f32[1,256]{1,0:T(1,128)S(1)}, f32[1,256]{1,0:T(1,128)S(1)}, u32[]{:S(2)}, u32[]{:S(2)}) collective-permute-start(f32[1,256]{1,0:T(1,128)S(1)} %get-tuple-element.71.r0), channel_id=1, source_target_pairs={{0,6},{2,4},{4,2},{6,0},{1,7},{3,5},{5,3},{7,1},{8,14},{10,12},{12... | collective-permute-start | bytes 3080 | tf_op jit(solution)/shard_map/ppermute | solution.py:668
  31.6 8.5 %collective-permute-start.3 = (f32[8,128]{1,0:T(8,128)S(1)}, f32[8,128]{1,0:T(8,128)S(1)}, u32[]{:S(2)}, u32[]{:S(2)}) collective-permute-start(f32[8,128]{1,0:T(8,128)S(1)} %get-tuple-element.83), channel_id=1, source_target_pairs={{0,1},{1,0},{2,3},{3,2},{4,5},{5,4},{6,7},{7,6},{8,9},{9,8},{10,11... | collective-permute-start | bytes 12296 | tf_op jit(solution)/shard_map/ppermute | solution.py:664
  32.4 7.7 %collective-permute-start.4 = (f32[8,128]{1,0:T(8,128)S(1)}, f32[8,128]{1,0:T(8,128)S(1)}, u32[]{:S(2)}, u32[]{:S(2)}) collective-permute-start(f32[8,128]{1,0:T(8,128)S(1)} %get-tuple-element.84), channel_id=1, source_target_pairs={{0,248},{8,16},{16,8},{24,32},{32,24},{40,48},{48,40},{56,64},{64,... | collective-permute-start | bytes 12296 | tf_op jit(solution)/shard_map/ppermute | solution.py:664
  34.3 5.8 %collective-permute-start.5 = (f32[8,128]{1,0:T(8,128)S(1)}, f32[8,128]{1,0:T(8,128)S(1)}, u32[]{:S(2)}, u32[]{:S(2)}) collective-permute-start(f32[8,128]{1,0:T(8,128)S(1)} %get-tuple-element.85), channel_id=1, source_target_pairs={{0,2},{2,0},{4,6},{6,4},{1,3},{3,1},{5,7},{7,5},{8,10},{10,8},{12,... | collective-permute-start | bytes 12296 | tf_op jit(solution)/shard_map/ppermute | solution.py:664
  35.1 5.0 %collective-permute-start.6 = (f32[8,128]{1,0:T(8,128)S(1)}, f32[8,128]{1,0:T(8,128)S(1)}, u32[]{:S(2)}, u32[]{:S(2)}) collective-permute-start(f32[8,128]{1,0:T(8,128)S(1)} %get-tuple-element.86), channel_id=1, source_target_pairs={{0,6},{2,4},{4,2},{6,0},{1,7},{3,5},{5,3},{7,1},{8,14},{10,12},{12... | collective-permute-start | bytes 12296 | tf_op jit(solution)/shard_map/ppermute | solution.py:664
  41.5 6.8 %collective-permute-start.8 = (f32[8,128]{1,0:T(8,128)S(1)}, f32[8,128]{1,0:T(8,128)S(1)}, u32[]{:S(2)}, u32[]{:S(2)}) collective-permute-start(f32[8,128]{1,0:T(8,128)S(1)} %get-tuple-element.93), channel_id=1, source_target_pairs={{0,1},{1,0},{2,3},{3,2},{4,5},{5,4},{6,7},{7,6},{8,9},{9,8},{10,11... | collective-permute-start | bytes 12296 | tf_op jit(solution)/shard_map/ppermute | solution.py:664
  43.4 5.0 %collective-permute-start.9 = (f32[8,128]{1,0:T(8,128)S(1)}, f32[8,128]{1,0:T(8,128)S(1)}, u32[]{:S(2)}, u32[]{:S(2)}) collective-permute-start(f32[8,128]{1,0:T(8,128)S(1)} %get-tuple-element.94), channel_id=1, source_target_pairs={{0,248},{8,16},{16,8},{24,32},{32,24},{40,48},{48,40},{56,64},{64,... | collective-permute-start | bytes 12296 | tf_op jit(solution)/shard_map/ppermute | solution.py:664
  43.5 4.9 %collective-permute-start.10 = (f32[8,128]{1,0:T(8,128)S(1)}, f32[8,128]{1,0:T(8,128)S(1)}, u32[]{:S(2)}, u32[]{:S(2)}) collective-permute-start(f32[8,128]{1,0:T(8,128)S(1)} %get-tuple-element.95), channel_id=1, source_target_pairs={{0,2},{2,0},{4,6},{6,4},{1,3},{3,1},{5,7},{7,5},{8,10},{10,8},{12,... | collective-permute-start | bytes 12296 | tf_op jit(solution)/shard_map/ppermute | solution.py:664
  43.5 4.9 %collective-permute-start.11 = (f32[8,128]{1,0:T(8,128)S(1)}, f32[8,128]{1,0:T(8,128)S(1)}, u32[]{:S(2)}, u32[]{:S(2)}) collective-permute-start(f32[8,128]{1,0:T(8,128)S(1)} %get-tuple-element.96), channel_id=1, source_target_pairs={{0,6},{2,4},{4,2},{6,0},{1,7},{3,5},{5,3},{7,1},{8,14},{10,12},{12... | collective-permute-start | bytes 12296 | tf_op jit(solution)/shard_map/ppermute | solution.py:664
  44.2 4.3 %collective-permute-start.12 = (f32[8,128]{1,0:T(8,128)S(1)}, f32[8,128]{1,0:T(8,128)S(1)}, u32[]{:S(2)}, u32[]{:S(2)}) collective-permute-start(f32[8,128]{1,0:T(8,128)S(1)} %get-tuple-element.97), channel_id=1, source_target_pairs={{0,8},{8,0},{16,24},{24,16},{32,40},{40,32},{48,56},{56,48},{64,72... | collective-permute-start | bytes 12296 | tf_op jit(solution)/shard_map/ppermute | solution.py:664
  49.8 24.0 %all-to-all-start.1 = ((f32[256,1,128]{2,1,0:T(1,128)}), f32[256,1,128]{2,1,0:T(1,128)S(1)}, u32[]{:S(2)}, u32[]{:S(2)}) async-start(f32[256,1,128]{2,1,0:T(1,128)} %bitcast.13), calls=%async_computation.1 | async-start | bytes 262144 | tf_op jit(solution)/shard_map/all_to_all | solution.py:773
  61.0 4.0 %collective-permute-start.13 = (f32[1,256]{1,0:T(1,128)S(1)}, f32[1,256]{1,0:T(1,128)S(1)}, u32[]{:S(2)}, u32[]{:S(2)}) collective-permute-start(f32[1,256]{1,0:T(1,128)S(1)} %row0.1.r0), channel_id=1, source_target_pairs={{0,4},{2,6},{4,0},{6,2},{1,5},{3,7},{5,1},{7,3},{8,12},{10,14},{12... | collective-permute-start | bytes 3080 | tf_op jit(solution)/shard_map/ppermute | solution.py:668
  64.0 3.9 %collective-permute-start.14 = (f32[1,256]{1,0:T(1,128)S(1)}, f32[1,256]{1,0:T(1,128)S(1)}, u32[]{:S(2)}, u32[]{:S(2)}) collective-permute-start(f32[1,256]{1,0:T(1,128)S(1)} %row0.1.r0), channel_id=1, source_target_pairs={{0,6},{2,4},{4,2},{6,0},{1,7},{3,5},{5,3},{7,1},{8,14},{10,12},{12... | collective-permute-start | bytes 3080 | tf_op jit(solution)/shard_map/ppermute | solution.py:668
  74.6 4.7 %collective-permute-start.16 = (f32[8,128]{1,0:T(8,128)S(1)}, f32[8,128]{1,0:T(8,128)S(1)}, u32[]{:S(2)}, u32[]{:S(2)}) collective-permute-start(f32[8,128]{1,0:T(8,128)S(1)} %get-tuple-element.104), channel_id=1, source_target_pairs={{0,1},{1,0},{2,3},{3,2},{4,5},{5,4},{6,7},{7,6},{8,9},{9,8},{10,11... | collective-permute-start | bytes 12296 | tf_op jit(solution)/shard_map/ppermute | solution.py:664
  75.4 3.9 %collective-permute-start.17 = (f32[8,128]{1,0:T(8,128)S(1)}, f32[8,128]{1,0:T(8,128)S(1)}, u32[]{:S(2)}, u32[]{:S(2)}) collective-permute-start(f32[8,128]{1,0:T(8,128)S(1)} %get-tuple-element.105), channel_id=1, source_target_pairs={{0,248},{8,16},{16,8},{24,32},{32,24},{40,48},{48,40},{56,64},{64,... | collective-permute-start | bytes 12296 | tf_op jit(solution)/shard_map/ppermute | solution.py:664
  77.7 4.0 %collective-permute-start.19 = (f32[8,128]{1,0:T(8,128)S(1)}, f32[8,128]{1,0:T(8,128)S(1)}, u32[]{:S(2)}, u32[]{:S(2)}) collective-permute-start(f32[8,128]{1,0:T(8,128)S(1)} %get-tuple-element.107), channel_id=1, source_target_pairs={{0,6},{2,4},{4,2},{6,0},{1,7},{3,5},{5,3},{7,1},{8,14},{10,12},{12... | collective-permute-start | bytes 12296 | tf_op jit(solution)/shard_map/ppermute | solution.py:664
  78.0 3.7 %collective-permute-start.20 = (f32[8,128]{1,0:T(8,128)S(1)}, f32[8,128]{1,0:T(8,128)S(1)}, u32[]{:S(2)}, u32[]{:S(2)}) collective-permute-start(f32[8,128]{1,0:T(8,128)S(1)} %get-tuple-element.108), channel_id=1, source_target_pairs={{0,8},{8,0},{16,24},{24,16},{32,40},{40,32},{48,56},{56,48},{64,72... | collective-permute-start | bytes 12296 | tf_op jit(solution)/shard_map/ppermute | solution.py:664
  83.0 6.3 %collective-permute-start.21 = (f32[8,128]{1,0:T(8,128)S(1)}, f32[8,128]{1,0:T(8,128)S(1)}, u32[]{:S(2)}, u32[]{:S(2)}) collective-permute-start(f32[8,128]{1,0:T(8,128)S(1)} %get-tuple-element.111), channel_id=1, source_target_pairs={{0,1},{1,0},{2,3},{3,2},{4,5},{5,4},{6,7},{7,6},{8,9},{9,8},{10,11... | collective-permute-start | bytes 12296 | tf_op jit(solution)/shard_map/ppermute | solution.py:664
  84.4 4.9 %collective-permute-start.22 = (f32[8,128]{1,0:T(8,128)S(1)}, f32[8,128]{1,0:T(8,128)S(1)}, u32[]{:S(2)}, u32[]{:S(2)}) collective-permute-start(f32[8,128]{1,0:T(8,128)S(1)} %get-tuple-element.112), channel_id=1, source_target_pairs={{0,248},{8,16},{16,8},{24,32},{32,24},{40,48},{48,40},{56,64},{64,... | collective-permute-start | bytes 12296 | tf_op jit(solution)/shard_map/ppermute | solution.py:664
  86.5 3.7 %collective-permute-start.24 = (f32[8,128]{1,0:T(8,128)S(1)}, f32[8,128]{1,0:T(8,128)S(1)}, u32[]{:S(2)}, u32[]{:S(2)}) collective-permute-start(f32[8,128]{1,0:T(8,128)S(1)} %get-tuple-element.114), channel_id=1, source_target_pairs={{0,6},{2,4},{4,2},{6,0},{1,7},{3,5},{5,3},{7,1},{8,14},{10,12},{12... | collective-permute-start | bytes 12296 | tf_op jit(solution)/shard_map/ppermute | solution.py:664
  91.0 4.0 %collective-permute-start.26 = (f32[1,256]{1,0:T(1,128)S(1)}, f32[1,256]{1,0:T(1,128)S(1)}, u32[]{:S(2)}, u32[]{:S(2)}) collective-permute-start(f32[1,256]{1,0:T(1,128)S(1)} %get-tuple-element.117.r0), channel_id=1, source_target_pairs={{0,4},{2,6},{4,0},{6,2},{1,5},{3,7},{5,1},{7,3},{8,12},{10,14},{12... | collective-permute-start | bytes 3080 | tf_op jit(solution)/shard_map/ppermute | solution.py:668
  97.4 7.8 %collective-permute-start.29 = (f32[8,128]{1,0:T(8,128)S(1)}, f32[8,128]{1,0:T(8,128)S(1)}, u32[]{:S(2)}, u32[]{:S(2)}) collective-permute-start(f32[8,128]{1,0:T(8,128)S(1)} %get-tuple-element.120), channel_id=1, source_target_pairs={{0,1},{1,0},{2,3},{3,2},{4,5},{5,4},{6,7},{7,6},{8,9},{9,8},{10,11... | collective-permute-start | bytes 12296 | tf_op jit(solution)/shard_map/ppermute | solution.py:664
  99.4 5.8 %collective-permute-start.30 = (f32[8,128]{1,0:T(8,128)S(1)}, f32[8,128]{1,0:T(8,128)S(1)}, u32[]{:S(2)}, u32[]{:S(2)}) collective-permute-start(f32[8,128]{1,0:T(8,128)S(1)} %get-tuple-element.121), channel_id=1, source_target_pairs={{0,248},{8,16},{16,8},{24,32},{32,24},{40,48},{48,40},{56,64},{64,... | collective-permute-start | bytes 12296 | tf_op jit(solution)/shard_map/ppermute | solution.py:664
  101.6 3.7 %collective-permute-start.31 = (f32[8,128]{1,0:T(8,128)S(1)}, f32[8,128]{1,0:T(8,128)S(1)}, u32[]{:S(2)}, u32[]{:S(2)}) collective-permute-start(f32[8,128]{1,0:T(8,128)S(1)} %get-tuple-element.122), channel_id=1, source_target_pairs={{0,2},{2,0},{4,6},{6,4},{1,3},{3,1},{5,7},{7,5},{8,10},{10,8},{12,... | collective-permute-start | bytes 12296 | tf_op jit(solution)/shard_map/ppermute | solution.py:664
  101.6 3.7 %collective-permute-start.32 = (f32[8,128]{1,0:T(8,128)S(1)}, f32[8,128]{1,0:T(8,128)S(1)}, u32[]{:S(2)}, u32[]{:S(2)}) collective-permute-start(f32[8,128]{1,0:T(8,128)S(1)} %get-tuple-element.123), channel_id=1, source_target_pairs={{0,6},{2,4},{4,2},{6,0},{1,7},{3,5},{5,3},{7,1},{8,14},{10,12},{12... | collective-permute-start | bytes 12296 | tf_op jit(solution)/shard_map/ppermute | solution.py:664
  106.6 8.2 %collective-permute-start.34 = (f32[8,128]{1,0:T(8,128)S(1)}, f32[8,128]{1,0:T(8,128)S(1)}, u32[]{:S(2)}, u32[]{:S(2)}) collective-permute-start(f32[8,128]{1,0:T(8,128)S(1)} %get-tuple-element.127), channel_id=1, source_target_pairs={{0,1},{1,0},{2,3},{3,2},{4,5},{5,4},{6,7},{7,6},{8,9},{9,8},{10,11... | collective-permute-start | bytes 12296 | tf_op jit(solution)/shard_map/ppermute | solution.py:664
  108.3 6.5 %collective-permute-start.35 = (f32[8,128]{1,0:T(8,128)S(1)}, f32[8,128]{1,0:T(8,128)S(1)}, u32[]{:S(2)}, u32[]{:S(2)}) collective-permute-start(f32[8,128]{1,0:T(8,128)S(1)} %get-tuple-element.128), channel_id=1, source_target_pairs={{0,248},{8,16},{16,8},{24,32},{32,24},{40,48},{48,40},{56,64},{64,... | collective-permute-start | bytes 12296 | tf_op jit(solution)/shard_map/ppermute | solution.py:664
  110.0 4.9 %collective-permute-start.36 = (f32[8,128]{1,0:T(8,128)S(1)}, f32[8,128]{1,0:T(8,128)S(1)}, u32[]{:S(2)}, u32[]{:S(2)}) collective-permute-start(f32[8,128]{1,0:T(8,128)S(1)} %get-tuple-element.129), channel_id=1, source_target_pairs={{0,2},{2,0},{4,6},{6,4},{1,3},{3,1},{5,7},{7,5},{8,10},{10,8},{12,... | collective-permute-start | bytes 12296 | tf_op jit(solution)/shard_map/ppermute | solution.py:664
  110.3 4.5 %collective-permute-start.37 = (f32[8,128]{1,0:T(8,128)S(1)}, f32[8,128]{1,0:T(8,128)S(1)}, u32[]{:S(2)}, u32[]{:S(2)}) collective-permute-start(f32[8,128]{1,0:T(8,128)S(1)} %get-tuple-element.130), channel_id=1, source_target_pairs={{0,6},{2,4},{4,2},{6,0},{1,7},{3,5},{5,3},{7,1},{8,14},{10,12},{12... | collective-permute-start | bytes 12296 | tf_op jit(solution)/shard_map/ppermute | solution.py:664
  111.2 3.7 %collective-permute-start.38 = (f32[8,128]{1,0:T(8,128)S(1)}, f32[8,128]{1,0:T(8,128)S(1)}, u32[]{:S(2)}, u32[]{:S(2)}) collective-permute-start(f32[8,128]{1,0:T(8,128)S(1)} %get-tuple-element.131), channel_id=1, source_target_pairs={{0,8},{8,0},{16,24},{24,16},{32,40},{40,32},{48,56},{56,48},{64,72... | collective-permute-start | bytes 12296 | tf_op jit(solution)/shard_map/ppermute | solution.py:664
  (26 other events, 212.9 us)

commit v7 on v6

--- a/solution.py
+++ b/solution.py
@@ -318,7 +318,10 @@
     return place_terms(groups, omask_ref, lay_ref, 0)
 
 
-def start_kernel(rs_ref, table_ref):
+def start_kernel(rs_hbm, table_ref, rs_ref, sem):
+    copy = pltpu.make_async_copy(rs_hbm, rs_ref, sem)
+    copy.start()
+    copy.wait()
     rs = rs_ref[...]
     table_ref[...] = jnp.broadcast_to(scalar_row([total(rs * rs)]), table_ref.shape)
 
@@ -676,7 +679,14 @@
     def half_floats(*shape):
         return jax.ShapeDtypeStruct(shape, jnp.bfloat16)
 
-    (table,) = call(start_kernel, "start", (right_side,), [table_shape], raw=(0,))
+    table = pl.pallas_call(
+        start_kernel,
+        name="start",
+        out_shape=jax.ShapeDtypeStruct(table_shape, F32),
+        in_specs=[pl.BlockSpec(memory_space=pl.ANY)],
+        out_specs=pl.BlockSpec(memory_space=VMEM),
+        scratch_shapes=[VMEM(right_side.shape, F32), pltpu.SemaphoreType.DMA],
+    )(right_side)
     table = lax.all_to_all(table, AXES, 0, 0, tiled=True)
     x, massw, member, odd, row = call(
         prepare_kernel,

time: 139 us -> 139 us (level)
    pallas_call x0 -> x1, Pallas kernels: none -> 1.52 us  [body(): pl.pallas_call(start_kernel, name='start', out_shape=jax.ShapeDtypeStruct...]
    pallas_call x23 -> x22, Pallas kernels: 18.3 us -> 17.5 us  [call(): pl.pallas_call(kernel, name=name, out_shape=[shape_of(out) for out in out...]
where the time goes in v7:
time: 139 us
  starting transfers between devices  75.5 us (54%)
  blocking collectives  22.2 us (16%)
  Pallas kernels  19 us (14%)
  waiting for transfers between devices  18.6 us (13%)
  local copies, waits for them, and re-layouts  2.31 us (2%)
    ppermute x30, starting transfers between devices, exchange(): return [lax.ppermute(x, axis, way) for x, (axis, way) in zip(sends, ways)]  38.3 us
    all_to_all x2, starting transfers between devices, body(): table = lax.all_to_all(table, AXES, 0, 0, tiled=True)  26.6 us
    all_to_all x1, blocking collectives, body(): table = lax.all_to_all(table, AXES, 0, 0, tiled=True)  22.2 us
    pallas_call x22, Pallas kernels, call(): pl.pallas_call(kernel, name=name, out_shape=[shape_of(out) for out in out...  17.5 us
    ppermute x9, starting transfers between devices, span_rows(): lax.ppermute(row, 'span', [(i, i ^ k) for i in range(n_span)])  10.5 us
    all_to_all x2, waiting for transfers between devices, body(): table = lax.all_to_all(table, AXES, 0, 0, tiled=True)  9.5 us
    ppermute x9, waiting for transfers between devices, span_rows(): lax.ppermute(row, 'span', [(i, i ^ k) for i in range(n_span)])  5.37 us
    ppermute x30, waiting for transfers between devices, exchange(): return [lax.ppermute(x, axis, way) for x, (axis, way) in zip(sends, ways)]  3.75 us
  transfers between devices with their start and end apart: 41, of which 14 were waited for; matrix products, arithmetic and copies ran while one was open for 0% of the time, Pallas kernels for 6%

profile of v7, /device:TPU:1, one launch (start us, length us, event | category | flops | bytes accessed | tf_op | source)
XLA Modules:
  0.0 138.8 jit_solution(3015694324057368918)
XLA Ops:
  0.7 1.5 %start.1 = f32[256,128]{1,0:T(8,128)} custom-call(f32[4,320]{1,0:T(4,128)} %rs_hbm.1), custom_call_target="tpu_custom_call" | custom-call | tf_op jit(solution)/shard_map/start/pallas_call | solution.py:682
  2.3 15.7 %all-to-all-start = ((f32[256,1,128]{2,1,0:T(1,128)}), f32[256,1,128]{2,1,0:T(1,128)S(1)}, u32[]{:S(2)}, u32[]{:S(2)}) async-start(f32[256,1,128]{2,1,0:T(1,128)} %bitcast.29), calls=%async_computation | async-start | bytes 262144 | tf_op jit(solution)/shard_map/all_to_all | solution.py:690
  19.2 3.0 %collective-permute-start = (f32[1,256]{1,0:T(1,128)S(1)}, f32[1,256]{1,0:T(1,128)S(1)}, u32[]{:S(2)}, u32[]{:S(2)}) collective-permute-start(f32[1,256]{1,0:T(1,128)S(1)} %get-tuple-element.71.r0), channel_id=1, source_target_pairs={{0,4},{2,6},{4,0},{6,2},{1,5},{3,7},{5,1},{7,3},{8,12},{10,14},{12... | collective-permute-start | bytes 3080 | tf_op jit(solution)/shard_map/ppermute | solution.py:671
  25.1 1.4 %setup.1 = (bf16[64,768]{1,0:T(8,128)(2,1)S(1)}, bf16[64,768]{1,0:T(8,128)(2,1)S(1)}, bf16[64,384]{1,0:T(8,128)(2,1)S(1)}, bf16[64,768]{1,0:T(8,128)(2,1)S(1)}, ...) custom-call(s32[4,20]{1,0:T(4,128)S(1)} %concatenate.3.ints_ref, ...), custom_call_target="tpu_custom_call" | custom-call | tf_op jit(solution)/shard_map/setup/pallas_call | solution.py:606
  26.9 4.0 %all-to-all-done = f32[256,1,128]{2,1,0:T(1,128)S(1)} async-done(((f32[256,1,128]{2,1,0:T(1,128)}), f32[256,1,128]{2,1,0:T(1,128)S(1)}, u32[]{:S(2)}, u32[]{:S(2)}) %all-to-all-start) | async-done | bytes 131104 | tf_op jit(solution)/shard_map/all_to_all | solution.py:690
  32.5 2.0 %collective-permute-start.4 = (f32[8,128]{1,0:T(8,128)S(1)}, f32[8,128]{1,0:T(8,128)S(1)}, u32[]{:S(2)}, u32[]{:S(2)}) collective-permute-start(f32[8,128]{1,0:T(8,128)S(1)} %get-tuple-element.84), channel_id=1, source_target_pairs={{0,248},{8,16},{16,8},{24,32},{32,24},{40,48},{48,40},{56,64},{64,... | collective-permute-start | bytes 12296 | tf_op jit(solution)/shard_map/ppermute | solution.py:667
  35.2 1.9 %collective-permute-start.6 = (f32[8,128]{1,0:T(8,128)S(1)}, f32[8,128]{1,0:T(8,128)S(1)}, u32[]{:S(2)}, u32[]{:S(2)}) collective-permute-start(f32[8,128]{1,0:T(8,128)S(1)} %get-tuple-element.86), channel_id=1, source_target_pairs={{0,6},{2,4},{4,2},{6,0},{1,7},{3,5},{5,3},{7,1},{8,14},{10,12},{12... | collective-permute-start | bytes 12296 | tf_op jit(solution)/shard_map/ppermute | solution.py:667
  37.1 2.4 %collective-permute-start.7 = (f32[8,128]{1,0:T(8,128)S(1)}, f32[8,128]{1,0:T(8,128)S(1)}, u32[]{:S(2)}, u32[]{:S(2)}) collective-permute-start(f32[8,128]{1,0:T(8,128)S(1)} %get-tuple-element.87), channel_id=1, source_target_pairs={{0,8},{8,0},{16,24},{24,16},{32,40},{40,32},{48,56},{56,48},{64,72... | collective-permute-start | bytes 12296 | tf_op jit(solution)/shard_map/ppermute | solution.py:667
  40.3 1.3 second0.1
  41.6 1.8 %collective-permute-start.8 = (f32[8,128]{1,0:T(8,128)S(1)}, f32[8,128]{1,0:T(8,128)S(1)}, u32[]{:S(2)}, u32[]{:S(2)}) collective-permute-start(f32[8,128]{1,0:T(8,128)S(1)} %get-tuple-element.93), channel_id=1, source_target_pairs={{0,1},{1,0},{2,3},{3,2},{4,5},{5,4},{6,7},{7,6},{8,9},{9,8},{10,11... | collective-permute-start | bytes 12296 | tf_op jit(solution)/shard_map/ppermute | solution.py:667
  44.3 3.4 %collective-permute-start.12 = (f32[8,128]{1,0:T(8,128)S(1)}, f32[8,128]{1,0:T(8,128)S(1)}, u32[]{:S(2)}, u32[]{:S(2)}) collective-permute-start(f32[8,128]{1,0:T(8,128)S(1)} %get-tuple-element.97), channel_id=1, source_target_pairs={{0,8},{8,0},{16,24},{24,16},{32,40},{40,32},{48,56},{56,48},{64,72... | collective-permute-start | bytes 12296 | tf_op jit(solution)/shard_map/ppermute | solution.py:667
  48.6 1.4 third0.1
  49.9 11.0 %all-to-all-start.1 = ((f32[256,1,128]{2,1,0:T(1,128)}), f32[256,1,128]{2,1,0:T(1,128)S(1)}, u32[]{:S(2)}, u32[]{:S(2)}) async-start(f32[256,1,128]{2,1,0:T(1,128)} %bitcast.13), calls=%async_computation.1 | async-start | bytes 262144 | tf_op jit(solution)/shard_map/all_to_all | solution.py:783
  61.1 3.0 %collective-permute-start.13 = (f32[1,256]{1,0:T(1,128)S(1)}, f32[1,256]{1,0:T(1,128)S(1)}, u32[]{:S(2)}, u32[]{:S(2)}) collective-permute-start(f32[1,256]{1,0:T(1,128)S(1)} %row0.1.r0), channel_id=1, source_target_pairs={{0,4},{2,6},{4,0},{6,2},{1,5},{3,7},{5,1},{7,3},{8,12},{10,14},{12... | collective-permute-start | bytes 3080 | tf_op jit(solution)/shard_map/ppermute | solution.py:671
  65.1 2.9 %collective-permute-done.14.r2 = f32[1,256]{1,0:T(1,128)S(1)} collective-permute-done((f32[1,256]{1,0:T(1,128)S(1)}, f32[1,256]{1,0:T(1,128)S(1)}, u32[]{:S(2)}, u32[]{:S(2)}) %collective-permute-start.14) | collective-permute-done | bytes 1056 | tf_op jit(solution)/shard_map/ppermute | solution.py:671
  68.4 5.5 %all-to-all-done.1 = f32[256,1,128]{2,1,0:T(1,128)S(1)} async-done(((f32[256,1,128]{2,1,0:T(1,128)}), f32[256,1,128]{2,1,0:T(1,128)S(1)}, u32[]{:S(2)}, u32[]{:S(2)}) %all-to-all-start.1) | async-done | bytes 131104 | tf_op jit(solution)/shard_map/all_to_all | solution.py:783
  75.5 2.0 %collective-permute-start.17 = (f32[8,128]{1,0:T(8,128)S(1)}, f32[8,128]{1,0:T(8,128)S(1)}, u32[]{:S(2)}, u32[]{:S(2)}) collective-permute-start(f32[8,128]{1,0:T(8,128)S(1)} %get-tuple-element.105), channel_id=1, source_target_pairs={{0,248},{8,16},{16,8},{24,32},{32,24},{40,48},{48,40},{56,64},{64,... | collective-permute-start | bytes 12296 | tf_op jit(solution)/shard_map/ppermute | solution.py:667
  79.9 1.5 %collective-permute-done.19.refs_7_ = f32[8,128]{1,0:T(8,128)S(1)} collective-permute-done((f32[8,128]{1,0:T(8,128)S(1)}, f32[8,128]{1,0:T(8,128)S(1)}, u32[]{:S(2)}, u32[]{:S(2)}) %collective-permute-start.19) | collective-permute-done | bytes 4128 | tf_op jit(solution)/shard_map/ppermute | solution.py:667
  81.5 1.3 second1.1
  82.8 1.7 %collective-permute-start.21 = (f32[8,128]{1,0:T(8,128)S(1)}, f32[8,128]{1,0:T(8,128)S(1)}, u32[]{:S(2)}, u32[]{:S(2)}) collective-permute-start(f32[8,128]{1,0:T(8,128)S(1)} %get-tuple-element.111), channel_id=1, source_target_pairs={{0,1},{1,0},{2,3},{3,2},{4,5},{5,4},{6,7},{7,6},{8,9},{9,8},{10,11... | collective-permute-start | bytes 12296 | tf_op jit(solution)/shard_map/ppermute | solution.py:667
  84.5 2.2 %collective-permute-start.22 = (f32[8,128]{1,0:T(8,128)S(1)}, f32[8,128]{1,0:T(8,128)S(1)}, u32[]{:S(2)}, u32[]{:S(2)}) collective-permute-start(f32[8,128]{1,0:T(8,128)S(1)} %get-tuple-element.112), channel_id=1, source_target_pairs={{0,248},{8,16},{16,8},{24,32},{32,24},{40,48},{48,40},{56,64},{64,... | collective-permute-start | bytes 12296 | tf_op jit(solution)/shard_map/ppermute | solution.py:667
  87.3 1.3 collective-permute-start.25
  89.4 1.3 collective-permute-done.24.refs_4_
  92.4 1.7 %collective-permute-start.27 = (f32[1,256]{1,0:T(1,128)S(1)}, f32[1,256]{1,0:T(1,128)S(1)}, u32[]{:S(2)}, u32[]{:S(2)}) collective-permute-start(f32[1,256]{1,0:T(1,128)S(1)} %get-tuple-element.117.r0), channel_id=1, source_target_pairs={{0,6},{2,4},{4,2},{6,0},{1,7},{3,5},{5,3},{7,1},{8,14},{10,12},{12... | collective-permute-start | bytes 3080 | tf_op jit(solution)/shard_map/ppermute | solution.py:671
  97.5 1.9 %collective-permute-start.29 = (f32[8,128]{1,0:T(8,128)S(1)}, f32[8,128]{1,0:T(8,128)S(1)}, u32[]{:S(2)}, u32[]{:S(2)}) collective-permute-start(f32[8,128]{1,0:T(8,128)S(1)} %get-tuple-element.120), channel_id=1, source_target_pairs={{0,1},{1,0},{2,3},{3,2},{4,5},{5,4},{6,7},{7,6},{8,9},{9,8},{10,11... | collective-permute-start | bytes 12296 | tf_op jit(solution)/shard_map/ppermute | solution.py:667
  99.5 1.9 %collective-permute-start.30 = (f32[8,128]{1,0:T(8,128)S(1)}, f32[8,128]{1,0:T(8,128)S(1)}, u32[]{:S(2)}, u32[]{:S(2)}) collective-permute-start(f32[8,128]{1,0:T(8,128)S(1)} %get-tuple-element.121), channel_id=1, source_target_pairs={{0,248},{8,16},{16,8},{24,32},{32,24},{40,48},{48,40},{56,64},{64,... | collective-permute-start | bytes 12296 | tf_op jit(solution)/shard_map/ppermute | solution.py:667
  102.3 2.3 %collective-permute-start.33 = (f32[8,128]{1,0:T(8,128)S(1)}, f32[8,128]{1,0:T(8,128)S(1)}, u32[]{:S(2)}, u32[]{:S(2)}) collective-permute-start(f32[8,128]{1,0:T(8,128)S(1)} %get-tuple-element.124), channel_id=1, source_target_pairs={{0,8},{8,0},{16,24},{24,16},{32,40},{40,32},{48,56},{56,48},{64,72... | collective-permute-start | bytes 12296 | tf_op jit(solution)/shard_map/ppermute | solution.py:667
  105.4 1.3 second2.1
  106.7 1.8 %collective-permute-start.34 = (f32[8,128]{1,0:T(8,128)S(1)}, f32[8,128]{1,0:T(8,128)S(1)}, u32[]{:S(2)}, u32[]{:S(2)}) collective-permute-start(f32[8,128]{1,0:T(8,128)S(1)} %get-tuple-element.127), channel_id=1, source_target_pairs={{0,1},{1,0},{2,3},{3,2},{4,5},{5,4},{6,7},{7,6},{8,9},{9,8},{10,11... | collective-permute-start | bytes 12296 | tf_op jit(solution)/shard_map/ppermute | solution.py:667
  108.5 1.6 %collective-permute-start.35 = (f32[8,128]{1,0:T(8,128)S(1)}, f32[8,128]{1,0:T(8,128)S(1)}, u32[]{:S(2)}, u32[]{:S(2)}) collective-permute-start(f32[8,128]{1,0:T(8,128)S(1)} %get-tuple-element.128), channel_id=1, source_target_pairs={{0,248},{8,16},{16,8},{24,32},{32,24},{40,48},{48,40},{56,64},{64,... | collective-permute-start | bytes 12296 | tf_op jit(solution)/shard_map/ppermute | solution.py:667
  111.4 2.9 %collective-permute-start.38 = (f32[8,128]{1,0:T(8,128)S(1)}, f32[8,128]{1,0:T(8,128)S(1)}, u32[]{:S(2)}, u32[]{:S(2)}) collective-permute-start(f32[8,128]{1,0:T(8,128)S(1)} %get-tuple-element.131), channel_id=1, source_target_pairs={{0,8},{8,0},{16,24},{24,16},{32,40},{40,32},{48,56},{56,48},{64,72... | collective-permute-start | bytes 12296 | tf_op jit(solution)/shard_map/ppermute | solution.py:667
  115.8 22.2 %all_to_all.33 = f32[256,1,128]{2,1,0:T(1,128)S(1)} all-to-all(f32[256,1,128]{2,1,0:T(1,128)S(1)} %bitcast.25), channel_id=1, replica_groups=mesh['passage'=32,'span'=4,'radial'=2] {'passage','span','radial'}, dimensions={0} | all-to-all | bytes 262144 | tf_op jit(solution)/shard_map/all_to_all | solution.py:791
  (110 shorter events, 26.8 us)
Async XLA Ops:
  2.3 28.7 %all-to-all-start = ((f32[256,1,128]{2,1,0:T(1,128)}), f32[256,1,128]{2,1,0:T(1,128)S(1)}, u32[]{:S(2)}, u32[]{:S(2)}) async-start(f32[256,1,128]{2,1,0:T(1,128)} %bitcast.29), calls=%async_computation | async-start | bytes 262144 | tf_op jit(solution)/shard_map/all_to_all | solution.py:690
  19.2 7.3 %collective-permute-start = (f32[1,256]{1,0:T(1,128)S(1)}, f32[1,256]{1,0:T(1,128)S(1)}, u32[]{:S(2)}, u32[]{:S(2)}) collective-permute-start(f32[1,256]{1,0:T(1,128)S(1)} %get-tuple-element.71.r0), channel_id=1, source_target_pairs={{0,4},{2,6},{4,0},{6,2},{1,5},{3,7},{5,1},{7,3},{8,12},{10,14},{12... | collective-permute-start | bytes 3080 | tf_op jit(solution)/shard_map/ppermute | solution.py:671
  22.2 4.3 %collective-permute-start.1 = (f32[1,256]{1,0:T(1,128)S(1)}, f32[1,256]{1,0:T(1,128)S(1)}, u32[]{:S(2)}, u32[]{:S(2)}) collective-permute-start(f32[1,256]{1,0:T(1,128)S(1)} %get-tuple-element.71.r0), channel_id=1, source_target_pairs={{0,6},{2,4},{4,2},{6,0},{1,7},{3,5},{5,3},{7,1},{8,14},{10,12},{12... | collective-permute-start | bytes 3080 | tf_op jit(solution)/shard_map/ppermute | solution.py:671
  31.7 8.5 %collective-permute-start.3 = (f32[8,128]{1,0:T(8,128)S(1)}, f32[8,128]{1,0:T(8,128)S(1)}, u32[]{:S(2)}, u32[]{:S(2)}) collective-permute-start(f32[8,128]{1,0:T(8,128)S(1)} %get-tuple-element.83), channel_id=1, source_target_pairs={{0,1},{1,0},{2,3},{3,2},{4,5},{5,4},{6,7},{7,6},{8,9},{9,8},{10,11... | collective-permute-start | bytes 12296 | tf_op jit(solution)/shard_map/ppermute | solution.py:667
  32.5 7.7 %collective-permute-start.4 = (f32[8,128]{1,0:T(8,128)S(1)}, f32[8,128]{1,0:T(8,128)S(1)}, u32[]{:S(2)}, u32[]{:S(2)}) collective-permute-start(f32[8,128]{1,0:T(8,128)S(1)} %get-tuple-element.84), channel_id=1, source_target_pairs={{0,248},{8,16},{16,8},{24,32},{32,24},{40,48},{48,40},{56,64},{64,... | collective-permute-start | bytes 12296 | tf_op jit(solution)/shard_map/ppermute | solution.py:667
  34.5 5.8 %collective-permute-start.5 = (f32[8,128]{1,0:T(8,128)S(1)}, f32[8,128]{1,0:T(8,128)S(1)}, u32[]{:S(2)}, u32[]{:S(2)}) collective-permute-start(f32[8,128]{1,0:T(8,128)S(1)} %get-tuple-element.85), channel_id=1, source_target_pairs={{0,2},{2,0},{4,6},{6,4},{1,3},{3,1},{5,7},{7,5},{8,10},{10,8},{12,... | collective-permute-start | bytes 12296 | tf_op jit(solution)/shard_map/ppermute | solution.py:667
  35.2 5.0 %collective-permute-start.6 = (f32[8,128]{1,0:T(8,128)S(1)}, f32[8,128]{1,0:T(8,128)S(1)}, u32[]{:S(2)}, u32[]{:S(2)}) collective-permute-start(f32[8,128]{1,0:T(8,128)S(1)} %get-tuple-element.86), channel_id=1, source_target_pairs={{0,6},{2,4},{4,2},{6,0},{1,7},{3,5},{5,3},{7,1},{8,14},{10,12},{12... | collective-permute-start | bytes 12296 | tf_op jit(solution)/shard_map/ppermute | solution.py:667
  41.6 6.8 %collective-permute-start.8 = (f32[8,128]{1,0:T(8,128)S(1)}, f32[8,128]{1,0:T(8,128)S(1)}, u32[]{:S(2)}, u32[]{:S(2)}) collective-permute-start(f32[8,128]{1,0:T(8,128)S(1)} %get-tuple-element.93), channel_id=1, source_target_pairs={{0,1},{1,0},{2,3},{3,2},{4,5},{5,4},{6,7},{7,6},{8,9},{9,8},{10,11... | collective-permute-start | bytes 12296 | tf_op jit(solution)/shard_map/ppermute | solution.py:667
  43.5 5.0 %collective-permute-start.9 = (f32[8,128]{1,0:T(8,128)S(1)}, f32[8,128]{1,0:T(8,128)S(1)}, u32[]{:S(2)}, u32[]{:S(2)}) collective-permute-start(f32[8,128]{1,0:T(8,128)S(1)} %get-tuple-element.94), channel_id=1, source_target_pairs={{0,248},{8,16},{16,8},{24,32},{32,24},{40,48},{48,40},{56,64},{64,... | collective-permute-start | bytes 12296 | tf_op jit(solution)/shard_map/ppermute | solution.py:667
  43.7 4.8 %collective-permute-start.10 = (f32[8,128]{1,0:T(8,128)S(1)}, f32[8,128]{1,0:T(8,128)S(1)}, u32[]{:S(2)}, u32[]{:S(2)}) collective-permute-start(f32[8,128]{1,0:T(8,128)S(1)} %get-tuple-element.95), channel_id=1, source_target_pairs={{0,2},{2,0},{4,6},{6,4},{1,3},{3,1},{5,7},{7,5},{8,10},{10,8},{12,... | collective-permute-start | bytes 12296 | tf_op jit(solution)/shard_map/ppermute | solution.py:667
  43.7 4.8 %collective-permute-start.11 = (f32[8,128]{1,0:T(8,128)S(1)}, f32[8,128]{1,0:T(8,128)S(1)}, u32[]{:S(2)}, u32[]{:S(2)}) collective-permute-start(f32[8,128]{1,0:T(8,128)S(1)} %get-tuple-element.96), channel_id=1, source_target_pairs={{0,6},{2,4},{4,2},{6,0},{1,7},{3,5},{5,3},{7,1},{8,14},{10,12},{12... | collective-permute-start | bytes 12296 | tf_op jit(solution)/shard_map/ppermute | solution.py:667
  44.3 4.3 %collective-permute-start.12 = (f32[8,128]{1,0:T(8,128)S(1)}, f32[8,128]{1,0:T(8,128)S(1)}, u32[]{:S(2)}, u32[]{:S(2)}) collective-permute-start(f32[8,128]{1,0:T(8,128)S(1)} %get-tuple-element.97), channel_id=1, source_target_pairs={{0,8},{8,0},{16,24},{24,16},{32,40},{40,32},{48,56},{56,48},{64,72... | collective-permute-start | bytes 12296 | tf_op jit(solution)/shard_map/ppermute | solution.py:667
  49.9 24.0 %all-to-all-start.1 = ((f32[256,1,128]{2,1,0:T(1,128)}), f32[256,1,128]{2,1,0:T(1,128)S(1)}, u32[]{:S(2)}, u32[]{:S(2)}) async-start(f32[256,1,128]{2,1,0:T(1,128)} %bitcast.13), calls=%async_computation.1 | async-start | bytes 262144 | tf_op jit(solution)/shard_map/all_to_all | solution.py:783
  61.1 4.0 %collective-permute-start.13 = (f32[1,256]{1,0:T(1,128)S(1)}, f32[1,256]{1,0:T(1,128)S(1)}, u32[]{:S(2)}, u32[]{:S(2)}) collective-permute-start(f32[1,256]{1,0:T(1,128)S(1)} %row0.1.r0), channel_id=1, source_target_pairs={{0,4},{2,6},{4,0},{6,2},{1,5},{3,7},{5,1},{7,3},{8,12},{10,14},{12... | collective-permute-start | bytes 3080 | tf_op jit(solution)/shard_map/ppermute | solution.py:671
  64.1 3.9 %collective-permute-start.14 = (f32[1,256]{1,0:T(1,128)S(1)}, f32[1,256]{1,0:T(1,128)S(1)}, u32[]{:S(2)}, u32[]{:S(2)}) collective-permute-start(f32[1,256]{1,0:T(1,128)S(1)} %row0.1.r0), channel_id=1, source_target_pairs={{0,6},{2,4},{4,2},{6,0},{1,7},{3,5},{5,3},{7,1},{8,14},{10,12},{12... | collective-permute-start | bytes 3080 | tf_op jit(solution)/shard_map/ppermute | solution.py:671
  74.7 4.7 %collective-permute-start.16 = (f32[8,128]{1,0:T(8,128)S(1)}, f32[8,128]{1,0:T(8,128)S(1)}, u32[]{:S(2)}, u32[]{:S(2)}) collective-permute-start(f32[8,128]{1,0:T(8,128)S(1)} %get-tuple-element.104), channel_id=1, source_target_pairs={{0,1},{1,0},{2,3},{3,2},{4,5},{5,4},{6,7},{7,6},{8,9},{9,8},{10,11... | collective-permute-start | bytes 12296 | tf_op jit(solution)/shard_map/ppermute | solution.py:667
  75.5 3.9 %collective-permute-start.17 = (f32[8,128]{1,0:T(8,128)S(1)}, f32[8,128]{1,0:T(8,128)S(1)}, u32[]{:S(2)}, u32[]{:S(2)}) collective-permute-start(f32[8,128]{1,0:T(8,128)S(1)} %get-tuple-element.105), channel_id=1, source_target_pairs={{0,248},{8,16},{16,8},{24,32},{32,24},{40,48},{48,40},{56,64},{64,... | collective-permute-start | bytes 12296 | tf_op jit(solution)/shard_map/ppermute | solution.py:667
  77.8 3.7 %collective-permute-start.19 = (f32[8,128]{1,0:T(8,128)S(1)}, f32[8,128]{1,0:T(8,128)S(1)}, u32[]{:S(2)}, u32[]{:S(2)}) collective-permute-start(f32[8,128]{1,0:T(8,128)S(1)} %get-tuple-element.107), channel_id=1, source_target_pairs={{0,6},{2,4},{4,2},{6,0},{1,7},{3,5},{5,3},{7,1},{8,14},{10,12},{12... | collective-permute-start | bytes 12296 | tf_op jit(solution)/shard_map/ppermute | solution.py:667
  82.8 6.6 %collective-permute-start.21 = (f32[8,128]{1,0:T(8,128)S(1)}, f32[8,128]{1,0:T(8,128)S(1)}, u32[]{:S(2)}, u32[]{:S(2)}) collective-permute-start(f32[8,128]{1,0:T(8,128)S(1)} %get-tuple-element.111), channel_id=1, source_target_pairs={{0,1},{1,0},{2,3},{3,2},{4,5},{5,4},{6,7},{7,6},{8,9},{9,8},{10,11... | collective-permute-start | bytes 12296 | tf_op jit(solution)/shard_map/ppermute | solution.py:667
  84.5 4.9 %collective-permute-start.22 = (f32[8,128]{1,0:T(8,128)S(1)}, f32[8,128]{1,0:T(8,128)S(1)}, u32[]{:S(2)}, u32[]{:S(2)}) collective-permute-start(f32[8,128]{1,0:T(8,128)S(1)} %get-tuple-element.112), channel_id=1, source_target_pairs={{0,248},{8,16},{16,8},{24,32},{32,24},{40,48},{48,40},{56,64},{64,... | collective-permute-start | bytes 12296 | tf_op jit(solution)/shard_map/ppermute | solution.py:667
  86.7 4.0 %collective-permute-start.24 = (f32[8,128]{1,0:T(8,128)S(1)}, f32[8,128]{1,0:T(8,128)S(1)}, u32[]{:S(2)}, u32[]{:S(2)}) collective-permute-start(f32[8,128]{1,0:T(8,128)S(1)} %get-tuple-element.114), channel_id=1, source_target_pairs={{0,6},{2,4},{4,2},{6,0},{1,7},{3,5},{5,3},{7,1},{8,14},{10,12},{12... | collective-permute-start | bytes 12296 | tf_op jit(solution)/shard_map/ppermute | solution.py:667
  91.4 4.0 %collective-permute-start.26 = (f32[1,256]{1,0:T(1,128)S(1)}, f32[1,256]{1,0:T(1,128)S(1)}, u32[]{:S(2)}, u32[]{:S(2)}) collective-permute-start(f32[1,256]{1,0:T(1,128)S(1)} %get-tuple-element.117.r0), channel_id=1, source_target_pairs={{0,4},{2,6},{4,0},{6,2},{1,5},{3,7},{5,1},{7,3},{8,12},{10,14},{12... | collective-permute-start | bytes 3080 | tf_op jit(solution)/shard_map/ppermute | solution.py:671
  92.4 3.6 %collective-permute-start.27 = (f32[1,256]{1,0:T(1,128)S(1)}, f32[1,256]{1,0:T(1,128)S(1)}, u32[]{:S(2)}, u32[]{:S(2)}) collective-permute-start(f32[1,256]{1,0:T(1,128)S(1)} %get-tuple-element.117.r0), channel_id=1, source_target_pairs={{0,6},{2,4},{4,2},{6,0},{1,7},{3,5},{5,3},{7,1},{8,14},{10,12},{12... | collective-permute-start | bytes 3080 | tf_op jit(solution)/shard_map/ppermute | solution.py:671
  97.5 7.8 %collective-permute-start.29 = (f32[8,128]{1,0:T(8,128)S(1)}, f32[8,128]{1,0:T(8,128)S(1)}, u32[]{:S(2)}, u32[]{:S(2)}) collective-permute-start(f32[8,128]{1,0:T(8,128)S(1)} %get-tuple-element.120), channel_id=1, source_target_pairs={{0,1},{1,0},{2,3},{3,2},{4,5},{5,4},{6,7},{7,6},{8,9},{9,8},{10,11... | collective-permute-start | bytes 12296 | tf_op jit(solution)/shard_map/ppermute | solution.py:667
  99.5 5.8 %collective-permute-start.30 = (f32[8,128]{1,0:T(8,128)S(1)}, f32[8,128]{1,0:T(8,128)S(1)}, u32[]{:S(2)}, u32[]{:S(2)}) collective-permute-start(f32[8,128]{1,0:T(8,128)S(1)} %get-tuple-element.121), channel_id=1, source_target_pairs={{0,248},{8,16},{16,8},{24,32},{32,24},{40,48},{48,40},{56,64},{64,... | collective-permute-start | bytes 12296 | tf_op jit(solution)/shard_map/ppermute | solution.py:667
  101.4 3.9 %collective-permute-start.31 = (f32[8,128]{1,0:T(8,128)S(1)}, f32[8,128]{1,0:T(8,128)S(1)}, u32[]{:S(2)}, u32[]{:S(2)}) collective-permute-start(f32[8,128]{1,0:T(8,128)S(1)} %get-tuple-element.122), channel_id=1, source_target_pairs={{0,2},{2,0},{4,6},{6,4},{1,3},{3,1},{5,7},{7,5},{8,10},{10,8},{12,... | collective-permute-start | bytes 12296 | tf_op jit(solution)/shard_map/ppermute | solution.py:667
  101.6 3.7 %collective-permute-start.32 = (f32[8,128]{1,0:T(8,128)S(1)}, f32[8,128]{1,0:T(8,128)S(1)}, u32[]{:S(2)}, u32[]{:S(2)}) collective-permute-start(f32[8,128]{1,0:T(8,128)S(1)} %get-tuple-element.123), channel_id=1, source_target_pairs={{0,6},{2,4},{4,2},{6,0},{1,7},{3,5},{5,3},{7,1},{8,14},{10,12},{12... | collective-permute-start | bytes 12296 | tf_op jit(solution)/shard_map/ppermute | solution.py:667
  106.7 8.2 %collective-permute-start.34 = (f32[8,128]{1,0:T(8,128)S(1)}, f32[8,128]{1,0:T(8,128)S(1)}, u32[]{:S(2)}, u32[]{:S(2)}) collective-permute-start(f32[8,128]{1,0:T(8,128)S(1)} %get-tuple-element.127), channel_id=1, source_target_pairs={{0,1},{1,0},{2,3},{3,2},{4,5},{5,4},{6,7},{7,6},{8,9},{9,8},{10,11... | collective-permute-start | bytes 12296 | tf_op jit(solution)/shard_map/ppermute | solution.py:667
  108.5 6.5 %collective-permute-start.35 = (f32[8,128]{1,0:T(8,128)S(1)}, f32[8,128]{1,0:T(8,128)S(1)}, u32[]{:S(2)}, u32[]{:S(2)}) collective-permute-start(f32[8,128]{1,0:T(8,128)S(1)} %get-tuple-element.128), channel_id=1, source_target_pairs={{0,248},{8,16},{16,8},{24,32},{32,24},{40,48},{48,40},{56,64},{64,... | collective-permute-start | bytes 12296 | tf_op jit(solution)/shard_map/ppermute | solution.py:667
  110.1 4.9 %collective-permute-start.36 = (f32[8,128]{1,0:T(8,128)S(1)}, f32[8,128]{1,0:T(8,128)S(1)}, u32[]{:S(2)}, u32[]{:S(2)}) collective-permute-start(f32[8,128]{1,0:T(8,128)S(1)} %get-tuple-element.129), channel_id=1, source_target_pairs={{0,2},{2,0},{4,6},{6,4},{1,3},{3,1},{5,7},{7,5},{8,10},{10,8},{12,... | collective-permute-start | bytes 12296 | tf_op jit(solution)/shard_map/ppermute | solution.py:667
  110.5 4.5 %collective-permute-start.37 = (f32[8,128]{1,0:T(8,128)S(1)}, f32[8,128]{1,0:T(8,128)S(1)}, u32[]{:S(2)}, u32[]{:S(2)}) collective-permute-start(f32[8,128]{1,0:T(8,128)S(1)} %get-tuple-element.130), channel_id=1, source_target_pairs={{0,6},{2,4},{4,2},{6,0},{1,7},{3,5},{5,3},{7,1},{8,14},{10,12},{12... | collective-permute-start | bytes 12296 | tf_op jit(solution)/shard_map/ppermute | solution.py:667
  111.4 3.7 %collective-permute-start.38 = (f32[8,128]{1,0:T(8,128)S(1)}, f32[8,128]{1,0:T(8,128)S(1)}, u32[]{:S(2)}, u32[]{:S(2)}) collective-permute-start(f32[8,128]{1,0:T(8,128)S(1)} %get-tuple-element.131), channel_id=1, source_target_pairs={{0,8},{8,0},{16,24},{24,16},{32,40},{40,32},{48,56},{56,48},{64,72... | collective-permute-start | bytes 12296 | tf_op jit(solution)/shard_map/ppermute | solution.py:667
  (25 other events, 218.2 us)
